TPU v7x, 32 devices: a whole 2x2x4 slice. The times are simulated.
32 devices in a mesh: dp: 2 (over x), row: 4 (over y, core), col: 4 (over z).
Axes of the slice: x: 2, y: 2, z: 4, core: 2. Of those that a mesh axis runs over, the one named last changes fastest.
Arguments:
- tokens: bfloat16 [4096, 8192], P(('dp', 'row', 'col')), parts along dimension 0, may hold values from -60 to 60
- norm_gain: float32 [8192], replicated, may hold values from 0.1 to 1.9
- w_key: bfloat16 [8192, 1024], P('row', 'col'), may hold values from -0.0625 to 0.0625
- w_value: bfloat16 [8192, 1024], P('row', 'col'), may hold values from -0.0625 to 0.0625
Outputs:
- key_rows: bfloat16 [4096, 1024], P(('dp', 'row', 'col')), parts along dimension 0
- value_rows: bfloat16 [4096, 1024], P(('dp', 'row', 'col')), parts along dimension 0
There are 2 independent parts, one for each index of `dp`. A program takes and returns all parts, laid end to end along the dimension named above; an argument that names none is the same for every part. Nothing has to cross between parts.
All inputs are finite; a program needn't handle non-finite values.
Results may differ from a plain program's by a relative error of at most 0.014.
Values may be sent and summed in bfloat16 or wider, within the bound.
No kernel may reach another device: no remote copies, remote signals or barrier semaphores. Data moves between devices by JAX's collectives and lax.ppermute only.
A program may use at most 64 MiB of HBM per device.

v0:
```python
import jax
import jax.numpy as jnp
from jax import lax
from jax.sharding import PartitionSpec as P

HEAD = 128


rope_base = 500000.0


def rotate(projected, positions):
    row_count = projected.shape[0]
    head_count = projected.shape[1] // HEAD
    half_head = HEAD // 2
    frequency = rope_base ** (-2.0 * jnp.arange(half_head, dtype=jnp.float32) / HEAD)
    angles = positions.astype(jnp.float32)[:, None] * frequency[None, :]
    cosine = jnp.cos(angles)[:, None, :]
    sine = jnp.sin(angles)[:, None, :]
    split_heads = projected.reshape(row_count, head_count, HEAD)
    first = split_heads[:, :, :half_head]
    second = split_heads[:, :, half_head:]
    turned = jnp.concatenate(
        [first * cosine - second * sine, second * cosine + first * sine], axis=2
    )
    return turned.reshape(row_count, head_count * HEAD)


def body(tokens, norm_gain, w_key, w_value):
    col_count = lax.axis_size("col")
    row_index = lax.axis_index("row")
    col_index = lax.axis_index("col")
    own_rows = tokens.shape[0]
    widened = tokens.astype(jnp.float32)
    inverse_rms = lax.rsqrt(jnp.mean(widened * widened, axis=1, keepdims=True) + 1e-05)
    normed = (widened * inverse_rms * norm_gain[None, :]).astype(jnp.bfloat16)
    tile = lax.all_to_all(normed, "row", split_axis=1, concat_axis=0, tiled=True)
    key_weights, value_weights = (
        lax.all_gather(w_key, "col", axis=1, tiled=True),
        lax.all_gather(w_value, "col", axis=1, tiled=True),
    )
    key_part = jnp.dot(tile, key_weights, preferred_element_type=jnp.float32)
    value_part = jnp.dot(tile, value_weights, preferred_element_type=jnp.float32)
    key_sum, value_sum = (
        lax.psum_scatter(
            key_part.astype(jnp.bfloat16), "row", scatter_dimension=0, tiled=True
        ).astype(jnp.float32),
        lax.psum_scatter(
            value_part.astype(jnp.bfloat16), "row", scatter_dimension=0, tiled=True
        ).astype(jnp.float32),
    )
    positions = (row_index * col_count + col_index) * own_rows + jnp.arange(
        own_rows, dtype=jnp.int32
    )
    key_rows = rotate(key_sum, positions).astype(jnp.bfloat16)
    value_rows = value_sum.astype(jnp.bfloat16)
    return (key_rows, value_rows)


def solution(mesh):
    placed = (P(("dp", "row", "col"), None), P(), P("row", "col"), P("row", "col"))
    return jax.shard_map(
        body,
        mesh=mesh,
        in_specs=placed,
        out_specs=(P(("dp", "row", "col"), None), P(("dp", "row", "col"), None)),
        check_vma=False,
    )
```

profile of v0, /device:TPU:0, one launch (start us, length us, event | category | flops | bytes accessed | tf_op | source)
XLA Modules:
  0.0 233.3 jit_solution(15419187633096253787)
XLA Ops:
  7.2 0.0 all-gather.3.cloned.1.call-start
  7.2 0.7 all-gather.3.cloned.1.call-update
  7.9 0.0 all-gather.5.cloned.1.call-start
  7.9 0.7 all-gather.5.cloned.1.call-update
  8.6 0.0 reduce-scatter.3.cloned.1.call-start
  8.7 3.2 %copy.6 = bf16[128,8192]{0,1:T(8,128)(2,1)S(1)} copy(bf16[128,8192]{1,0:T(8,128)(2,1)} %param.4) | data formatting | bytes 4194304 | tf_op args[0]
  11.9 0.0 copy-start.1
  11.9 1.1 fusion
  13.0 0.0 copy-done.1
  13.0 3.5 %fusion.2 = bf16[128,8192]{0,1:T(8,128)(2,1)S(1)} fusion(bf16[128,8192]{0,1:T(8,128)(2,1)S(1)} %copy.6, f32[8192]{0:T(1024)S(1)} %copy-done.1, f32[128]{0:T(128)S(1)} %add_rsqrt_fusion), kind=kLoop, calls=%fused_computation.4 | loop fusion | flops 4194304 | bytes 4227584 | tf_op jit(solution)/shard_map/convert_element_type | solution.py:36
  16.5 29.7 %all_to_all.19 = bf16[128,4,2048]{0,2,1:T(8,128)(2,1)S(1)} all-to-all(bf16[128,4,2048]{0,2,1:T(8,128)(2,1)S(1)} %bitcast.14), channel_id=1, replica_groups=mesh['dp'=2,'row'=4,'col'=4] {'row'}, dimensions={1} | all-to-all | bytes 4194304 | tf_op jit(solution)/shard_map/all_to_all | solution.py:37
  46.3 2.7 %copy.7 = bf16[4,128,2048]{2,1,0:T(8,128)(2,1)} copy(bf16[4,128,2048]{1,2,0:T(8,128)(2,1)S(1)} %bitcast.15) | data formatting | bytes 4194304 | tf_op jit(solution)/shard_map/all_to_all | solution.py:37
  49.0 43.9 %all-gather.3.cloned.1.call-done = bf16[2048,1024]{1,0:T(8,128)(2,1)} async-done(((bf16[2048,256]{1,0:T(8,128)(2,1)}), bf16[2048,1024]{1,0:T(8,128)(2,1)}) %all-gather.3.cloned.1.call-update) | async-done | bytes 4194320 | tf_op jit(solution)/shard_map/all_gather | solution.py:39
  92.9 0.0 copy-start
  92.9 6.3 %convolution_convert_fusion.1 = bf16[512,1024]{1,0:T(8,128)(2,1)} fusion(bf16[512,2048]{1,0:T(8,128)(2,1)} %bitcast.17, bf16[2048,1024]{1,0:T(8,128)(2,1)} %all-gather.3.cloned.1.call-done), kind=kOutput, calls=%fused_computation.6 | convolution fusion | flops 2148007936 | bytes 7340032 | tf_op jit(solution)/shard_map/dot_general | solution.py:42
  99.1 0.0 reduce-scatter.3.cloned.1.call-update
  99.2 0.0 reduce-scatter.5.cloned.1.call-start
  99.2 74.0 %all-gather.5.cloned.1.call-done = bf16[2048,1024]{1,0:T(8,128)(2,1)} async-done(((bf16[2048,256]{1,0:T(8,128)(2,1)}), bf16[2048,1024]{1,0:T(8,128)(2,1)}) %all-gather.5.cloned.1.call-update) | async-done | bytes 4194320 | tf_op jit(solution)/shard_map/all_gather | solution.py:40
  173.2 0.0 copy-done
  173.2 5.5 %convolution_convert_fusion = bf16[512,1024]{1,0:T(8,128)(2,1)} fusion(bf16[512,2048]{1,0:T(8,128)(2,1)S(1)} %bitcast.18, bf16[2048,1024]{1,0:T(8,128)(2,1)} %all-gather.5.cloned.1.call-done), kind=kOutput, calls=%fused_computation.5 | convolution fusion | flops 2148007936 | bytes 7340032 | tf_op jit(solution)/shard_map/dot_general | solution.py:43
  178.7 0.0 reduce-scatter.5.cloned.1.call-update
  178.7 0.3 multiply_cosine_fusion
  179.1 19.7 %reduce-scatter.3.cloned.1.call-done = bf16[128,1024]{1,0:T(8,128)(2,1)} async-done(((bf16[512,1024]{1,0:T(8,128)(2,1)}), bf16[128,1024]{1,0:T(8,128)(2,1)}) %reduce-scatter.3.cloned.1.call-update) | async-done | bytes 262160 | tf_op jit(solution)/shard_map/reduce_scatter | solution.py:45
  198.8 1.0 convert_bitcast_fusion
  199.8 0.1 copy.8
  199.9 0.3 subtract_convert_fusion
  200.2 0.1 pad_maximum_fusion
  200.3 0.8 copy.11
  201.1 25.7 %reduce-scatter.5.cloned.1.call-done = bf16[128,1024]{1,0:T(8,128)(2,1)} async-done(((bf16[512,1024]{1,0:T(8,128)(2,1)}), bf16[128,1024]{1,0:T(8,128)(2,1)}) %reduce-scatter.5.cloned.1.call-update) | async-done | bytes 262160 | tf_op jit(solution)/shard_map/reduce_scatter | solution.py:48
  (3 shorter events, 0.0 us)
Async XLA Ops:
  7.2 85.7 %all-gather.3.cloned.1.call-start = ((), (), s32[]{:S(2)}) async-start(), calls=%async_computation.3 | async-start | bytes 5242880 | tf_op jit(solution)/shard_map/all_gather | solution.py:39
  7.9 165.3 %all-gather.5.cloned.1.call-start = ((), (), s32[]{:S(2)}) async-start(), calls=%async_computation.5 | async-start | bytes 5242880 | tf_op jit(solution)/shard_map/all_gather | solution.py:40
  8.6 190.2 %reduce-scatter.3.cloned.1.call-start = ((), (), s32[]{:S(2)}) async-start(), calls=%async_computation.4 | async-start | bytes 1310720 | tf_op jit(solution)/shard_map/reduce_scatter | solution.py:45
  11.9 1.1 copy-start.1
  92.9 80.3 %copy-start = (bf16[4,128,2048]{2,1,0:T(8,128)(2,1)S(1)}, bf16[4,128,2048]{2,1,0:T(8,128)(2,1)}, u32[]{:S(2)}) copy-start(bf16[4,128,2048]{2,1,0:T(8,128)(2,1)} %copy.7) | copy-start | bytes 6291460
  99.2 127.6 %reduce-scatter.5.cloned.1.call-start = ((), (), s32[]{:S(2)}) async-start(), calls=%async_computation.6 | async-start | bytes 1310720 | tf_op jit(solution)/shard_map/reduce_scatter | solution.py:48
Sparse Core Ops, SparseCore 0:
  9.6 83.2 all-gather.2
  94.4 78.7 all-gather.4
  175.7 23.0 reduce-scatter.2
  201.9 24.8 reduce-scatter.4
where the time goes:
time: 234 us; the launch traced here: 233 us
  waiting for transfers between devices  165 us (71%)
  blocking collectives  29.7 us (13%)
  between operations  13.8 us (6%)
  matrix products  11.8 us (5%)
  local copies, waits for them, and re-layouts  6.78 us (3%)
  other arithmetic  6.31 us (3%)
    all_gather x1, waiting for transfers between devices, body(): lax.all_gather(w_value, 'col', axis=1, tiled=True)  74 us
    all_gather x1, waiting for transfers between devices, body(): lax.all_gather(w_key, 'col', axis=1, tiled=True)  43.9 us
    all_to_all x1, blocking collectives, body(): lax.all_to_all(normed, 'row', split_axis=1, concat_axis=0, tiled=True)  29.7 us
    reduce_scatter x1, waiting for transfers between devices, body(): lax.psum_scatter(value_part.astype(jnp.bfloat16), 'row', scatter_dimensio...  25.7 us
    reduce_scatter x1, waiting for transfers between devices, body(): lax.psum_scatter(key_part.astype(jnp.bfloat16), 'row', scatter_dimension=...  19.7 us
    dot_general x1, matrix products, body(): key_part = jnp.dot(tile, key_weights, preferred_element_type=jnp.float32)  6.28 us
    dot_general x1, matrix products, body(): jnp.dot(tile, value_weights, preferred_element_type=jnp.float32)  5.49 us
  transfers between devices with their start and end apart: 4, of which 4 were waited for; matrix products, arithmetic and copies ran while one was open for 11% of the time, Pallas kernels for 0%

commit v1 on v0

--- a/solution.py
+++ b/solution.py
@@ -27,28 +27,94 @@
 
 
 def body(tokens, norm_gain, w_key, w_value):
+    dp_count = lax.axis_size("dp")
+    row_count = lax.axis_size("row")
     col_count = lax.axis_size("col")
+    dp_index = lax.axis_index("dp")
     row_index = lax.axis_index("row")
     col_index = lax.axis_index("col")
-    own_rows = tokens.shape[0]
+    own_rows, features = tokens.shape
+    block, width = w_key.shape
+    pair_count = 2 if dp_count % 2 == 0 else 1
+    pair_index = dp_index % pair_count
+    part = block // pair_count
+
+    def swap(array, row_bits, pair_bits):
+        pairs = []
+        for d in range(dp_count):
+            for r in range(row_count):
+                target = (d ^ pair_bits) * row_count + (r ^ row_bits)
+                pairs.append((d * row_count + r, target))
+        return lax.ppermute(array, ("dp", "row"), pairs)
+
+    def shift(array, step, sources):
+        return lax.ppermute(array, "col", [(i, i + step) for i in sources])
+
+    start = pair_index * part
+    own_weights = jnp.concatenate(
+        [
+            lax.dynamic_slice_in_dim(w_key, start, part, 0),
+            lax.dynamic_slice_in_dim(w_value, start, part, 0),
+        ],
+        axis=1,
+    )
+    groups = [[own_weights]]
+    from_left, from_right = own_weights, own_weights
+    for s in range(1, col_count):
+        from_left = shift(from_left, 1, range(s - 1, col_count - 1))
+        from_right = shift(from_right, -1, range(1, col_count - s + 1))
+        if 2 * s < col_count:
+            groups.append([from_left, from_right])
+        else:
+            groups.append([jnp.where(col_index >= s, from_left, from_right)])
+
     widened = tokens.astype(jnp.float32)
     inverse_rms = lax.rsqrt(jnp.mean(widened * widened, axis=1, keepdims=True) + 1e-05)
     normed = (widened * inverse_rms * norm_gain[None, :]).astype(jnp.bfloat16)
-    tile = lax.all_to_all(normed, "row", split_axis=1, concat_axis=0, tiled=True)
-    key_weights, value_weights = (
-        lax.all_gather(w_key, "col", axis=1, tiled=True),
-        lax.all_gather(w_value, "col", axis=1, tiled=True),
-    )
-    key_part = jnp.dot(tile, key_weights, preferred_element_type=jnp.float32)
-    value_part = jnp.dot(tile, value_weights, preferred_element_type=jnp.float32)
-    key_sum, value_sum = (
-        lax.psum_scatter(
-            key_part.astype(jnp.bfloat16), "row", scatter_dimension=0, tiled=True
-        ).astype(jnp.float32),
-        lax.psum_scatter(
-            value_part.astype(jnp.bfloat16), "row", scatter_dimension=0, tiled=True
-        ).astype(jnp.float32),
-    )
+    order = [(r, d) for odd in (1, 0) for r in range(odd, row_count, 2) for d in range(pair_count)]
+    half = len(order) // 2
+    received = []
+    for r, d in order:
+        index = (row_index ^ r) * pair_count + (pair_index ^ d)
+        piece = lax.dynamic_slice_in_dim(normed, index * part, part, 1)
+        received.append(piece if (r, d) == (0, 0) else swap(piece, r, d))
+    far = jnp.concatenate(received[:half], axis=0)
+    near = jnp.concatenate(received[half:], axis=0)
+
+    def reduce(weights):
+        n = weights.shape[1]
+        far_part = jnp.dot(far, weights, preferred_element_type=jnp.float32).astype(jnp.bfloat16)
+        other = swap(far_part, 1, 0)
+        near_part = jnp.dot(near, weights, preferred_element_type=jnp.float32)
+        both = (near_part + other.astype(jnp.float32)).astype(jnp.bfloat16)
+        both = both.reshape(half, own_rows, n)
+        total = both[0].astype(jnp.float32)
+        for k in range(1, half):
+            r, d = order[half + k]
+            total = total + swap(both[k], r, d).astype(jnp.float32)
+        return total
+
+    slots = []
+    for group in groups:
+        total = reduce(group[0] if len(group) == 1 else jnp.concatenate(group, axis=1))
+        slots += [total[:, i * 2 * width : (i + 1) * 2 * width] for i in range(len(group))]
+    stack = jnp.stack(slots)
+    ordered = []
+    for b in range(col_count):
+        distance = jnp.abs(col_index - b)
+        paired = (col_count - 1) // 2
+        slot = jnp.where(
+            distance == 0,
+            0,
+            jnp.where(
+                distance <= paired,
+                2 * distance - 1 + (b > col_index),
+                distance + paired,
+            ),
+        )
+        ordered.append(lax.dynamic_index_in_dim(stack, slot, 0, keepdims=False))
+    key_sum = jnp.concatenate([o[:, :width] for o in ordered], axis=1)
+    value_sum = jnp.concatenate([o[:, width:] for o in ordered], axis=1)
     positions = (row_index * col_count + col_index) * own_rows + jnp.arange(
         own_rows, dtype=jnp.int32
     )

time: 234 us -> 121 us (0.52)
  waiting for transfers between devices: 165 us -> 64.5 us
  starting transfers between devices: 0.16 us -> 34.7 us
  blocking collectives: 29.7 us -> 0 us
  between operations: 13.8 us -> 1.39 us
    all_gather x2 -> x0, waiting for transfers between devices: 118 us -> none  [the longest x1 74 us: body(): lax.all_gather(w_value, 'col', axis=1, tiled=True)]
    ppermute x0 -> x29, waiting for transfers between devices: none -> 64.5 us  [the longest x6 37.2 us: shift(): return lax.ppermute(array, 'col', [(i, i + step) for i in sources])]
    reduce_scatter x2 -> x0, waiting for transfers between devices: 45.5 us -> none  [the longest x1 25.7 us: body(): lax.psum_scatter(value_part.astype(jnp.bfloat16), 'row', scatter_dimensio...]
    ppermute x0 -> x29, starting transfers between devices: none -> 34.7 us  [the longest x23 23.3 us: swap(): return lax.ppermute(array, ('dp', 'row'), pairs)]
    all_to_all x1 -> x0, blocking collectives: 29.7 us -> none  [body(): lax.all_to_all(normed, 'row', split_axis=1, concat_axis=0, tiled=True)]
    convert_element_type x1, other arithmetic: 3.48 us -> 0.58 us  [body(): normed = (widened * inverse_rms * norm_gain[None, :]).astype(jnp.bfloat16)]
    all_to_all x1 -> x0, local copies, waits for them, and re-layouts: 2.7 us -> none  [body(): lax.all_to_all(normed, 'row', split_axis=1, concat_axis=0, tiled=True)]
    dot_general x2 -> x8, matrix products: 11.8 us -> 10.4 us  [the longest x4 5.8 us: reduce(): near_part = jnp.dot(near, weights, preferred_element_type=jnp.float32)]
  transfers between devices with their start and end apart: 4 -> 29, of which waited for: 4 -> 11; matrix products, arithmetic and copies ran while one was open for 11% -> 12% of each run, Pallas kernels for 0% -> 0%
where the time goes in v1:
time: 121 us
  waiting for transfers between devices  64.5 us (53%)
  starting transfers between devices  34.7 us (29%)
  matrix products  10.4 us (9%)
  local copies, waits for them, and re-layouts  6.25 us (5%)
  other arithmetic  4 us (3%)
  between operations  1.39 us (1%)
    ppermute x6, waiting for transfers between devices, shift(): return lax.ppermute(array, 'col', [(i, i + step) for i in sources])  37.2 us
    ppermute x23, waiting for transfers between devices, swap(): return lax.ppermute(array, ('dp', 'row'), pairs)  27.3 us
    ppermute x23, starting transfers between devices, swap(): return lax.ppermute(array, ('dp', 'row'), pairs)  23.3 us
    ppermute x6, starting transfers between devices, shift(): return lax.ppermute(array, 'col', [(i, i + step) for i in sources])  11.4 us
    dot_general x4, matrix products, reduce(): near_part = jnp.dot(near, weights, preferred_element_type=jnp.float32)  5.8 us
    dot_general x4, matrix products, reduce(): jnp.dot(far, weights, preferred_element_type=jnp.float32)  4.57 us
    unnamed x32, local copies, waits for them, and re-layouts  3.45 us
  transfers between devices with their start and end apart: 29, of which 11 were waited for; matrix products, arithmetic and copies ran while one was open for 12% of the time, Pallas kernels for 0%

profile of v1, /device:TPU:0, one launch (start us, length us, event | category | flops | bytes accessed | tf_op | source)
XLA Modules:
  0.0 121.2 jit_solution(3795170851095276532)
XLA Ops:
  0.7 1.4 %constant_dynamic-slice_fusion.8 = (bf16[1024,256]{1,0:T(8,128)(2,1)S(1)}, bf16[1024,256]{1,0:T(8,128)(2,1)S(1)}) fusion(bf16[2048,256]{1,0:T(8,128)(2,1)} %param.7, s32[]{:T(128)S(6)} %select_n.92, bf16[2048,256]{1,0:T(8,128)(2,1)} %param.6), kind=kLoop, calls=%fused_computation.54 | loop fusion | bytes 2097156 | tf_op jit(solution)/shard_map/dynamic_slice | solution.py:57
  2.1 1.1 pad_maximum_fusion.1
  3.2 5.9 %collective-permute-start.11 = (bf16[1024,512]{1,0:T(8,128)(2,1)}, bf16[1024,512]{1,0:T(8,128)(2,1)}, u32[]{:S(2)}, u32[]{:S(2)}) collective-permute-start(bf16[1024,512]{1,0:T(8,128)(2,1)} %pad_maximum_fusion.1), channel_id=1, source_target_pairs={{0,1},{1,2},{2,3},{4,5},{5,6},{6,7},{8,9},{9,10},{10,11},{12,13},{... | collective-permute-start | bytes 3145736 | tf_op jit(solution)/shard_map/ppermute | solution.py:51
  9.1 0.5 fusion
  9.6 1.1 copy-done.1
  10.7 0.6 fusion.2
  11.6 1.3 %collective-permute-start.12 = (bf16[1024,512]{1,0:T(8,128)(2,1)}, bf16[1024,512]{1,0:T(8,128)(2,1)S(1)}, u32[]{:S(2)}, u32[]{:S(2)}) collective-permute-start(bf16[1024,512]{1,0:T(8,128)(2,1)} %pad_maximum_fusion.1), channel_id=1, source_target_pairs={{1,0},{2,1},{3,2},{5,4},{6,5},{7,6},{9,8},{10,9},{11,10},{13,12},{... | collective-permute-start | bytes 3145736 | tf_op jit(solution)/shard_map/ppermute | solution.py:51
  12.9 1.6 %collective-permute-start.4 = (bf16[128,1024]{1,0:T(8,128)(2,1)S(1)}, bf16[128,1024]{1,0:T(8,128)(2,1)S(1)}, u32[]{:S(2)}, u32[]{:S(2)}) collective-permute-start(bf16[128,1024]{1,0:T(8,128)(2,1)S(1)} %get-tuple-element.5), channel_id=1, source_target_pairs={{0,20},{4,16},{8,28},{12,24},{16,4},{20,0},{24,12},{28,8},{1,21},{... | collective-permute-start | bytes 786440 | tf_op jit(solution)/shard_map/ppermute | solution.py:48
  14.5 1.1 collective-permute-start.5
  15.7 0.6 collective-permute-start.6
  16.3 4.9 %collective-permute-done.4 = bf16[128,1024]{1,0:T(8,128)(2,1)S(1)} collective-permute-done((bf16[128,1024]{1,0:T(8,128)(2,1)S(1)}, bf16[128,1024]{1,0:T(8,128)(2,1)S(1)}, u32[]{:S(2)}, u32[]{:S(2)}) %collective-permute-start.4) | collective-permute-done | bytes 262176 | tf_op jit(solution)/shard_map/ppermute | solution.py:48
  21.2 2.2 %collective-permute-start.2 = (bf16[128,1024]{1,0:T(8,128)(2,1)S(1)}, bf16[128,1024]{1,0:T(8,128)(2,1)S(1)}, u32[]{:S(2)}, u32[]{:S(2)}) collective-permute-start(bf16[128,1024]{1,0:T(8,128)(2,1)S(1)} %get-tuple-element.7), channel_id=1, source_target_pairs={{0,24},{4,28},{8,16},{12,20},{16,8},{20,12},{24,0},{28,4},{1,25},{... | collective-permute-start | bytes 786440 | tf_op jit(solution)/shard_map/ppermute | solution.py:48
  23.4 10.8 %collective-permute-done.5 = bf16[128,1024]{1,0:T(8,128)(2,1)S(1)} collective-permute-done((bf16[128,1024]{1,0:T(8,128)(2,1)S(1)}, bf16[128,1024]{1,0:T(8,128)(2,1)S(1)}, u32[]{:S(2)}, u32[]{:S(2)}) %collective-permute-start.5) | collective-permute-done | bytes 262176 | tf_op jit(solution)/shard_map/ppermute | solution.py:48
  34.2 1.5 %collective-permute-start.1 = (bf16[128,1024]{1,0:T(8,128)(2,1)S(1)}, bf16[128,1024]{1,0:T(8,128)(2,1)S(1)}, u32[]{:S(2)}, u32[]{:S(2)}) collective-permute-start(bf16[128,1024]{1,0:T(8,128)(2,1)S(1)} %get-tuple-element.8), channel_id=1, source_target_pairs={{0,8},{4,12},{8,0},{12,4},{16,24},{20,28},{24,16},{28,20},{1,9},{5... | collective-permute-start | bytes 786440 | tf_op jit(solution)/shard_map/ppermute | solution.py:48
  35.7 0.6 collective-permute-start
  36.3 0.8 convolution_convert_fusion.3
  37.2 1.4 %constant_dynamic-update-slice_fusion.5 = bf16[1024,1024]{1,0:T(8,128)(2,1)S(1)} fusion(bf16[1024,512]{1,0:T(8,128)(2,1)} %collective-permute-done.11), kind=kLoop, calls=%fused_computation.45 | loop fusion | bytes 2097152
  38.6 0.6 collective-permute-done.12
  39.4 2.3 %convolution_convert_fusion = bf16[512,1024]{0,1:T(8,128)(2,1)} fusion(bf16[512,1024]{1,0:T(8,128)(2,1)S(1)} %constant_dynamic-update-slice_fusion, bf16[1024,1024]{1,0:T(8,128)(2,1)S(1)} %constant_dynamic-update-slice_fusion.4), kind=kOutput, calls=%fused_computation.6 | convolution fusion | flops 1074266112 | bytes 4194304 | tf_op jit(solution)/shard_map/dot_general | solution.py:86
  41.7 1.0 collective-permute-done.1
  42.7 1.3 %collective-permute-done = bf16[128,1024]{1,0:T(8,128)(2,1)S(1)} collective-permute-done((bf16[128,1024]{1,0:T(8,128)(2,1)S(1)}, bf16[128,1024]{1,0:T(8,128)(2,1)S(1)}, u32[]{:S(2)}, u32[]{:S(2)}) %collective-permute-start) | collective-permute-done | bytes 262176 | tf_op jit(solution)/shard_map/ppermute | solution.py:48
  44.0 0.8 fusion.3
  45.3 1.8 %collective-permute-start.9 = (bf16[128,512]{0,1:T(8,128)(2,1)S(1)}, bf16[128,512]{0,1:T(8,128)(2,1)S(1)}, u32[]{:S(2)}, u32[]{:S(2)}) collective-permute-start(bf16[128,512]{0,1:T(8,128)(2,1)S(1)} %get-tuple-element.27), channel_id=1, source_target_pairs={{0,8},{4,12},{8,0},{12,4},{16,24},{20,28},{24,16},{28,20},{1,9},{5... | collective-permute-start | bytes 393224 | tf_op jit(solution)/shard_map/ppermute | solution.py:48
  47.1 1.5 %collective-permute-start.8 = (bf16[128,512]{0,1:T(8,128)(2,1)S(1)}, bf16[128,512]{0,1:T(8,128)(2,1)S(1)}, u32[]{:S(2)}, u32[]{:S(2)}) collective-permute-start(bf16[128,512]{0,1:T(8,128)(2,1)S(1)} %get-tuple-element.25), channel_id=1, source_target_pairs={{0,16},{4,20},{8,24},{12,28},{16,0},{20,4},{24,8},{28,12},{1,17},{... | collective-permute-start | bytes 393224 | tf_op jit(solution)/shard_map/ppermute | solution.py:48
  48.6 0.7 collective-permute-start.17
  49.4 2.8 %collective-permute-done.10 = bf16[128,512]{0,1:T(8,128)(2,1)S(1)} collective-permute-done((bf16[128,512]{0,1:T(8,128)(2,1)S(1)}, bf16[128,512]{0,1:T(8,128)(2,1)S(1)}, u32[]{:S(2)}, u32[]{:S(2)}) %collective-permute-start.10) | collective-permute-done | bytes 131104 | tf_op jit(solution)/shard_map/ppermute | solution.py:48
  52.2 1.3 %collective-permute-start.18 = (bf16[1024,512]{1,0:T(8,128)(2,1)S(1)}, bf16[1024,512]{1,0:T(8,128)(2,1)S(1)}, u32[]{:S(2)}, u32[]{:S(2)}) collective-permute-start(bf16[1024,512]{1,0:T(8,128)(2,1)S(1)} %collective-permute-done.12), channel_id=1, source_target_pairs={{1,0},{2,1},{5,4},{6,5},{9,8},{10,9},{13,12},{14,13},{17,16},{18,1... | collective-permute-start | bytes 3145736 | tf_op jit(solution)/shard_map/ppermute | solution.py:51
  53.9 3.5 %add_convert_fusion = bf16[512,1024]{0,1:T(8,128)(2,1)S(1)} fusion(bf16[512,1024]{0,1:T(8,128)(2,1)} %collective-permute-done.13, bf16[1024,1024]{1,0:T(8,128)(2,1)} %copy-done.2, bf16[128,1024]{1,0:T(8,128)(2,1)} %copy-done.6, bf16[128,1024]{1,0:T(8,128)(2,1)} %copy-done.8, bf16[128,1024]{1,0:T(8,128)(2,1)} %copy-done.10, ...), kind=kOutput, calls=%fused_computation.5 | convolution fusion | flops 1079508992 | bytes 5242880 | tf_op jit(solution)/shard_map/dot_general | solution.py:88
  57.5 1.1 collective-permute-start.16
  58.6 1.0 collective-permute-start.15
  59.6 1.5 %collective-permute-start.14 = (bf16[128,1024]{0,1:T(8,128)(2,1)S(1)}, bf16[128,1024]{0,1:T(8,128)(2,1)S(1)}, u32[]{:S(2)}, u32[]{:S(2)}) collective-permute-start(bf16[128,1024]{0,1:T(8,128)(2,1)S(1)} %get-tuple-element.14), channel_id=1, source_target_pairs={{0,16},{4,20},{8,24},{12,28},{16,0},{20,4},{24,8},{28,12},{1,17},{... | collective-permute-start | bytes 786440 | tf_op jit(solution)/shard_map/ppermute | solution.py:48
  61.1 0.7 collective-permute-start.23
  61.8 15.4 %collective-permute-done.18 = bf16[1024,512]{1,0:T(8,128)(2,1)S(1)} collective-permute-done((bf16[1024,512]{1,0:T(8,128)(2,1)S(1)}, bf16[1024,512]{1,0:T(8,128)(2,1)S(1)}, u32[]{:S(2)}, u32[]{:S(2)}) %collective-permute-start.18) | collective-permute-done | bytes 1048608 | tf_op jit(solution)/shard_map/ppermute | solution.py:51
  77.2 1.5 %collective-permute-start.24 = (bf16[1024,512]{1,0:T(8,128)(2,1)S(1)}, bf16[1024,512]{1,0:T(8,128)(2,1)S(1)}, u32[]{:S(2)}, u32[]{:S(2)}) collective-permute-start(bf16[1024,512]{1,0:T(8,128)(2,1)S(1)} %collective-permute-done.18), channel_id=1, source_target_pairs={{1,0},{5,4},{9,8},{13,12},{17,16},{21,20},{25,24},{29,28}} | collective-permute-start | bytes 3145736 | tf_op jit(solution)/shard_map/ppermute | solution.py:51
  78.7 0.8 convolution_convert_fusion.2
  79.8 21.1 %collective-permute-done.24 = bf16[1024,512]{1,0:T(8,128)(2,1)S(1)} collective-permute-done((bf16[1024,512]{1,0:T(8,128)(2,1)S(1)}, bf16[1024,512]{1,0:T(8,128)(2,1)S(1)}, u32[]{:S(2)}, u32[]{:S(2)}) %collective-permute-start.24) | collective-permute-done | bytes 1048608 | tf_op jit(solution)/shard_map/ppermute | solution.py:51
  100.9 0.8 convolution_convert_fusion.1
  101.8 0.8 fusion.4
  102.7 3.0 %collective-permute-start.22 = (bf16[128,512]{0,1:T(8,128)(2,1)S(1)}, bf16[128,512]{0,1:T(8,128)(2,1)S(1)}, u32[]{:S(2)}, u32[]{:S(2)}) collective-permute-start(bf16[128,512]{0,1:T(8,128)(2,1)S(1)} %get-tuple-element.23), channel_id=1, source_target_pairs={{0,24},{4,28},{8,16},{12,20},{16,8},{20,12},{24,0},{28,4},{1,25},{... | collective-permute-start | bytes 393224 | tf_op jit(solution)/shard_map/ppermute | solution.py:48
  105.9 0.4 collective-permute-start.20
  106.3 0.8 fusion.5
  107.2 2.9 %collective-permute-start.28 = (bf16[128,512]{0,1:T(8,128)(2,1)S(1)}, bf16[128,512]{0,1:T(8,128)(2,1)S(1)}, u32[]{:S(2)}, u32[]{:S(2)}) collective-permute-start(bf16[128,512]{0,1:T(8,128)(2,1)S(1)} %get-tuple-element.20), channel_id=1, source_target_pairs={{0,24},{4,28},{8,16},{12,20},{16,8},{20,12},{24,0},{28,4},{1,25},{... | collective-permute-start | bytes 393224 | tf_op jit(solution)/shard_map/ppermute | solution.py:48
  110.4 1.4 %collective-permute-start.26 = (bf16[128,512]{0,1:T(8,128)(2,1)S(1)}, bf16[128,512]{0,1:T(8,128)(2,1)S(1)}, u32[]{:S(2)}, u32[]{:S(2)}) collective-permute-start(bf16[128,512]{0,1:T(8,128)(2,1)S(1)} %get-tuple-element.19), channel_id=1, source_target_pairs={{0,16},{4,20},{8,24},{12,28},{16,0},{20,4},{24,8},{28,12},{1,17},{... | collective-permute-start | bytes 393224 | tf_op jit(solution)/shard_map/ppermute | solution.py:48
  111.7 1.9 %collective-permute-done.21 = bf16[128,512]{0,1:T(8,128)(2,1)S(1)} collective-permute-done((bf16[128,512]{0,1:T(8,128)(2,1)S(1)}, bf16[128,512]{0,1:T(8,128)(2,1)S(1)}, u32[]{:S(2)}, u32[]{:S(2)}) %collective-permute-start.21) | collective-permute-done | bytes 131104 | tf_op jit(solution)/shard_map/ppermute | solution.py:48
  113.7 2.7 %collective-permute-done.28 = bf16[128,512]{0,1:T(8,128)(2,1)S(1)} collective-permute-done((bf16[128,512]{0,1:T(8,128)(2,1)S(1)}, bf16[128,512]{0,1:T(8,128)(2,1)S(1)}, u32[]{:S(2)}, u32[]{:S(2)}) %collective-permute-start.28) | collective-permute-done | bytes 131104 | tf_op jit(solution)/shard_map/ppermute | solution.py:48
  116.4 1.9 %collective-permute-done.27 = bf16[128,512]{0,1:T(8,128)(2,1)S(1)} collective-permute-done((bf16[128,512]{0,1:T(8,128)(2,1)S(1)}, bf16[128,512]{0,1:T(8,128)(2,1)S(1)}, u32[]{:S(2)}, u32[]{:S(2)}) %collective-permute-start.27) | collective-permute-done | bytes 131104 | tf_op jit(solution)/shard_map/ppermute | solution.py:48
  119.7 0.8 copy.28
  120.5 0.7 pad_maximum_fusion.3
  (86 shorter events, 3.9 us)
Async XLA Ops:
  0.6 8.4 %copy-start = (bf16[128,8192]{1,0:T(8,128)(2,1)S(1)}, bf16[128,8192]{1,0:T(8,128)(2,1)}, u32[]{:S(2)}) copy-start(bf16[128,8192]{1,0:T(8,128)(2,1)} %param.4) | copy-start | bytes 6291460
  2.1 7.5 %copy-start.5 = (f32[8192]{0:T(1024)S(1)}, f32[8192]{0:T(1024)}, u32[]{:S(2)}) copy-start(f32[8192]{0:T(1024)} %param.5) | copy-start | bytes 98308
  3.2 33.9 %collective-permute-start.11 = (bf16[1024,512]{1,0:T(8,128)(2,1)}, bf16[1024,512]{1,0:T(8,128)(2,1)}, u32[]{:S(2)}, u32[]{:S(2)}) collective-permute-start(bf16[1024,512]{1,0:T(8,128)(2,1)} %pad_maximum_fusion.1), channel_id=1, source_target_pairs={{0,1},{1,2},{2,3},{4,5},{5,6},{6,7},{8,9},{9,10},{10,11},{12,13},{... | collective-permute-start | bytes 3145736 | tf_op jit(solution)/shard_map/ppermute | solution.py:51
  9.1 1.6 %copy-start.1 = (bf16[128,8192]{1,0:T(8,128)(2,1)S(1)}, bf16[128,8192]{1,0:T(8,128)(2,1)}, u32[]{:S(2)}) copy-start(bf16[128,8192]{1,0:T(8,128)(2,1)} %param.4) | copy-start | bytes 6291460
  11.5 4.2 %collective-permute-start.3 = (bf16[128,1024]{1,0:T(8,128)(2,1)S(1)}, bf16[128,1024]{1,0:T(8,128)(2,1)S(1)}, u32[]{:S(2)}, u32[]{:S(2)}) collective-permute-start(bf16[128,1024]{1,0:T(8,128)(2,1)S(1)} %get-tuple-element.6), channel_id=1, source_target_pairs={{0,4},{4,0},{8,12},{12,8},{16,20},{20,16},{24,28},{28,24},{1,5},{5... | collective-permute-start | bytes 786440 | tf_op jit(solution)/shard_map/ppermute | solution.py:48
  11.6 27.7 %collective-permute-start.12 = (bf16[1024,512]{1,0:T(8,128)(2,1)}, bf16[1024,512]{1,0:T(8,128)(2,1)S(1)}, u32[]{:S(2)}, u32[]{:S(2)}) collective-permute-start(bf16[1024,512]{1,0:T(8,128)(2,1)} %pad_maximum_fusion.1), channel_id=1, source_target_pairs={{1,0},{2,1},{3,2},{5,4},{6,5},{7,6},{9,8},{10,9},{11,10},{13,12},{... | collective-permute-start | bytes 3145736 | tf_op jit(solution)/shard_map/ppermute | solution.py:51
  12.9 8.3 %collective-permute-start.4 = (bf16[128,1024]{1,0:T(8,128)(2,1)S(1)}, bf16[128,1024]{1,0:T(8,128)(2,1)S(1)}, u32[]{:S(2)}, u32[]{:S(2)}) collective-permute-start(bf16[128,1024]{1,0:T(8,128)(2,1)S(1)} %get-tuple-element.5), channel_id=1, source_target_pairs={{0,20},{4,16},{8,28},{12,24},{16,4},{20,0},{24,12},{28,8},{1,21},{... | collective-permute-start | bytes 786440 | tf_op jit(solution)/shard_map/ppermute | solution.py:48
  14.5 19.6 %collective-permute-start.5 = (bf16[128,1024]{1,0:T(8,128)(2,1)S(1)}, bf16[128,1024]{1,0:T(8,128)(2,1)S(1)}, u32[]{:S(2)}, u32[]{:S(2)}) collective-permute-start(bf16[128,1024]{1,0:T(8,128)(2,1)S(1)} %get-tuple-element.4), channel_id=1, source_target_pairs={{0,12},{4,8},{8,4},{12,0},{16,28},{20,24},{24,20},{28,16},{1,13},{... | collective-permute-start | bytes 786440 | tf_op jit(solution)/shard_map/ppermute | solution.py:48
  15.7 20.0 %collective-permute-start.6 = (bf16[128,1024]{1,0:T(8,128)(2,1)S(1)}, bf16[128,1024]{1,0:T(8,128)(2,1)S(1)}, u32[]{:S(2)}, u32[]{:S(2)}) collective-permute-start(bf16[128,1024]{1,0:T(8,128)(2,1)S(1)} %get-tuple-element.3), channel_id=1, source_target_pairs={{0,28},{4,24},{8,20},{12,16},{16,12},{20,8},{24,4},{28,0},{1,29},{... | collective-permute-start | bytes 786440 | tf_op jit(solution)/shard_map/ppermute | solution.py:48
  21.2 20.5 %collective-permute-start.2 = (bf16[128,1024]{1,0:T(8,128)(2,1)S(1)}, bf16[128,1024]{1,0:T(8,128)(2,1)S(1)}, u32[]{:S(2)}, u32[]{:S(2)}) collective-permute-start(bf16[128,1024]{1,0:T(8,128)(2,1)S(1)} %get-tuple-element.7), channel_id=1, source_target_pairs={{0,24},{4,28},{8,16},{12,20},{16,8},{20,12},{24,0},{28,4},{1,25},{... | collective-permute-start | bytes 786440 | tf_op jit(solution)/shard_map/ppermute | solution.py:48
  34.2 8.5 %collective-permute-start.1 = (bf16[128,1024]{1,0:T(8,128)(2,1)S(1)}, bf16[128,1024]{1,0:T(8,128)(2,1)S(1)}, u32[]{:S(2)}, u32[]{:S(2)}) collective-permute-start(bf16[128,1024]{1,0:T(8,128)(2,1)S(1)} %get-tuple-element.8), channel_id=1, source_target_pairs={{0,8},{4,12},{8,0},{12,4},{16,24},{20,28},{24,16},{28,20},{1,9},{5... | collective-permute-start | bytes 786440 | tf_op jit(solution)/shard_map/ppermute | solution.py:48
  35.7 8.3 %collective-permute-start = (bf16[128,1024]{1,0:T(8,128)(2,1)S(1)}, bf16[128,1024]{1,0:T(8,128)(2,1)S(1)}, u32[]{:S(2)}, u32[]{:S(2)}) collective-permute-start(bf16[128,1024]{1,0:T(8,128)(2,1)S(1)} %get-tuple-element.9), channel_id=1, source_target_pairs={{0,16},{4,20},{8,24},{12,28},{16,0},{20,4},{24,8},{28,12},{1,17},{... | collective-permute-start | bytes 786440 | tf_op jit(solution)/shard_map/ppermute | solution.py:48
  36.3 3.1 %copy-start.3 = (bf16[512,1024]{1,0:T(8,128)(2,1)}, bf16[512,1024]{1,0:T(8,128)(2,1)S(1)}, u32[]{:S(2)}) copy-start(bf16[512,1024]{1,0:T(8,128)(2,1)S(1)} %constant_dynamic-update-slice_fusion) | copy-start | bytes 3145732
  37.1 6.9 %collective-permute-start.7 = (bf16[512,512]{0,1:T(8,128)(2,1)S(1)}, bf16[512,512]{0,1:T(8,128)(2,1)S(1)}, u32[]{:S(2)}, u32[]{:S(2)}) collective-permute-start(bf16[512,512]{0,1:T(8,128)(2,1)S(1)} %convolution_convert_fusion.3), channel_id=1, source_target_pairs={{0,4},{4,0},{8,12},{12,8},{16,20},{20,16},{24,28},{28,24},{1,5},{5... | collective-permute-start | bytes 1572872 | tf_op jit(solution)/shard_map/ppermute | solution.py:48
  39.4 5.4 %copy-start.2 = (bf16[1024,1024]{1,0:T(8,128)(2,1)}, bf16[1024,1024]{1,0:T(8,128)(2,1)S(1)}, u32[]{:S(2)}) copy-start(bf16[1024,1024]{1,0:T(8,128)(2,1)S(1)} %constant_dynamic-update-slice_fusion.4) | copy-start | bytes 6291460
  41.7 12.2 %collective-permute-start.13 = (bf16[512,1024]{0,1:T(8,128)(2,1)}, bf16[512,1024]{0,1:T(8,128)(2,1)}, u32[]{:S(2)}, u32[]{:S(2)}) collective-permute-start(bf16[512,1024]{0,1:T(8,128)(2,1)} %convolution_convert_fusion), channel_id=1, source_target_pairs={{0,4},{4,0},{8,12},{12,8},{16,20},{20,16},{24,28},{28,24},{1,5},{5... | collective-permute-start | bytes 3145736 | tf_op jit(solution)/shard_map/ppermute | solution.py:48
  41.7 3.5 %copy-start.6 = (bf16[128,1024]{1,0:T(8,128)(2,1)}, bf16[128,1024]{1,0:T(8,128)(2,1)S(1)}, u32[]{:S(2)}) copy-start(bf16[128,1024]{1,0:T(8,128)(2,1)S(1)} %collective-permute-done.2) | copy-start | bytes 786436
  42.7 2.1 %copy-start.8 = (bf16[128,1024]{1,0:T(8,128)(2,1)}, bf16[128,1024]{1,0:T(8,128)(2,1)S(1)}, u32[]{:S(2)}) copy-start(bf16[128,1024]{1,0:T(8,128)(2,1)S(1)} %collective-permute-done.1) | copy-start | bytes 786436
  44.0 0.8 copy-start.10
  44.9 7.3 %collective-permute-start.10 = (bf16[128,512]{0,1:T(8,128)(2,1)S(1)}, bf16[128,512]{0,1:T(8,128)(2,1)S(1)}, u32[]{:S(2)}, u32[]{:S(2)}) collective-permute-start(bf16[128,512]{0,1:T(8,128)(2,1)S(1)} %get-tuple-element.26), channel_id=1, source_target_pairs={{0,24},{4,28},{8,16},{12,20},{16,8},{20,12},{24,0},{28,4},{1,25},{... | collective-permute-start | bytes 393224 | tf_op jit(solution)/shard_map/ppermute | solution.py:48
  45.3 8.4 %collective-permute-start.9 = (bf16[128,512]{0,1:T(8,128)(2,1)S(1)}, bf16[128,512]{0,1:T(8,128)(2,1)S(1)}, u32[]{:S(2)}, u32[]{:S(2)}) collective-permute-start(bf16[128,512]{0,1:T(8,128)(2,1)S(1)} %get-tuple-element.27), channel_id=1, source_target_pairs={{0,8},{4,12},{8,0},{12,4},{16,24},{20,28},{24,16},{28,20},{1,9},{5... | collective-permute-start | bytes 393224 | tf_op jit(solution)/shard_map/ppermute | solution.py:48
  47.1 6.6 %collective-permute-start.8 = (bf16[128,512]{0,1:T(8,128)(2,1)S(1)}, bf16[128,512]{0,1:T(8,128)(2,1)S(1)}, u32[]{:S(2)}, u32[]{:S(2)}) collective-permute-start(bf16[128,512]{0,1:T(8,128)(2,1)S(1)} %get-tuple-element.25), channel_id=1, source_target_pairs={{0,16},{4,20},{8,24},{12,28},{16,0},{20,4},{24,8},{28,12},{1,17},{... | collective-permute-start | bytes 393224 | tf_op jit(solution)/shard_map/ppermute | solution.py:48
  48.6 12.4 %collective-permute-start.17 = (bf16[1024,512]{1,0:T(8,128)(2,1)}, bf16[1024,512]{1,0:T(8,128)(2,1)S(1)}, u32[]{:S(2)}, u32[]{:S(2)}) collective-permute-start(bf16[1024,512]{1,0:T(8,128)(2,1)} %collective-permute-done.11), channel_id=1, source_target_pairs={{1,2},{2,3},{5,6},{6,7},{9,10},{10,11},{13,14},{14,15},{17,18},{18... | collective-permute-start | bytes 3145736 | tf_op jit(solution)/shard_map/ppermute | solution.py:51
  52.2 25.0 %collective-permute-start.18 = (bf16[1024,512]{1,0:T(8,128)(2,1)S(1)}, bf16[1024,512]{1,0:T(8,128)(2,1)S(1)}, u32[]{:S(2)}, u32[]{:S(2)}) collective-permute-start(bf16[1024,512]{1,0:T(8,128)(2,1)S(1)} %collective-permute-done.12), channel_id=1, source_target_pairs={{1,0},{2,1},{5,4},{6,5},{9,8},{10,9},{13,12},{14,13},{17,16},{18,1... | collective-permute-start | bytes 3145736 | tf_op jit(solution)/shard_map/ppermute | solution.py:51
  53.9 24.8 %copy-start.4 = (bf16[512,1024]{1,0:T(8,128)(2,1)S(1)}, bf16[512,1024]{1,0:T(8,128)(2,1)}, u32[]{:S(2)}) copy-start(bf16[512,1024]{1,0:T(8,128)(2,1)} %copy-done.3) | copy-start | bytes 3145732
  57.5 21.9 %collective-permute-start.16 = (bf16[128,1024]{0,1:T(8,128)(2,1)S(1)}, bf16[128,1024]{0,1:T(8,128)(2,1)S(1)}, u32[]{:S(2)}, u32[]{:S(2)}) collective-permute-start(bf16[128,1024]{0,1:T(8,128)(2,1)S(1)} %get-tuple-element.15), channel_id=1, source_target_pairs={{0,24},{4,28},{8,16},{12,20},{16,8},{20,12},{24,0},{28,4},{1,25},{... | collective-permute-start | bytes 786440 | tf_op jit(solution)/shard_map/ppermute | solution.py:48
  58.6 20.9 %collective-permute-start.15 = (bf16[128,1024]{0,1:T(8,128)(2,1)S(1)}, bf16[128,1024]{0,1:T(8,128)(2,1)S(1)}, u32[]{:S(2)}, u32[]{:S(2)}) collective-permute-start(bf16[128,1024]{0,1:T(8,128)(2,1)S(1)} %get-tuple-element.16), channel_id=1, source_target_pairs={{0,8},{4,12},{8,0},{12,4},{16,24},{20,28},{24,16},{28,20},{1,9},{5... | collective-permute-start | bytes 786440 | tf_op jit(solution)/shard_map/ppermute | solution.py:48
  59.6 19.9 %collective-permute-start.14 = (bf16[128,1024]{0,1:T(8,128)(2,1)S(1)}, bf16[128,1024]{0,1:T(8,128)(2,1)S(1)}, u32[]{:S(2)}, u32[]{:S(2)}) collective-permute-start(bf16[128,1024]{0,1:T(8,128)(2,1)S(1)} %get-tuple-element.14), channel_id=1, source_target_pairs={{0,16},{4,20},{8,24},{12,28},{16,0},{20,4},{24,8},{28,12},{1,17},{... | collective-permute-start | bytes 786440 | tf_op jit(solution)/shard_map/ppermute | solution.py:48
  61.1 18.7 %collective-permute-start.23 = (bf16[1024,512]{1,0:T(8,128)(2,1)S(1)}, bf16[1024,512]{1,0:T(8,128)(2,1)S(1)}, u32[]{:S(2)}, u32[]{:S(2)}) collective-permute-start(bf16[1024,512]{1,0:T(8,128)(2,1)S(1)} %collective-permute-done.17), channel_id=1, source_target_pairs={{2,3},{6,7},{10,11},{14,15},{18,19},{22,23},{26,27},{30,31}} | collective-permute-start | bytes 3145736 | tf_op jit(solution)/shard_map/ppermute | solution.py:51
  77.2 23.7 %collective-permute-start.24 = (bf16[1024,512]{1,0:T(8,128)(2,1)S(1)}, bf16[1024,512]{1,0:T(8,128)(2,1)S(1)}, u32[]{:S(2)}, u32[]{:S(2)}) collective-permute-start(bf16[1024,512]{1,0:T(8,128)(2,1)S(1)} %collective-permute-done.18), channel_id=1, source_target_pairs={{1,0},{5,4},{9,8},{13,12},{17,16},{21,20},{25,24},{29,28}} | collective-permute-start | bytes 3145736 | tf_op jit(solution)/shard_map/ppermute | solution.py:51
  79.4 22.3 %collective-permute-start.19 = (bf16[512,512]{0,1:T(8,128)(2,1)S(1)}, bf16[512,512]{0,1:T(8,128)(2,1)S(1)}, u32[]{:S(2)}, u32[]{:S(2)}) collective-permute-start(bf16[512,512]{0,1:T(8,128)(2,1)S(1)} %convolution_convert_fusion.2), channel_id=1, source_target_pairs={{0,4},{4,0},{8,12},{12,8},{16,20},{20,16},{24,28},{28,24},{1,5},{5... | collective-permute-start | bytes 1572872 | tf_op jit(solution)/shard_map/ppermute | solution.py:48
  79.7 22.0 %copy-start.7 = (bf16[128,1024]{1,0:T(8,128)(2,1)S(1)}, bf16[128,1024]{1,0:T(8,128)(2,1)}, u32[]{:S(2)}) copy-start(bf16[128,1024]{1,0:T(8,128)(2,1)} %copy-done.6) | copy-start | bytes 786436
  79.7 22.0 %copy-start.9 = (bf16[128,1024]{1,0:T(8,128)(2,1)S(1)}, bf16[128,1024]{1,0:T(8,128)(2,1)}, u32[]{:S(2)}) copy-start(bf16[128,1024]{1,0:T(8,128)(2,1)} %copy-done.8) | copy-start | bytes 786436
  79.8 22.0 %copy-start.11 = (bf16[128,1024]{1,0:T(8,128)(2,1)S(1)}, bf16[128,1024]{1,0:T(8,128)(2,1)}, u32[]{:S(2)}) copy-start(bf16[128,1024]{1,0:T(8,128)(2,1)} %copy-done.10) | copy-start | bytes 786436
  101.7 4.7 %collective-permute-start.25 = (bf16[512,512]{0,1:T(8,128)(2,1)S(1)}, bf16[512,512]{0,1:T(8,128)(2,1)S(1)}, u32[]{:S(2)}, u32[]{:S(2)}) collective-permute-start(bf16[512,512]{0,1:T(8,128)(2,1)S(1)} %convolution_convert_fusion.1), channel_id=1, source_target_pairs={{0,4},{4,0},{8,12},{12,8},{16,20},{20,16},{24,28},{28,24},{1,5},{5... | collective-permute-start | bytes 1572872 | tf_op jit(solution)/shard_map/ppermute | solution.py:48
  102.7 7.7 %collective-permute-start.22 = (bf16[128,512]{0,1:T(8,128)(2,1)S(1)}, bf16[128,512]{0,1:T(8,128)(2,1)S(1)}, u32[]{:S(2)}, u32[]{:S(2)}) collective-permute-start(bf16[128,512]{0,1:T(8,128)(2,1)S(1)} %get-tuple-element.23), channel_id=1, source_target_pairs={{0,24},{4,28},{8,16},{12,20},{16,8},{20,12},{24,0},{28,4},{1,25},{... | collective-permute-start | bytes 393224 | tf_op jit(solution)/shard_map/ppermute | solution.py:48
  105.7 7.9 %collective-permute-start.21 = (bf16[128,512]{0,1:T(8,128)(2,1)S(1)}, bf16[128,512]{0,1:T(8,128)(2,1)S(1)}, u32[]{:S(2)}, u32[]{:S(2)}) collective-permute-start(bf16[128,512]{0,1:T(8,128)(2,1)S(1)} %get-tuple-element.24), channel_id=1, source_target_pairs={{0,8},{4,12},{8,0},{12,4},{16,24},{20,28},{24,16},{28,20},{1,9},{5... | collective-permute-start | bytes 393224 | tf_op jit(solution)/shard_map/ppermute | solution.py:48
  105.9 7.7 %collective-permute-start.20 = (bf16[128,512]{0,1:T(8,128)(2,1)S(1)}, bf16[128,512]{0,1:T(8,128)(2,1)S(1)}, u32[]{:S(2)}, u32[]{:S(2)}) collective-permute-start(bf16[128,512]{0,1:T(8,128)(2,1)S(1)} %get-tuple-element.22), channel_id=1, source_target_pairs={{0,16},{4,20},{8,24},{12,28},{16,0},{20,4},{24,8},{28,12},{1,17},{... | collective-permute-start | bytes 393224 | tf_op jit(solution)/shard_map/ppermute | solution.py:48
  107.2 9.2 %collective-permute-start.28 = (bf16[128,512]{0,1:T(8,128)(2,1)S(1)}, bf16[128,512]{0,1:T(8,128)(2,1)S(1)}, u32[]{:S(2)}, u32[]{:S(2)}) collective-permute-start(bf16[128,512]{0,1:T(8,128)(2,1)S(1)} %get-tuple-element.20), channel_id=1, source_target_pairs={{0,24},{4,28},{8,16},{12,20},{16,8},{20,12},{24,0},{28,4},{1,25},{... | collective-permute-start | bytes 393224 | tf_op jit(solution)/shard_map/ppermute | solution.py:48
  110.1 8.1 %collective-permute-start.27 = (bf16[128,512]{0,1:T(8,128)(2,1)S(1)}, bf16[128,512]{0,1:T(8,128)(2,1)S(1)}, u32[]{:S(2)}, u32[]{:S(2)}) collective-permute-start(bf16[128,512]{0,1:T(8,128)(2,1)S(1)} %get-tuple-element.21), channel_id=1, source_target_pairs={{0,8},{4,12},{8,0},{12,4},{16,24},{20,28},{24,16},{28,20},{1,9},{5... | collective-permute-start | bytes 393224 | tf_op jit(solution)/shard_map/ppermute | solution.py:48
  110.4 7.9 %collective-permute-start.26 = (bf16[128,512]{0,1:T(8,128)(2,1)S(1)}, bf16[128,512]{0,1:T(8,128)(2,1)S(1)}, u32[]{:S(2)}, u32[]{:S(2)}) collective-permute-start(bf16[128,512]{0,1:T(8,128)(2,1)S(1)} %get-tuple-element.19), channel_id=1, source_target_pairs={{0,16},{4,20},{8,24},{12,28},{16,0},{20,4},{24,8},{28,12},{1,17},{... | collective-permute-start | bytes 393224 | tf_op jit(solution)/shard_map/ppermute | solution.py:48

commit v2 on v0

v2 whole, which is shorter than its diff:
```python
import functools

import jax
import jax.numpy as jnp
from jax import lax
from jax.experimental import pallas as pl
from jax.experimental.pallas import tpu as pltpu
from jax.sharding import PartitionSpec as P

HEAD = 128


rope_base = 500000.0


def rotation(positions):
    half_head = HEAD // 2
    frequency = rope_base ** (-2.0 * jnp.arange(half_head, dtype=jnp.float32) / HEAD)
    angles = positions.astype(jnp.float32)[:, None] * frequency[None, :]
    cosine = jnp.cos(angles)
    sine = jnp.sin(angles)
    return (
        jnp.concatenate([cosine, cosine], axis=1),
        jnp.concatenate([-sine, sine], axis=1),
    )


def params():
    return pltpu.CompilerParams(vmem_limit_bytes=24 * 1024 * 1024)


def norm_kernel(tokens_ref, gain_ref, out_ref, *, row_count, pair_count, part):
    widened = tokens_ref[...].astype(jnp.float32)
    mean = jnp.mean(widened * widened, axis=1, keepdims=True)
    normed = (widened * lax.rsqrt(mean + 1e-05) * gain_ref[...]).astype(jnp.bfloat16)
    for r in range(row_count):
        for d in range(pair_count):
            at = (r * pair_count + d) * part
            out_ref[d * row_count + r] = normed[:, at : at + part]


def normalise(tokens, norm_gain, row_count, pair_count, part):
    rows, features = tokens.shape
    step = 32
    count = row_count * pair_count
    return pl.pallas_call(
        functools.partial(
            norm_kernel, row_count=row_count, pair_count=pair_count, part=part
        ),
        grid=(rows // step,),
        in_specs=[
            pl.BlockSpec((step, features), lambda i: (i, 0)),
            pl.BlockSpec((1, features), lambda i: (0, 0)),
        ],
        out_specs=pl.BlockSpec((count, step, part), lambda i: (0, i, 0)),
        out_shape=jax.ShapeDtypeStruct((count, rows, part), jnp.bfloat16),
        compiler_params=params(),
        name="norm",
    )(tokens, norm_gain[None, :])


def split_kernel(place_ref, near_ref, far_ref, near_out, far_out):
    near_out[...] = near_ref[...]
    far_out[...] = far_ref[...]


def split(place, tile, pair_count, row_count):
    rows, part = tile.shape[1:]
    chips = row_count // 2 * pair_count

    def index(odd):
        def at(k, place):
            pair = place[0] ^ (k % pair_count)
            row = place[1] ^ ((k // pair_count) * 2 + odd)
            return (pair * row_count + row, 0, 0)

        return at

    block = (1, rows, part)
    out = pl.BlockSpec(block, lambda k, place: (k, 0, 0))
    near, far = pl.pallas_call(
        split_kernel,
        grid_spec=pltpu.PrefetchScalarGridSpec(
            num_scalar_prefetch=1,
            grid=(chips,),
            in_specs=[pl.BlockSpec(block, index(0)), pl.BlockSpec(block, index(1))],
            out_specs=[out, out],
        ),
        out_shape=[jax.ShapeDtypeStruct((chips, rows, part), jnp.bfloat16)] * 2,
        compiler_params=params(),
        name="split",
    )(place, tile, tile)
    return near.reshape(chips * rows, part), far.reshape(chips * rows, part)


def sum_kernel(place_ref, *refs, terms, kinds, width, outs):
    cosine_ref, sine_ref = refs[terms : terms + 2]
    out_refs = refs[-outs:]
    total = refs[0][0].astype(jnp.float32)
    for ref in refs[1:terms]:
        total = total + ref[...].astype(jnp.float32)
    for i, kind in enumerate(kinds):
        block = total[:, i * width : (i + 1) * width]
        out_ref = out_refs[i]
        if kind == "key":
            for h in range(width // HEAD):
                head = block[:, h * HEAD : (h + 1) * HEAD]
                turned = head * cosine_ref[...] + pltpu.roll(
                    head, HEAD // 2, 1
                ) * sine_ref[...]
                out_ref[:, h * HEAD : (h + 1) * HEAD] = turned.astype(jnp.bfloat16)
        else:
            out_ref[...] = block.astype(jnp.bfloat16)


def finish(place, both, others, tables, held, slots, kinds, width, columns):
    rows = both.shape[1]
    n = len(kinds) * width
    first_slot = slots[0]
    arrays = [both, *others, *tables]
    specs = [pl.BlockSpec((1, rows, n), lambda k, place: (0, 0, k))]
    specs += [pl.BlockSpec((rows, n), lambda k, place: (0, k)) for o in others]
    specs += [pl.BlockSpec((rows, HEAD), lambda k, place: (0, 0)) for t in tables]
    aliases = {}
    for i, h in enumerate(held):
        aliases[1 + len(arrays)] = i
        arrays.append(h)
        specs.append(pl.BlockSpec(memory_space=pl.ANY))
    out_spec = pl.BlockSpec(
        (rows, width), lambda k, place: (0, place[2] ^ (k + first_slot))
    )
    return pl.pallas_call(
        functools.partial(
            sum_kernel, terms=1 + len(others), kinds=kinds, width=width, outs=len(kinds)
        ),
        grid_spec=pltpu.PrefetchScalarGridSpec(
            num_scalar_prefetch=1,
            grid=(len(slots),),
            in_specs=specs,
            out_specs=[out_spec] * len(kinds),
        ),
        out_shape=[jax.ShapeDtypeStruct((rows, columns), jnp.bfloat16)] * len(kinds),
        input_output_aliases=aliases,
        compiler_params=params(),
        name="finish",
    )(place, *arrays)


def body(tokens, norm_gain, w_key, w_value):
    dp_count = lax.axis_size("dp")
    row_count = lax.axis_size("row")
    col_count = lax.axis_size("col")
    dp_index = lax.axis_index("dp")
    row_index = lax.axis_index("row")
    col_index = lax.axis_index("col")
    own_rows = tokens.shape[0]
    block, width = w_key.shape
    columns = width * col_count
    pair_count = 2 if dp_count % 2 == 0 else 1
    pair_index = dp_index % pair_count
    part = block // pair_count
    inner = ((col_index + 1) % 4) // 2
    place = jnp.stack([pair_index, row_index, col_index, inner]).astype(jnp.int32)

    def swap(array, row_bits, pair_bits):
        pairs = []
        for d in range(dp_count):
            for r in range(row_count):
                target = (d ^ pair_bits) * row_count + (r ^ row_bits)
                pairs.append((d * row_count + r, target))
        return lax.ppermute(array, ("dp", "row"), pairs)

    def exchange(array, bits, places=(0, 1, 2, 3)):
        return lax.ppermute(
            array, "col", [(i, i ^ bits) for i in range(col_count) if i % 4 in places]
        )

    positions = (row_index * col_count + col_index) * own_rows + jnp.arange(
        own_rows, dtype=jnp.int32
    )
    tables = rotation(positions)

    always = col_index < col_count

    def stage(work, *args):
        shapes = jax.eval_shape(work, *args)

        def skip(*args):
            return jax.tree.map(lambda s: jnp.zeros(s.shape, s.dtype), shapes)

        return lax.cond(always, work, skip, *args)

    start = pair_index * part
    own = jnp.concatenate(
        [lax.dynamic_slice_in_dim(w, start, part, 0) for w in (w_key, w_value)], axis=1
    )
    slot2 = exchange(own, 2)
    slot1 = exchange(own, 1)
    chips = [(r, d) for r in range(0, row_count, 2) for d in range(pair_count)]
    (tokens, own) = lax.optimization_barrier((tokens, own))
    def spread(tokens):
        parts = normalise(tokens, norm_gain, row_count, pair_count, part)
        groups = [
            [(g * pair_count + d) * row_count + r for d in range(pair_count) for r in range(row_count)]
            for g in range(dp_count // pair_count)
        ]
        return lax.all_to_all(
            parts,
            ("dp", "row"),
            split_axis=0,
            concat_axis=0,
            tiled=True,
            axis_index_groups=groups if len(groups) > 1 else None,
        )

    tile = stage(spread, tokens)

    def first(near, far, weights):
        shape = (len(chips), own_rows, -1)
        far_part = jnp.dot(far, weights, preferred_element_type=jnp.float32)
        other = swap(far_part.astype(jnp.bfloat16).reshape(shape), 1, 0)
        near_part = jnp.dot(near, weights, preferred_element_type=jnp.float32)
        both = near_part.reshape(shape) + other.astype(jnp.float32)
        return both.astype(jnp.bfloat16)

    def first_of(near, far, inner_weights, outer_weights):
        def dot(rows):
            def product(rows, weights):
                return jnp.dot(rows, weights, preferred_element_type=jnp.float32).astype(jnp.bfloat16)

            return lax.cond(
                inner == 1,
                lambda r, i, o: product(r, i),
                lambda r, i, o: product(r, o),
                rows,
                inner_weights,
                outer_weights,
            ).reshape(len(chips), own_rows, -1)

        other = swap(dot(far), 1, 0)
        return dot(near), other

    def second(both):
        return [swap(both[k], *chips[k]) for k in range(1, len(chips))]

    def add(both, held, slots, kinds, others=None):
        others = second(both) if others is None else others
        return finish(place, both, others, tables, held, slots, kinds, width, columns)

    kinds = ("key", "value")
    (tile, own) = lax.optimization_barrier((tile, own))
    def own_work(tile, own):
        near, far = split(place, tile, pair_count, row_count)
        return near, far, first(near, far, own)

    near, far, both0 = stage(own_work, tile, own)
    (near, far, both0, own, slot1, slot2) = lax.optimization_barrier((near, far, both0, own, slot1, slot2))
    outer = exchange(slot2, 1, (1, 2))
    middle = exchange(own, 3, (1, 2))

    def middle_work(near, far, both0, slot1, slot2):
        both12 = first(near, far, jnp.concatenate([slot1, slot2], axis=1))
        both = jnp.concatenate([both0, both12], axis=2)
        return add(both, [], (0, 1, 2), kinds)

    held = stage(middle_work, near, far, both0, slot1, slot2)
    (held, outer, middle) = lax.optimization_barrier((held, outer, middle))
    third = lax.optimization_barrier(jnp.where(inner == 1, middle, outer))
    held = add(first(near, far, third), held, (3,), kinds)
    blocks = [own, slot1, slot2, third]
    while len(blocks) < col_count:
        blocks += [exchange(w, len(blocks)) for w in blocks]
    for k in range(4, col_count):
        held = add(first(near, far, blocks[k]), held, (k,), kinds)
    key_rows, value_rows = held
    return (key_rows, value_rows)


def solution(mesh):
    placed = (P(("dp", "row", "col"), None), P(), P("row", "col"), P("row", "col"))
    return jax.shard_map(
        body,
        mesh=mesh,
        in_specs=placed,
        out_specs=(P(("dp", "row", "col"), None), P(("dp", "row", "col"), None)),
        check_vma=False,
    )
```

time: 234 us -> 104 us (0.44)
  waiting for transfers between devices: 165 us -> 28.7 us
  starting transfers between devices: 0.16 us -> 15 us
  between operations: 13.8 us -> 0.78 us
  Pallas kernels: 0 us -> 9.13 us
  other arithmetic: 6.31 us -> 2.64 us
  local copies, waits for them, and re-layouts: 6.78 us -> 4 us
    all_gather x2 -> x0, waiting for transfers between devices: 118 us -> none  [the longest x1 74 us: body(): lax.all_gather(w_value, 'col', axis=1, tiled=True)]
    reduce_scatter x2 -> x0, waiting for transfers between devices: 45.5 us -> none  [the longest x1 25.7 us: body(): lax.psum_scatter(value_part.astype(jnp.bfloat16), 'row', scatter_dimensio...]
    ppermute x0 -> x13, waiting for transfers between devices: none -> 28.7 us  [the longest x9 25.4 us: swap(): return lax.ppermute(array, ('dp', 'row'), pairs)]
    ppermute x0 -> x13, starting transfers between devices: none -> 15 us  [the longest x4 7.69 us: exchange(): lax.ppermute(array, 'col', [(i, i ^ bits) for i in range(col_count) if i...]
    pallas_call x0 -> x4, Pallas kernels: none -> 9.13 us  [the longest x2 3.46 us: finish(): pl.pallas_call(functools.partial(sum_kernel, terms=1 + len(others), kinds...]
    unnamed x7 -> x2, local copies, waits for them, and re-layouts: 4.08 us -> 0.01 us
    convert_element_type x2 -> x3, other arithmetic: 3.49 us -> 0.54 us  [the longest x2 0.53 us: first(): return both.astype(jnp.bfloat16)]
    all_to_all x1 -> x0, local copies, waits for them, and re-layouts: 2.7 us -> none  [body(): lax.all_to_all(normed, 'row', split_axis=1, concat_axis=0, tiled=True)]
  transfers between devices with their start and end apart: 4 -> 13, of which waited for: 4 -> 8; matrix products, arithmetic and copies ran while one was open for 11% -> 14% of each run, Pallas kernels for 0% -> 8%
where the time goes in v2:
time: 104 us; the launch traced here: 103 us
  blocking collectives  29.5 us (28%)
  waiting for transfers between devices  28.7 us (28%)
  starting transfers between devices  15 us (14%)
  matrix products  12.8 us (12%)
  Pallas kernels  9.13 us (9%)
  local copies, waits for them, and re-layouts  4 us (4%)
  other arithmetic  2.64 us (3%)
    all_to_all x1, blocking collectives, spread(): lax.all_to_all(parts, ('dp', 'row'), split_axis=0, concat_axis=0, tiled=T...  29.5 us
    ppermute x9, waiting for transfers between devices, swap(): return lax.ppermute(array, ('dp', 'row'), pairs)  25.4 us
    ppermute x4, starting transfers between devices, exchange(): lax.ppermute(array, 'col', [(i, i ^ bits) for i in range(col_count) if i...  7.69 us
    ppermute x9, starting transfers between devices, swap(): return lax.ppermute(array, ('dp', 'row'), pairs)  7.33 us
    dot_general x3, matrix products, first(): near_part = jnp.dot(near, weights, preferred_element_type=jnp.float32)  6.38 us
    dot_general x3, matrix products, first(): far_part = jnp.dot(far, weights, preferred_element_type=jnp.float32)  6.37 us
    pallas_call x2, Pallas kernels, finish(): pl.pallas_call(functools.partial(sum_kernel, terms=1 + len(others), kinds...  3.46 us
    ppermute x4, waiting for transfers between devices, exchange(): lax.ppermute(array, 'col', [(i, i ^ bits) for i in range(col_count) if i...  3.33 us
  transfers between devices with their start and end apart: 13, of which 8 were waited for; matrix products, arithmetic and copies ran while one was open for 14% of the time, Pallas kernels for 8%

profile of v2, /device:TPU:0, one launch (start us, length us, event | category | flops | bytes accessed | tf_op | source)
XLA Modules:
  0.0 102.7 jit_solution(12490307333312769967)
XLA Ops:
  0.7 1.3 %constant_dynamic-slice_fusion = (bf16[1024,256]{1,0:T(8,128)(2,1)S(1)}, bf16[1024,256]{1,0:T(8,128)(2,1)S(1)}) fusion(bf16[2048,256]{1,0:T(8,128)(2,1)} %param.13, s32[]{:T(128)S(6)} %select_n.30, bf16[2048,256]{1,0:T(8,128)(2,1)} %param.12), kind=kLoop, calls=%fused_computation.36 | loop fusion | bytes 2097156 | tf_op jit(solution)/shard_map/dynamic_slice | solution.py:195
  1.9 0.1 pad_maximum_fusion.1
  2.0 4.1 %collective-permute-start.6 = (bf16[1024,512]{1,0:T(8,128)(2,1)S(1)}, bf16[1024,512]{1,0:T(8,128)(2,1)}, u32[]{:S(2)}, u32[]{:S(2)}) collective-permute-start(bf16[1024,512]{1,0:T(8,128)(2,1)S(1)} %pad_maximum_fusion.1), channel_id=1, source_target_pairs={{0,2},{1,3},{2,0},{3,1},{4,6},{5,7},{6,4},{7,5},{8,10},{9,11},{10,... | collective-permute-start | bytes 3145736 | tf_op jit(solution)/shard_map/ppermute | solution.py:174
  6.1 1.6 %collective-permute-start.5 = (bf16[1024,512]{1,0:T(8,128)(2,1)S(1)}, bf16[1024,512]{1,0:T(8,128)(2,1)}, u32[]{:S(2)}, u32[]{:S(2)}) collective-permute-start(bf16[1024,512]{1,0:T(8,128)(2,1)S(1)} %pad_maximum_fusion.1), channel_id=1, source_target_pairs={{0,1},{1,0},{2,3},{3,2},{4,5},{5,4},{6,7},{7,6},{8,9},{9,8},{10,11... | collective-permute-start | bytes 3145736 | tf_op jit(solution)/shard_map/ppermute | solution.py:174
  7.7 32.8 %conditional.3 = (bf16[8,128,1024]{2,1,0:T(8,128)(2,1)S(1)}) conditional(s32[]{:T(128)} %convert_element_type.42, () %tuple.33, (f32[8192]{0:T(1024)S(1)}, bf16[128,8192]{1,0:T(8,128)(2,1)}) %tuple.58), branch_computations={%region_0.1_spmd, %region_1.2_spmd} | conditional | bytes 4194312 | solution.py:191
  7.7 3.2 %norm.1 = bf16[8,128,1024]{2,1,0:T(8,128)(2,1)S(1)} custom-call(bf16[128,8192]{1,0:T(8,128)(2,1)} %get-tuple-element.17.tokens_ref, f32[1,8192]{1,0:T(1,128)S(1)} %bitcast.46), custom_call_target="tpu_custom_call" | custom-call | tf_op jit(solution)/shard_map/cond/branch_1_fun/norm/pallas_call | solution.py:46
  10.9 29.5 %all_to_all.4 = bf16[8,128,1024]{2,1,0:T(8,128)(2,1)S(1)} all-to-all(bf16[8,128,1024]{2,1,0:T(8,128)(2,1)S(1)} %norm.1), channel_id=1, replica_groups=mesh['dp'=2,'row'=4,'col'=4] {'dp','row'}, dimensions={0} | all-to-all | bytes 4194304 | tf_op jit(solution)/shard_map/cond/branch_1_fun/all_to_all | solution.py:207
  40.5 0.1 pad_add_fusion.place_ref
  40.5 8.3 %conditional.4 = (bf16[512,1024]{1,0:T(8,128)(2,1)}, bf16[512,1024]{1,0:T(8,128)(2,1)}, bf16[4,128,512]{2,1,0:T(8,128)(2,1)S(1)}) conditional(s32[]{:T(128)} %convert_element_type.42, () %tuple.32, (s32[4]{0:T(128)S(1)}, bf16[8,128,1024]{2,1,0:T(8,128)(2,1)S(1)}, bf16[1024,512]{1,0:T(8,128)(2,1)S(1)}) %tuple.37), branch_computations={%region_2.3_spmd, %region_3.4_spmd} | conditional | flops 1074790400 | bytes 7864384 | solution.py:191
  40.5 2.4 %split.1 = (bf16[4,128,1024]{2,1,0:T(8,128)(2,1)}, bf16[4,128,1024]{2,1,0:T(8,128)(2,1)}) custom-call(s32[4]{0:T(128)S(1)} %get-tuple-element.31.place_ref, bf16[8,128,1024]{2,1,0:T(8,128)(2,1)S(1)} %get-tuple-element.32.near_ref.far_ref, bf16[8,128,1024]{2,1,0:T(8,128)(2,1)S(1)} %get-tuple-element.32.near_ref.far_ref), custom_call_target="tpu_custom_call" | custom-call | tf_op jit(solution)/shard_map/cond/branch_1_fun/split/pallas_call | solution.py:81
  43.0 1.9 %convolution_convert_fusion = bf16[512,512]{1,0:T(8,128)(2,1)S(1)} fusion(bf16[512,1024]{1,0:T(8,128)(2,1)} %bitcast.2, bf16[1024,512]{1,0:T(8,128)(2,1)S(1)} %get-tuple-element.35), kind=kOutput, calls=%fused_computation | convolution fusion | flops 537133056 | bytes 2621440 | tf_op jit(solution)/shard_map/cond/branch_1_fun/dot_general | solution.py:220
  44.9 0.1 collective-permute-start
  45.0 1.9 %collective-permute-done = bf16[4,128,512]{2,1,0:T(8,128)(2,1)S(1)} collective-permute-done((bf16[4,128,512]{2,1,0:T(8,128)(2,1)S(1)}, bf16[4,128,512]{2,1,0:T(8,128)(2,1)S(1)}, u32[]{:S(2)}, u32[]{:S(2)}) %collective-permute-start) | collective-permute-done | bytes 524320 | tf_op jit(solution)/shard_map/cond/branch_1_fun/ppermute | solution.py:171
  46.9 1.9 %add_convert_fusion = bf16[4,128,512]{2,1,0:T(8,128)(2,1)S(1)} fusion(bf16[4,128,512]{2,1,0:T(8,128)(2,1)S(1)} %collective-permute-done, bf16[4,128,1024]{2,1,0:T(8,128)(2,1)} %get-tuple-element.33, bf16[1024,512]{1,0:T(8,128)(2,1)S(1)} %get-tuple-element.35), kind=kOutput, calls=%fused_computation.3 | convolution fusion | flops 537657344 | bytes 3145728 | tf_op jit(solution)/shard_map/cond/branch_1_fun/dot_general | solution.py:222
  48.8 3.1 %collective-permute-done.6 = bf16[1024,512]{1,0:T(8,128)(2,1)} collective-permute-done((bf16[1024,512]{1,0:T(8,128)(2,1)S(1)}, bf16[1024,512]{1,0:T(8,128)(2,1)}, u32[]{:S(2)}, u32[]{:S(2)}) %collective-permute-start.6) | collective-permute-done | bytes 1048608 | tf_op jit(solution)/shard_map/ppermute | solution.py:174
  52.0 0.2 collective-permute-done.5
  52.2 0.7 collective-permute-start.8
  52.9 1.3 %collective-permute-start.7 = (bf16[1024,512]{1,0:T(8,128)(2,1)}, bf16[1024,512]{1,0:T(8,128)(2,1)}, u32[]{:S(2)}, u32[]{:S(2)}) collective-permute-start(bf16[1024,512]{1,0:T(8,128)(2,1)} %collective-permute-done.6), channel_id=1, source_target_pairs={{1,0},{2,3},{5,4},{6,7},{9,8},{10,11},{13,12},{14,15},{17,16},{18,... | collective-permute-start | bytes 3145736 | tf_op jit(solution)/shard_map/ppermute | solution.py:174
  54.2 0.3 fusion.8
  54.5 0.1 pad_maximum_fusion.2
  54.6 31.5 %conditional.5 = ((bf16[128,1024]{1,0:T(8,128)(2,1)}, bf16[128,1024]{1,0:T(8,128)(2,1)})) conditional(s32[]{:T(128)} %convert_element_type.42, () %tuple.39, (bf16[1024,512]{1,0:T(8,128)(2,1)}, bf16[1024,512]{1,0:T(8,128)(2,1)}, bf16[512,1024]{1,0:T(8,128)(2,1)}, bf16[512,1024]{1,0:T(8,128)(2,1)}, bf16[4,128,512]{2,1,0:T(8,128)(2,1)S(1)}, ...), branch_computations={%region_4.5_spmd, %region_5.6_spmd} | conditional | flops 2155085824 | bytes 32637096 | solution.py:191
  54.7 1.3 %constant_dynamic-update-slice_fusion.1 = bf16[1024,1024]{1,0:T(8,128)(2,1)S(1)} fusion(bf16[1024,512]{1,0:T(8,128)(2,1)} %get-tuple-element.38), kind=kLoop, calls=%fused_computation.20 | loop fusion | bytes 2097152 | tf_op jit(solution)/shard_map/cond
  56.0 1.3 %constant_dynamic-update-slice_fusion = bf16[1024,1024]{1,0:T(8,128)(2,1)S(1)} fusion(bf16[1024,1024]{1,0:T(8,128)(2,1)S(1)} %constant_dynamic-update-slice_fusion.1, bf16[1024,512]{1,0:T(8,128)(2,1)} %get-tuple-element.39), kind=kLoop, calls=%fused_computation.19 | loop fusion | bytes 2097152 | tf_op jit(solution)/shard_map/cond/branch_1_fun/concatenate | solution.py:262
  57.4 2.5 %convolution_convert_fusion.1 = bf16[1024,512]{0,1:T(8,128)(2,1)S(1)} fusion(bf16[512,1024]{1,0:T(8,128)(2,1)} %get-tuple-element.41, bf16[1024,1024]{1,0:T(8,128)(2,1)S(1)} %constant_dynamic-update-slice_fusion), kind=kOutput, calls=%fused_computation.12 | convolution fusion | flops 1074266112 | bytes 4194304 | tf_op jit(solution)/shard_map/cond/branch_1_fun/dot_general | solution.py:220
  59.9 0.1 collective-permute-start.1
  60.0 2.5 %fusion.9 = f32[1024,512]{0,1:T(8,128)S(1)} fusion(bf16[512,1024]{1,0:T(8,128)(2,1)} %get-tuple-element.40, bf16[1024,1024]{1,0:T(8,128)(2,1)S(1)} %constant_dynamic-update-slice_fusion), kind=kOutput, calls=%fused_computation.38 | convolution fusion | flops 1073741824 | bytes 5242880 | tf_op jit(solution)/shard_map/cond/branch_1_fun/dot_general | solution.py:222
  62.5 0.1 collective-permute-done.1
  62.6 0.4 add_convert_fusion.1
  63.0 0.1 fusion.7
  63.1 2.6 %collective-permute-start.4 = (bf16[128,1536]{1,0:T(8,128)(2,1)S(1)}, bf16[128,1536]{1,0:T(8,128)(2,1)S(1)}, u32[]{:S(2)}, u32[]{:S(2)}) collective-permute-start(bf16[128,1536]{1,0:T(8,128)(2,1)S(1)} %get-tuple-element.86), channel_id=1, source_target_pairs={{0,24},{4,28},{8,16},{12,20},{16,8},{20,12},{24,0},{28,4},{1,25},{... | collective-permute-start | bytes 1179656 | tf_op jit(solution)/shard_map/cond/branch_1_fun/ppermute | solution.py:171
  65.6 0.5 collective-permute-start.2
  66.2 0.5 collective-permute-start.3
  66.6 0.1 pad_maximum_fusion.refs_0_
  66.7 9.3 %collective-permute-done.4.refs_3_ = bf16[128,1536]{1,0:T(8,128)(2,1)S(1)} collective-permute-done((bf16[128,1536]{1,0:T(8,128)(2,1)S(1)}, bf16[128,1536]{1,0:T(8,128)(2,1)S(1)}, u32[]{:S(2)}, u32[]{:S(2)}) %collective-permute-start.4) | collective-permute-done | bytes 393248 | tf_op jit(solution)/shard_map/cond/branch_1_fun/ppermute | solution.py:171
  76.0 8.0 %collective-permute-done.2.refs_1_ = bf16[128,1536]{1,0:T(8,128)(2,1)S(1)} collective-permute-done((bf16[128,1536]{1,0:T(8,128)(2,1)S(1)}, bf16[128,1536]{1,0:T(8,128)(2,1)S(1)}, u32[]{:S(2)}, u32[]{:S(2)}) %collective-permute-start.2) | collective-permute-done | bytes 393248 | tf_op jit(solution)/shard_map/cond/branch_1_fun/ppermute | solution.py:171
  84.0 2.2 %finish.2 = (bf16[128,1024]{1,0:T(8,128)(2,1)}, bf16[128,1024]{1,0:T(8,128)(2,1)}) custom-call(s32[4]{0:T(128)S(1)} %get-tuple-element.36.place_ref, bf16[4,128,1536]{2,1,0:T(8,128)(2,1)S(1)} %pad_maximum_fusion.refs_0_, bf16[128,1536]{1,0:T(8,128)(2,1)S(1)} %collective-permute-done.2.refs_1_, bf16[128,1536]{1,0:T(8,128)(2,1)S(1)} %collective-permute-done.3.refs_2_, ...), custom_call_target="tpu_custom_call" | custom-call | tf_op jit(solution)/shard_map/cond/branch_1_fun/finish/pallas_call | solution.py:132
  86.2 0.0 collective-permute-done.8
  86.2 1.3 %broadcast_select_fusion = bf16[1024,512]{1,0:T(8,128)(2,1)S(1)} fusion(bf16[1024,512]{1,0:T(8,128)(2,1)S(1)} %collective-permute-done.8, bf16[1024,512]{1,0:T(8,128)(2,1)} %collective-permute-done.7, pred[]{:T(512)S(6)} %eq.6), kind=kLoop, calls=%fused_computation.24 | loop fusion | flops 524288 | bytes 3145729 | tf_op jit(solution)/shard_map/jit(_where)/select_n | solution.py:268
  87.5 1.9 %convolution_convert_fusion.2 = bf16[512,512]{1,0:T(8,128)(2,1)S(1)} fusion(bf16[512,1024]{1,0:T(8,128)(2,1)} %get-tuple-element.75, bf16[1024,512]{1,0:T(8,128)(2,1)S(1)} %broadcast_select_fusion), kind=kOutput, calls=%fused_computation.21 | convolution fusion | flops 537133056 | bytes 2621440 | tf_op jit(solution)/shard_map/dot_general | solution.py:220
  89.5 0.1 collective-permute-start.9
  89.6 1.9 %fusion.10 = f32[512,512]{1,0:T(8,128)S(1)} fusion(bf16[512,1024]{1,0:T(8,128)(2,1)} %get-tuple-element.72, bf16[1024,512]{1,0:T(8,128)(2,1)S(1)} %broadcast_select_fusion), kind=kOutput, calls=%fused_computation.39 | convolution fusion | flops 536870912 | bytes 3145728 | tf_op jit(solution)/shard_map/dot_general | solution.py:222
  91.5 0.2 add_convert_fusion.2.refs_0_
  91.7 2.4 %collective-permute-start.12 = (bf16[128,512]{1,0:T(8,128)(2,1)S(1)}, bf16[128,512]{1,0:T(8,128)(2,1)S(1)}, u32[]{:S(2)}, u32[]{:S(2)}) collective-permute-start(bf16[128,512]{1,0:T(8,128)(2,1)S(1)} %get-tuple-element.89), channel_id=1, source_target_pairs={{0,24},{4,28},{8,16},{12,20},{16,8},{20,12},{24,0},{28,4},{1,25},{... | collective-permute-start | bytes 393224 | tf_op jit(solution)/shard_map/ppermute | solution.py:171
  94.1 0.6 collective-permute-start.11
  94.7 0.5 collective-permute-start.10
  95.3 3.7 %collective-permute-done.12.refs_3_ = bf16[128,512]{1,0:T(8,128)(2,1)S(1)} collective-permute-done((bf16[128,512]{1,0:T(8,128)(2,1)S(1)}, bf16[128,512]{1,0:T(8,128)(2,1)S(1)}, u32[]{:S(2)}, u32[]{:S(2)}) %collective-permute-start.12) | collective-permute-done | bytes 131104 | tf_op jit(solution)/shard_map/ppermute | solution.py:171
  99.0 2.4 %collective-permute-done.11.refs_2_ = bf16[128,512]{1,0:T(8,128)(2,1)S(1)} collective-permute-done((bf16[128,512]{1,0:T(8,128)(2,1)S(1)}, bf16[128,512]{1,0:T(8,128)(2,1)S(1)}, u32[]{:S(2)}, u32[]{:S(2)}) %collective-permute-start.11) | collective-permute-done | bytes 131104 | tf_op jit(solution)/shard_map/ppermute | solution.py:171
  101.4 1.3 %finish.3 = (bf16[128,1024]{1,0:T(8,128)(2,1)}, bf16[128,1024]{1,0:T(8,128)(2,1)}) custom-call(s32[4]{0:T(128)S(1)} %pad_add_fusion.place_ref, bf16[4,128,512]{2,1,0:T(8,128)(2,1)S(1)} %add_convert_fusion.2.refs_0_, bf16[128,512]{1,0:T(8,128)(2,1)S(1)} %collective-permute-done.10.refs_1_, ...), custom_call_target="tpu_custom_call", output_to_operand_aliasing={{0}: (7, {}), {1}: (8, {})} | custom-call | tf_op jit(solution)/shard_map/finish/pallas_call | solution.py:132
  (9 shorter events, 0.1 us)
Async XLA Ops:
  0.6 7.1 %copy-start = (f32[8192]{0:T(1024)S(1)}, f32[8192]{0:T(1024)}, u32[]{:S(2)}) copy-start(f32[8192]{0:T(1024)} %param.11) | copy-start | bytes 98308
  2.0 49.9 %collective-permute-start.6 = (bf16[1024,512]{1,0:T(8,128)(2,1)S(1)}, bf16[1024,512]{1,0:T(8,128)(2,1)}, u32[]{:S(2)}, u32[]{:S(2)}) collective-permute-start(bf16[1024,512]{1,0:T(8,128)(2,1)S(1)} %pad_maximum_fusion.1), channel_id=1, source_target_pairs={{0,2},{1,3},{2,0},{3,1},{4,6},{5,7},{6,4},{7,5},{8,10},{9,11},{10,... | collective-permute-start | bytes 3145736 | tf_op jit(solution)/shard_map/ppermute | solution.py:174
  6.1 46.0 %collective-permute-start.5 = (bf16[1024,512]{1,0:T(8,128)(2,1)S(1)}, bf16[1024,512]{1,0:T(8,128)(2,1)}, u32[]{:S(2)}, u32[]{:S(2)}) collective-permute-start(bf16[1024,512]{1,0:T(8,128)(2,1)S(1)} %pad_maximum_fusion.1), channel_id=1, source_target_pairs={{0,1},{1,0},{2,3},{3,2},{4,5},{5,4},{6,7},{7,6},{8,9},{9,8},{10,11... | collective-permute-start | bytes 3145736 | tf_op jit(solution)/shard_map/ppermute | solution.py:174
  44.9 2.0 %collective-permute-start = (bf16[4,128,512]{2,1,0:T(8,128)(2,1)S(1)}, bf16[4,128,512]{2,1,0:T(8,128)(2,1)S(1)}, u32[]{:S(2)}, u32[]{:S(2)}) collective-permute-start(bf16[4,128,512]{2,1,0:T(8,128)(2,1)S(1)} %bitcast.49), channel_id=1, source_target_pairs={{0,4},{4,0},{8,12},{12,8},{16,20},{20,16},{24,28},{28,24},{1,5},{5... | collective-permute-start | bytes 1572872 | tf_op jit(solution)/shard_map/cond/branch_1_fun/ppermute | solution.py:171
  52.2 34.0 %collective-permute-start.8 = (bf16[1024,512]{1,0:T(8,128)(2,1)S(1)}, bf16[1024,512]{1,0:T(8,128)(2,1)S(1)}, u32[]{:S(2)}, u32[]{:S(2)}) collective-permute-start(bf16[1024,512]{1,0:T(8,128)(2,1)S(1)} %pad_maximum_fusion.1), channel_id=1, source_target_pairs={{1,2},{2,1},{5,6},{6,5},{9,10},{10,9},{13,14},{14,13},{17,18},{18,... | collective-permute-start | bytes 3145736 | tf_op jit(solution)/shard_map/ppermute | solution.py:174
  52.9 33.3 %collective-permute-start.7 = (bf16[1024,512]{1,0:T(8,128)(2,1)}, bf16[1024,512]{1,0:T(8,128)(2,1)}, u32[]{:S(2)}, u32[]{:S(2)}) collective-permute-start(bf16[1024,512]{1,0:T(8,128)(2,1)} %collective-permute-done.6), channel_id=1, source_target_pairs={{1,0},{2,3},{5,4},{6,7},{9,8},{10,11},{13,12},{14,15},{17,16},{18,... | collective-permute-start | bytes 3145736 | tf_op jit(solution)/shard_map/ppermute | solution.py:174
  59.9 2.7 %collective-permute-start.1 = (bf16[4,128,1024]{2,1,0:T(8,128)(2,1)S(1)}, bf16[4,128,1024]{2,1,0:T(8,128)(2,1)S(1)}, u32[]{:S(2)}, u32[]{:S(2)}) collective-permute-start(bf16[4,128,1024]{2,1,0:T(8,128)(2,1)S(1)} %bitcast.47), channel_id=1, source_target_pairs={{0,4},{4,0},{8,12},{12,8},{16,20},{20,16},{24,28},{28,24},{1,5},{5... | collective-permute-start | bytes 3145736 | tf_op jit(solution)/shard_map/cond/branch_1_fun/ppermute | solution.py:171
  63.1 13.0 %collective-permute-start.4 = (bf16[128,1536]{1,0:T(8,128)(2,1)S(1)}, bf16[128,1536]{1,0:T(8,128)(2,1)S(1)}, u32[]{:S(2)}, u32[]{:S(2)}) collective-permute-start(bf16[128,1536]{1,0:T(8,128)(2,1)S(1)} %get-tuple-element.86), channel_id=1, source_target_pairs={{0,24},{4,28},{8,16},{12,20},{16,8},{20,12},{24,0},{28,4},{1,25},{... | collective-permute-start | bytes 1179656 | tf_op jit(solution)/shard_map/cond/branch_1_fun/ppermute | solution.py:171
  65.6 18.4 %collective-permute-start.2 = (bf16[128,1536]{1,0:T(8,128)(2,1)S(1)}, bf16[128,1536]{1,0:T(8,128)(2,1)S(1)}, u32[]{:S(2)}, u32[]{:S(2)}) collective-permute-start(bf16[128,1536]{1,0:T(8,128)(2,1)S(1)} %get-tuple-element.87), channel_id=1, source_target_pairs={{0,16},{4,20},{8,24},{12,28},{16,0},{20,4},{24,8},{28,12},{1,17},{... | collective-permute-start | bytes 1179656 | tf_op jit(solution)/shard_map/cond/branch_1_fun/ppermute | solution.py:171
  66.2 17.8 %collective-permute-start.3 = (bf16[128,1536]{1,0:T(8,128)(2,1)S(1)}, bf16[128,1536]{1,0:T(8,128)(2,1)S(1)}, u32[]{:S(2)}, u32[]{:S(2)}) collective-permute-start(bf16[128,1536]{1,0:T(8,128)(2,1)S(1)} %get-tuple-element.88), channel_id=1, source_target_pairs={{0,8},{4,12},{8,0},{12,4},{16,24},{20,28},{24,16},{28,20},{1,9},{5... | collective-permute-start | bytes 1179656 | tf_op jit(solution)/shard_map/cond/branch_1_fun/ppermute | solution.py:171
  89.5 2.0 %collective-permute-start.9 = (bf16[4,128,512]{2,1,0:T(8,128)(2,1)S(1)}, bf16[4,128,512]{2,1,0:T(8,128)(2,1)S(1)}, u32[]{:S(2)}, u32[]{:S(2)}) collective-permute-start(bf16[4,128,512]{2,1,0:T(8,128)(2,1)S(1)} %bitcast.48), channel_id=1, source_target_pairs={{0,4},{4,0},{8,12},{12,8},{16,20},{20,16},{24,28},{28,24},{1,5},{5... | collective-permute-start | bytes 1572872 | tf_op jit(solution)/shard_map/ppermute | solution.py:171
  91.7 7.3 %collective-permute-start.12 = (bf16[128,512]{1,0:T(8,128)(2,1)S(1)}, bf16[128,512]{1,0:T(8,128)(2,1)S(1)}, u32[]{:S(2)}, u32[]{:S(2)}) collective-permute-start(bf16[128,512]{1,0:T(8,128)(2,1)S(1)} %get-tuple-element.89), channel_id=1, source_target_pairs={{0,24},{4,28},{8,16},{12,20},{16,8},{20,12},{24,0},{28,4},{1,25},{... | collective-permute-start | bytes 393224 | tf_op jit(solution)/shard_map/ppermute | solution.py:171
  94.1 7.3 %collective-permute-start.11 = (bf16[128,512]{1,0:T(8,128)(2,1)S(1)}, bf16[128,512]{1,0:T(8,128)(2,1)S(1)}, u32[]{:S(2)}, u32[]{:S(2)}) collective-permute-start(bf16[128,512]{1,0:T(8,128)(2,1)S(1)} %get-tuple-element.90), channel_id=1, source_target_pairs={{0,8},{4,12},{8,0},{12,4},{16,24},{20,28},{24,16},{28,20},{1,9},{5... | collective-permute-start | bytes 393224 | tf_op jit(solution)/shard_map/ppermute | solution.py:171
  94.7 6.7 %collective-permute-start.10 = (bf16[128,512]{1,0:T(8,128)(2,1)S(1)}, bf16[128,512]{1,0:T(8,128)(2,1)S(1)}, u32[]{:S(2)}, u32[]{:S(2)}) collective-permute-start(bf16[128,512]{1,0:T(8,128)(2,1)S(1)} %get-tuple-element.91), channel_id=1, source_target_pairs={{0,16},{4,20},{8,24},{12,28},{16,0},{20,4},{24,8},{28,12},{1,17},{... | collective-permute-start | bytes 393224 | tf_op jit(solution)/shard_map/ppermute | solution.py:171

commit v3 on v2

--- a/solution.py
+++ b/solution.py
@@ -30,67 +30,91 @@
 
 
 def norm_kernel(tokens_ref, gain_ref, out_ref, *, row_count, pair_count, part):
-    widened = tokens_ref[...].astype(jnp.float32)
-    mean = jnp.mean(widened * widened, axis=1, keepdims=True)
-    normed = (widened * lax.rsqrt(mean + 1e-05) * gain_ref[...]).astype(jnp.bfloat16)
-    for r in range(row_count):
-        for d in range(pair_count):
-            at = (r * pair_count + d) * part
-            out_ref[d * row_count + r] = normed[:, at : at + part]
+    step = 32
+    blocks = [(d * row_count + r, r * pair_count + d) for r in range(row_count) for d in range(pair_count)]
+    count = len(blocks) * part
+
+    @pl.loop(0, tokens_ref.shape[0], step=step)
+    def _(at):
+        rows = pl.ds(pl.multiple_of(at, step), step)
+
+        def piece(k):
+            return tokens_ref[rows, k * part : (k + 1) * part].astype(jnp.float32)
+
+        squares = jnp.zeros((step, 128), jnp.float32)
+        for _, k in blocks:
+            square = piece(k) * piece(k)
+            for j in range(0, part, 128):
+                squares = squares + square[:, j : j + 128]
+        mean = jnp.sum(squares, axis=1, keepdims=True) / count
+        inverse_rms = lax.rsqrt(mean + 1e-05)
+        for place, k in blocks:
+            gain = gain_ref[:, k * part : (k + 1) * part]
+            out_ref[place, rows, :] = (piece(k) * inverse_rms * gain).astype(jnp.bfloat16)
 
 
 def normalise(tokens, norm_gain, row_count, pair_count, part):
-    rows, features = tokens.shape
-    step = 32
-    count = row_count * pair_count
+    rows = tokens.shape[0]
+    vmem = pl.BlockSpec(memory_space=pltpu.VMEM)
     return pl.pallas_call(
         functools.partial(
             norm_kernel, row_count=row_count, pair_count=pair_count, part=part
         ),
-        grid=(rows // step,),
-        in_specs=[
-            pl.BlockSpec((step, features), lambda i: (i, 0)),
-            pl.BlockSpec((1, features), lambda i: (0, 0)),
-        ],
-        out_specs=pl.BlockSpec((count, step, part), lambda i: (0, i, 0)),
-        out_shape=jax.ShapeDtypeStruct((count, rows, part), jnp.bfloat16),
+        in_specs=[vmem, vmem],
+        out_specs=vmem,
+        out_shape=pltpu.VMEM((row_count * pair_count, rows, part), jnp.bfloat16),
         compiler_params=params(),
         name="norm",
     )(tokens, norm_gain[None, :])
 
 
-def split_kernel(place_ref, near_ref, far_ref, near_out, far_out):
-    near_out[...] = near_ref[...]
-    far_out[...] = far_ref[...]
-
-
-def split(place, tile, pair_count, row_count):
-    rows, part = tile.shape[1:]
-    chips = row_count // 2 * pair_count
-
-    def index(odd):
-        def at(k, place):
-            pair = place[0] ^ (k % pair_count)
-            row = place[1] ^ ((k // pair_count) * 2 + odd)
-            return (pair * row_count + row, 0, 0)
-
-        return at
-
-    block = (1, rows, part)
-    out = pl.BlockSpec(block, lambda k, place: (k, 0, 0))
-    near, far = pl.pallas_call(
-        split_kernel,
-        grid_spec=pltpu.PrefetchScalarGridSpec(
-            num_scalar_prefetch=1,
-            grid=(chips,),
-            in_specs=[pl.BlockSpec(block, index(0)), pl.BlockSpec(block, index(1))],
-            out_specs=[out, out],
-        ),
-        out_shape=[jax.ShapeDtypeStruct((chips, rows, part), jnp.bfloat16)] * 2,
+def own_kernel(place_ref, tile_ref, weights_ref, near_rows, far_rows, near_ref, far_ref, weights, sems, *, pair_count, row_count):
+    rows = tile_ref.shape[1]
+    copies = [pltpu.make_async_copy(weights_ref, weights, sems.at[2, 0])]
+    halves = (near_rows, far_rows)
+    for odd in (1, 0):
+        for k in range(row_count // 2 * pair_count):
+            pair = place_ref[0] ^ (k % pair_count)
+            row = place_ref[1] ^ ((k // pair_count) * 2 + odd)
+            copies.append(
+                pltpu.make_async_copy(
+                    tile_ref.at[pair * row_count + row],
+                    halves[odd].at[pl.ds(k * rows, rows)],
+                    sems.at[odd, k],
+                )
+            )
+    for copy in copies:
+        copy.start()
+    for copy in copies:
+        copy.wait()
+    for half, out_ref in ((far_rows, far_ref), (near_rows, near_ref)):
+        product = jnp.dot(half[...], weights[...], preferred_element_type=jnp.float32)
+        out_ref[...] = product.reshape(out_ref.shape).astype(out_ref.dtype)
+
+
+def project_own(place, tile, weights, pair_count, row_count):
+    count, rows, part = tile.shape
+    chips = count // 2
+    n = weights.shape[1]
+    vmem = pl.BlockSpec(memory_space=pltpu.VMEM)
+    half = jax.ShapeDtypeStruct((chips * rows, part), jnp.bfloat16)
+    return pl.pallas_call(
+        functools.partial(own_kernel, pair_count=pair_count, row_count=row_count),
+        in_specs=[pl.BlockSpec(memory_space=pltpu.SMEM)] + [pl.BlockSpec(memory_space=pl.ANY)] * 2,
+        out_specs=[vmem] * 4,
+        out_shape=[
+            half,
+            half,
+            pltpu.VMEM((chips, rows, n), jnp.bfloat16),
+            pltpu.VMEM((chips, rows, n), jnp.bfloat16),
+        ],
+        scratch_shapes=[
+            pltpu.VMEM(weights.shape, jnp.bfloat16),
+            pltpu.SemaphoreType.DMA((3, chips)),
+        ],
         compiler_params=params(),
-        name="split",
-    )(place, tile, tile)
-    return near.reshape(chips * rows, part), far.reshape(chips * rows, part)
+        name="project_own",
+    )(place, tile, weights)
 
 
 def sum_kernel(place_ref, *refs, terms, kinds, width, outs):
@@ -198,8 +222,9 @@
     slot1 = exchange(own, 1)
     chips = [(r, d) for r in range(0, row_count, 2) for d in range(pair_count)]
     (tokens, own) = lax.optimization_barrier((tokens, own))
-    def spread(tokens):
-        parts = normalise(tokens, norm_gain, row_count, pair_count, part)
+    parts = normalise(tokens, norm_gain, row_count, pair_count, part)
+
+    def spread(parts):
         groups = [
             [(g * pair_count + d) * row_count + r for d in range(pair_count) for r in range(row_count)]
             for g in range(dp_count // pair_count)
@@ -213,32 +238,23 @@
             axis_index_groups=groups if len(groups) > 1 else None,
         )
 
-    tile = stage(spread, tokens)
-
-    def first(near, far, weights):
-        shape = (len(chips), own_rows, -1)
-        far_part = jnp.dot(far, weights, preferred_element_type=jnp.float32)
-        other = swap(far_part.astype(jnp.bfloat16).reshape(shape), 1, 0)
-        near_part = jnp.dot(near, weights, preferred_element_type=jnp.float32)
-        both = near_part.reshape(shape) + other.astype(jnp.float32)
-        return both.astype(jnp.bfloat16)
-
-    def first_of(near, far, inner_weights, outer_weights):
-        def dot(rows):
-            def product(rows, weights):
-                return jnp.dot(rows, weights, preferred_element_type=jnp.float32).astype(jnp.bfloat16)
-
-            return lax.cond(
-                inner == 1,
-                lambda r, i, o: product(r, i),
-                lambda r, i, o: product(r, o),
-                rows,
-                inner_weights,
-                outer_weights,
-            ).reshape(len(chips), own_rows, -1)
-
-        other = swap(dot(far), 1, 0)
-        return dot(near), other
+    tile = stage(spread, parts)
+
+    shape = (len(chips), own_rows, -1)
+
+    def dot(rows, weights):
+        product = jnp.dot(rows, weights, preferred_element_type=jnp.float32)
+        return product.reshape(shape)
+
+    def far_parts(blocks):
+        return [dot(far, w).astype(jnp.bfloat16) for w in blocks]
+
+    def first(near, far_parts, blocks):
+        others = [swap(part, 1, 0) for part in far_parts]
+        return [
+            (dot(near, w) + other.astype(jnp.float32)).astype(jnp.bfloat16)
+            for w, other in zip(blocks, others)
+        ]
 
     def second(both):
         return [swap(both[k], *chips[k]) for k in range(1, len(chips))]
@@ -248,30 +264,30 @@
         return finish(place, both, others, tables, held, slots, kinds, width, columns)
 
     kinds = ("key", "value")
+    def both_cores(near_part, far_part):
+        other = swap(far_part, 1, 0)
+        return (near_part.astype(jnp.float32) + other.astype(jnp.float32)).astype(jnp.bfloat16)
+
     (tile, own) = lax.optimization_barrier((tile, own))
-    def own_work(tile, own):
-        near, far = split(place, tile, pair_count, row_count)
-        return near, far, first(near, far, own)
-
-    near, far, both0 = stage(own_work, tile, own)
-    (near, far, both0, own, slot1, slot2) = lax.optimization_barrier((near, far, both0, own, slot1, slot2))
-    outer = exchange(slot2, 1, (1, 2))
+    near, far, near0, far0 = project_own(place, tile, own, pair_count, row_count)
+    held = stage(lambda n, f: add(both_cores(n, f), [], (0,), kinds), near0, far0)
+    (near, far, held, own, slot2) = lax.optimization_barrier((near, far, held, own, slot2))
+    outer = exchange(slot2, 1)
     middle = exchange(own, 3, (1, 2))
 
-    def middle_work(near, far, both0, slot1, slot2):
-        both12 = first(near, far, jnp.concatenate([slot1, slot2], axis=1))
-        both = jnp.concatenate([both0, both12], axis=2)
-        return add(both, [], (0, 1, 2), kinds)
-
-    held = stage(middle_work, near, far, both0, slot1, slot2)
+    def middle_work(near, far12, held, slot1, slot2):
+        both12 = first(near, far12, [slot1, slot2])
+        return add(jnp.concatenate(both12, axis=2), held, (1, 2), kinds)
+
+    held = stage(middle_work, near, far_parts([slot1, slot2]), held, slot1, slot2)
     (held, outer, middle) = lax.optimization_barrier((held, outer, middle))
     third = lax.optimization_barrier(jnp.where(inner == 1, middle, outer))
-    held = add(first(near, far, third), held, (3,), kinds)
+    held = add(first(near, far_parts([third]), [third])[0], held, (3,), kinds)
     blocks = [own, slot1, slot2, third]
     while len(blocks) < col_count:
         blocks += [exchange(w, len(blocks)) for w in blocks]
     for k in range(4, col_count):
-        held = add(first(near, far, blocks[k]), held, (k,), kinds)
+        held = add(first(near, far_parts([blocks[k]]), [blocks[k]])[0], held, (k,), kinds)
     key_rows, value_rows = held
     return (key_rows, value_rows)
 

time: 104 us -> 99 us (0.952)
  starting transfers between devices: 15 us -> 19.2 us
  waiting for transfers between devices: 28.7 us -> 25.1 us
  matrix products: 12.8 us -> 9.47 us
  Pallas kernels: 9.13 us -> 7.86 us
    ppermute x9 -> x13, starting transfers between devices: 7.33 us -> 11.4 us  [swap(): return lax.ppermute(array, ('dp', 'row'), pairs)]
    ppermute x4, waiting for transfers between devices: 3.33 us -> 0.01 us  [exchange(): lax.ppermute(array, 'col', [(i, i ^ bits) for i in range(col_count) if i...]
    dot_general x6, matrix products: 12.8 us -> 9.47 us  [dot(): product = jnp.dot(rows, weights, preferred_element_type=jnp.float32)]
    pallas_call x1, Pallas kernels: 3.23 us -> 1.11 us  [normalise(): pl.pallas_call(functools.partial(norm_kernel, row_count=row_count, pair_c...]
    unnamed x2 -> x10, local copies, waits for them, and re-layouts: 0.01 us -> 2.01 us
    concatenate x1 -> x0, local copies, waits for them, and re-layouts: 1.35 us -> none  [middle_work(): both12 = first(near, far, jnp.concatenate([slot1, slot2], axis=1))]
    pallas_call x1, Pallas kernels: 2.44 us -> 3.79 us  [project_own(): pl.pallas_call(functools.partial(own_kernel, pair_count=pair_count, row_c...]
    cond x1 -> x2, local copies, waits for them, and re-layouts: 1.34 us -> 0.01 us
  transfers between devices with their start and end apart: 13 -> 17, of which waited for: 8 -> 10; matrix products, arithmetic and copies ran while one was open for 14% -> 10% of each run, Pallas kernels for 8% -> 7%
where the time goes in v3:
time: 99 us; the launch traced here: 98.6 us
  blocking collectives  29.6 us (30%)
  waiting for transfers between devices  25.1 us (25%)
  starting transfers between devices  19.2 us (19%)
  matrix products  9.47 us (10%)
  Pallas kernels  7.86 us (8%)
  local copies, waits for them, and re-layouts  3.35 us (3%)
  other arithmetic  3 us (3%)
    all_to_all x1, blocking collectives, spread(): lax.all_to_all(parts, ('dp', 'row'), split_axis=0, concat_axis=0, tiled=T...  29.6 us
    ppermute x13, waiting for transfers between devices, swap(): return lax.ppermute(array, ('dp', 'row'), pairs)  25.1 us
    ppermute x13, starting transfers between devices, swap(): return lax.ppermute(array, ('dp', 'row'), pairs)  11.4 us
    dot_general x6, matrix products, dot(): product = jnp.dot(rows, weights, preferred_element_type=jnp.float32)  9.47 us
    ppermute x4, starting transfers between devices, exchange(): lax.ppermute(array, 'col', [(i, i ^ bits) for i in range(col_count) if i...  7.83 us
    pallas_call x1, Pallas kernels, project_own(): pl.pallas_call(functools.partial(own_kernel, pair_count=pair_count, row_c...  3.79 us
    pallas_call x3, Pallas kernels, finish(): pl.pallas_call(functools.partial(sum_kernel, terms=1 + len(others), kinds...  2.97 us
    unnamed x10, local copies, waits for them, and re-layouts  2.01 us
  transfers between devices with their start and end apart: 17, of which 10 were waited for; matrix products, arithmetic and copies ran while one was open for 10% of the time, Pallas kernels for 7%

profile of v3, /device:TPU:0, one launch (start us, length us, event | category | flops | bytes accessed | tf_op | source)
XLA Modules:
  0.0 98.6 jit_solution(16939664040281660349)
XLA Ops:
  0.7 1.3 %constant_dynamic-slice_fusion = (bf16[1024,256]{1,0:T(8,128)(2,1)S(1)}, bf16[1024,256]{1,0:T(8,128)(2,1)S(1)}) fusion(bf16[2048,256]{1,0:T(8,128)(2,1)} %param.13, s32[]{:T(128)S(6)} %select_n.30, bf16[2048,256]{1,0:T(8,128)(2,1)} %param.12), kind=kLoop, calls=%fused_computation.34 | loop fusion | bytes 2097156 | tf_op jit(solution)/shard_map/dynamic_slice | solution.py:219
  2.0 4.1 %collective-permute-start.9 = (bf16[1024,512]{1,0:T(8,128)(2,1)S(1)}, bf16[1024,512]{1,0:T(8,128)(2,1)}, u32[]{:S(2)}, u32[]{:S(2)}) collective-permute-start(bf16[1024,512]{1,0:T(8,128)(2,1)S(1)} %pad_maximum_fusion.1.weights_ref), channel_id=1, source_target_pairs={{0,2},{1,3},{2,0},{3,1},{4,6},{5,7},{6,4},{7,5},{8,10},{9,11},{10,... | collective-permute-start | bytes 3145736 | tf_op jit(solution)/shard_map/ppermute | solution.py:198
  6.1 1.6 %collective-permute-start.10 = (bf16[1024,512]{1,0:T(8,128)(2,1)S(1)}, bf16[1024,512]{1,0:T(8,128)(2,1)}, u32[]{:S(2)}, u32[]{:S(2)}) collective-permute-start(bf16[1024,512]{1,0:T(8,128)(2,1)S(1)} %pad_maximum_fusion.1.weights_ref), channel_id=1, source_target_pairs={{0,1},{1,0},{2,3},{3,2},{4,5},{5,4},{6,7},{7,6},{8,9},{9,8},{10,11... | collective-permute-start | bytes 3145736 | tf_op jit(solution)/shard_map/ppermute | solution.py:198
  7.7 1.6 %copy-done = bf16[128,8192]{1,0:T(8,128)(2,1)S(1)} copy-done((bf16[128,8192]{1,0:T(8,128)(2,1)S(1)}, bf16[128,8192]{1,0:T(8,128)(2,1)}, u32[]{:S(2)}) %copy-start) | copy-done | bytes 2097176
  9.3 1.1 %norm.1 = bf16[8,128,1024]{2,1,0:T(8,128)(2,1)S(1)} custom-call(bf16[128,8192]{1,0:T(8,128)(2,1)S(1)} %copy-done, f32[1,8192]{1,0:T(1,128)S(1)} %bitcast.41), custom_call_target="tpu_custom_call" | custom-call | tf_op jit(solution)/shard_map/norm/pallas_call | solution.py:59
  10.4 29.6 %conditional.3 = (bf16[8,128,1024]{2,1,0:T(8,128)(2,1)}) conditional(s32[]{:T(128)} %convert_element_type.59, () %tuple.31, bf16[8,128,1024]{2,1,0:T(8,128)(2,1)S(1)} %norm.1), branch_computations={%region_0.1_spmd, %region_1.2_spmd} | conditional | bytes 4194312 | solution.py:215
  10.4 29.6 %all_to_all.4 = bf16[8,128,1024]{2,1,0:T(8,128)(2,1)} all-to-all(bf16[8,128,1024]{2,1,0:T(8,128)(2,1)S(1)} %param.1), channel_id=1, replica_groups=mesh['dp'=2,'row'=4,'col'=4] {'dp','row'}, dimensions={0} | all-to-all | bytes 4194304 | tf_op jit(solution)/shard_map/cond/branch_1_fun/all_to_all | solution.py:232
  40.1 3.8 %project_own.1 = (bf16[512,1024]{1,0:T(8,128)(2,1)}, bf16[512,1024]{1,0:T(8,128)(2,1)S(1)}, bf16[4,128,512]{2,1,0:T(8,128)(2,1)S(1)}, bf16[4,128,512]{2,1,0:T(8,128)(2,1)S(1)}) custom-call(s32[4]{0:T(128)S(1)} %pad_add_fusion.place_ref, bf16[8,128,1024]{2,1,0:T(8,128)(2,1)} %get-tuple-element.123.tile_ref, bf16[1024,512]{1,0:T(8,128)(2,1)S(1)} %pad_maximum_fusion.1.weights_ref), custom_call_target="tpu_custom_call" | custom-call | tf_op jit(solution)/shard_map/project_own/pallas_call | solution.py:101
  43.9 0.3 fusion.6
  44.4 12.1 %conditional.4 = ((bf16[128,1024]{1,0:T(8,128)(2,1)S(1)}, bf16[128,1024]{1,0:T(8,128)(2,1)S(1)})) conditional(s32[]{:T(128)} %convert_element_type.59, () %tuple.34, (bf16[4,128,512]{2,1,0:T(8,128)(2,1)S(1)}, bf16[4,128,512]{2,1,0:T(8,128)(2,1)S(1)}, s32[4]{0:T(128)S(1)}, f32[128,128]{1,0:T(8,128)S(1)}, f32[128,128]{1,0:T(8,128)S(1)}) %tuple.35), branch_computations={%region_2.3_spmd, %region_3.4_spmd} | conditional | flops 1048576 | bytes 6029480 | solution.py:215
  44.5 1.9 %collective-permute-done = bf16[4,128,512]{2,1,0:T(8,128)(2,1)S(1)} collective-permute-done((bf16[4,128,512]{2,1,0:T(8,128)(2,1)S(1)}, bf16[4,128,512]{2,1,0:T(8,128)(2,1)S(1)}, u32[]{:S(2)}, u32[]{:S(2)}) %collective-permute-start) | collective-permute-done | bytes 524320 | tf_op jit(solution)/shard_map/cond/branch_1_fun/ppermute | solution.py:195
  46.4 0.1 add_convert_fusion.refs_0_
  46.5 1.2 %collective-permute-start.1 = (bf16[128,512]{1,0:T(8,128)(2,1)S(1)}, bf16[128,512]{1,0:T(8,128)(2,1)S(1)}, u32[]{:S(2)}, u32[]{:S(2)}) collective-permute-start(bf16[128,512]{1,0:T(8,128)(2,1)S(1)} %get-tuple-element.101), channel_id=1, source_target_pairs={{0,16},{4,20},{8,24},{12,28},{16,0},{20,4},{24,8},{28,12},{1,17},{... | collective-permute-start | bytes 393224 | tf_op jit(solution)/shard_map/cond/branch_1_fun/ppermute | solution.py:195
  47.7 0.9 collective-permute-start.2
  48.7 1.4 %collective-permute-start.3 = (bf16[128,512]{1,0:T(8,128)(2,1)S(1)}, bf16[128,512]{1,0:T(8,128)(2,1)S(1)}, u32[]{:S(2)}, u32[]{:S(2)}) collective-permute-start(bf16[128,512]{1,0:T(8,128)(2,1)S(1)} %get-tuple-element.99), channel_id=1, source_target_pairs={{0,24},{4,28},{8,16},{12,20},{16,8},{20,12},{24,0},{28,4},{1,25},{... | collective-permute-start | bytes 393224 | tf_op jit(solution)/shard_map/cond/branch_1_fun/ppermute | solution.py:195
  50.1 2.8 %collective-permute-done.1.refs_1_ = bf16[128,512]{1,0:T(8,128)(2,1)S(1)} collective-permute-done((bf16[128,512]{1,0:T(8,128)(2,1)S(1)}, bf16[128,512]{1,0:T(8,128)(2,1)S(1)}, u32[]{:S(2)}, u32[]{:S(2)}) %collective-permute-start.1) | collective-permute-done | bytes 131104 | tf_op jit(solution)/shard_map/cond/branch_1_fun/ppermute | solution.py:195
  52.9 1.4 %collective-permute-done.2.refs_2_ = bf16[128,512]{1,0:T(8,128)(2,1)S(1)} collective-permute-done((bf16[128,512]{1,0:T(8,128)(2,1)S(1)}, bf16[128,512]{1,0:T(8,128)(2,1)S(1)}, u32[]{:S(2)}, u32[]{:S(2)}) %collective-permute-start.2) | collective-permute-done | bytes 131104 | tf_op jit(solution)/shard_map/cond/branch_1_fun/ppermute | solution.py:195
  54.3 1.6 %collective-permute-done.3.refs_3_ = bf16[128,512]{1,0:T(8,128)(2,1)S(1)} collective-permute-done((bf16[128,512]{1,0:T(8,128)(2,1)S(1)}, bf16[128,512]{1,0:T(8,128)(2,1)S(1)}, u32[]{:S(2)}, u32[]{:S(2)}) %collective-permute-start.3) | collective-permute-done | bytes 131104 | tf_op jit(solution)/shard_map/cond/branch_1_fun/ppermute | solution.py:195
  55.8 0.7 finish.3
  56.5 0.5 collective-permute-start.11
  57.0 1.6 %collective-permute-start.12 = (bf16[1024,512]{1,0:T(8,128)(2,1)S(1)}, bf16[1024,512]{1,0:T(8,128)(2,1)}, u32[]{:S(2)}, u32[]{:S(2)}) collective-permute-start(bf16[1024,512]{1,0:T(8,128)(2,1)S(1)} %pad_maximum_fusion.1.weights_ref), channel_id=1, source_target_pairs={{1,2},{2,1},{5,6},{6,5},{9,10},{10,9},{13,14},{14,13},{17,18},{18,... | collective-permute-start | bytes 3145736 | tf_op jit(solution)/shard_map/ppermute | solution.py:198
  58.7 1.9 %fusion.10 = bf16[512,512]{1,0:T(8,128)(2,1)S(1)} fusion(bf16[512,1024]{1,0:T(8,128)(2,1)S(1)} %get-tuple-element.88, bf16[1024,512]{1,0:T(8,128)(2,1)} %collective-permute-done.9), kind=kOutput, calls=%fused_computation.39 | convolution fusion | flops 536870912 | bytes 2621440 | tf_op jit(solution)/shard_map/dot_general | solution.py:246
  60.6 1.9 %fusion.9 = bf16[512,512]{1,0:T(8,128)(2,1)S(1)} fusion(bf16[512,1024]{1,0:T(8,128)(2,1)S(1)} %get-tuple-element.88, bf16[1024,512]{1,0:T(8,128)(2,1)} %collective-permute-done.10), kind=kOutput, calls=%fused_computation.38 | convolution fusion | flops 536870912 | bytes 2621440 | tf_op jit(solution)/shard_map/dot_general | solution.py:246
  62.6 20.9 %conditional.5 = ((bf16[128,1024]{1,0:T(8,128)(2,1)S(1)}, bf16[128,1024]{1,0:T(8,128)(2,1)S(1)})) conditional(s32[]{:T(128)} %convert_element_type.59, () %tuple.37, (bf16[512,1024]{1,0:T(8,128)(2,1)}, bf16[1024,512]{1,0:T(8,128)(2,1)}, bf16[512,512]{1,0:T(8,128)(2,1)S(1)}, bf16[1024,512]{1,0:T(8,128)(2,1)}, bf16[512,512]{1,0:T(8,128)(2,1)S(1)}, ...), branch_computations={%region_4.5_spmd, %region_5.6_spmd} | conditional | flops 1078984704 | bytes 25952492 | solution.py:215
  62.7 0.5 collective-permute-start.4
  63.2 2.2 %fusion.8 = f32[512,512]{1,0:T(8,128)S(1)} fusion(bf16[512,1024]{1,0:T(8,128)(2,1)} %get-tuple-element.44, bf16[1024,512]{1,0:T(8,128)(2,1)} %get-tuple-element.47), kind=kOutput, calls=%fused_computation.37 | convolution fusion | flops 536870912 | bytes 3145728 | tf_op jit(solution)/shard_map/cond/branch_1_fun/dot_general | solution.py:246
  65.4 1.9 %fusion.7 = f32[512,512]{1,0:T(8,128)S(1)} fusion(bf16[512,1024]{1,0:T(8,128)(2,1)S(1)} %copy-done.5, bf16[1024,512]{1,0:T(8,128)(2,1)} %get-tuple-element.45), kind=kOutput, calls=%fused_computation.36 | convolution fusion | flops 536870912 | bytes 3145728 | tf_op jit(solution)/shard_map/cond/branch_1_fun/dot_general | solution.py:246
  67.4 0.2 add_convert_fusion.1
  67.6 0.2 add_convert_fusion.2
  67.9 0.9 collective-permute-start.6
  68.8 1.5 %collective-permute-start.7 = (bf16[128,1024]{1,0:T(8,128)(2,1)S(1)}, bf16[128,1024]{1,0:T(8,128)(2,1)S(1)}, u32[]{:S(2)}, u32[]{:S(2)}) collective-permute-start(bf16[128,1024]{1,0:T(8,128)(2,1)S(1)} %get-tuple-element.104), channel_id=1, source_target_pairs={{0,8},{4,12},{8,0},{12,4},{16,24},{20,28},{24,16},{28,20},{1,9},{5... | collective-permute-start | bytes 786440 | tf_op jit(solution)/shard_map/cond/branch_1_fun/ppermute | solution.py:195
  70.3 1.2 %collective-permute-start.8 = (bf16[128,1024]{1,0:T(8,128)(2,1)S(1)}, bf16[128,1024]{1,0:T(8,128)(2,1)S(1)}, u32[]{:S(2)}, u32[]{:S(2)}) collective-permute-start(bf16[128,1024]{1,0:T(8,128)(2,1)S(1)} %get-tuple-element.102), channel_id=1, source_target_pairs={{0,24},{4,28},{8,16},{12,20},{16,8},{20,12},{24,0},{28,4},{1,25},{... | collective-permute-start | bytes 786440 | tf_op jit(solution)/shard_map/cond/branch_1_fun/ppermute | solution.py:195
  71.6 5.5 %collective-permute-done.6.refs_1_ = bf16[128,1024]{1,0:T(8,128)(2,1)S(1)} collective-permute-done((bf16[128,1024]{1,0:T(8,128)(2,1)S(1)}, bf16[128,1024]{1,0:T(8,128)(2,1)S(1)}, u32[]{:S(2)}, u32[]{:S(2)}) %collective-permute-start.6) | collective-permute-done | bytes 262176 | tf_op jit(solution)/shard_map/cond/branch_1_fun/ppermute | solution.py:195
  77.1 5.3 %collective-permute-done.7.refs_2_ = bf16[128,1024]{1,0:T(8,128)(2,1)S(1)} collective-permute-done((bf16[128,1024]{1,0:T(8,128)(2,1)S(1)}, bf16[128,1024]{1,0:T(8,128)(2,1)S(1)}, u32[]{:S(2)}, u32[]{:S(2)}) %collective-permute-start.7) | collective-permute-done | bytes 262176 | tf_op jit(solution)/shard_map/cond/branch_1_fun/ppermute | solution.py:195
  82.4 1.0 %finish.4 = (bf16[128,1024]{1,0:T(8,128)(2,1)S(1)}, bf16[128,1024]{1,0:T(8,128)(2,1)S(1)}) custom-call(s32[4]{0:T(128)S(1)} %get-tuple-element.43.place_ref, bf16[4,128,1024]{2,1,0:T(8,128)(2,1)S(1)} %pad_maximum_fusion.refs_0_, bf16[128,1024]{1,0:T(8,128)(2,1)S(1)} %collective-permute-done.6.refs_1_, ...), custom_call_target="tpu_custom_call", output_to_operand_aliasing={{0}: (7, {}), {1}: (8, {})} | custom-call | tf_op jit(solution)/shard_map/cond/branch_1_fun/finish/pallas_call | solution.py:156
  83.5 1.5 %broadcast_select_fusion = bf16[1024,512]{1,0:T(8,128)(2,1)S(1)} fusion(bf16[1024,512]{1,0:T(8,128)(2,1)} %collective-permute-done.12, bf16[1024,512]{1,0:T(8,128)(2,1)} %collective-permute-done.11, pred[]{:T(512)S(6)} %eq.6), kind=kLoop, calls=%fused_computation.22 | loop fusion | flops 524288 | bytes 3145729 | tf_op jit(solution)/shard_map/jit(_where)/select_n | solution.py:284
  85.0 0.7 convolution_convert_fusion
  85.8 0.4 copy-done.4
  86.2 0.7 fusion.11
  87.0 0.8 collective-permute-done.13
  87.7 0.2 add_convert_fusion.3.refs_0_
  87.9 1.3 %collective-permute-start.14 = (bf16[128,512]{1,0:T(8,128)(2,1)S(1)}, bf16[128,512]{1,0:T(8,128)(2,1)S(1)}, u32[]{:S(2)}, u32[]{:S(2)}) collective-permute-start(bf16[128,512]{1,0:T(8,128)(2,1)S(1)} %get-tuple-element.107), channel_id=1, source_target_pairs={{0,16},{4,20},{8,24},{12,28},{16,0},{20,4},{24,8},{28,12},{1,17},{... | collective-permute-start | bytes 393224 | tf_op jit(solution)/shard_map/ppermute | solution.py:195
  89.2 0.9 collective-permute-start.15
  90.1 1.4 %collective-permute-start.16 = (bf16[128,512]{1,0:T(8,128)(2,1)S(1)}, bf16[128,512]{1,0:T(8,128)(2,1)S(1)}, u32[]{:S(2)}, u32[]{:S(2)}) collective-permute-start(bf16[128,512]{1,0:T(8,128)(2,1)S(1)} %get-tuple-element.105), channel_id=1, source_target_pairs={{0,24},{4,28},{8,16},{12,20},{16,8},{20,12},{24,0},{28,4},{1,25},{... | collective-permute-start | bytes 393224 | tf_op jit(solution)/shard_map/ppermute | solution.py:195
  91.5 2.7 %collective-permute-done.14.refs_1_ = bf16[128,512]{1,0:T(8,128)(2,1)S(1)} collective-permute-done((bf16[128,512]{1,0:T(8,128)(2,1)S(1)}, bf16[128,512]{1,0:T(8,128)(2,1)S(1)}, u32[]{:S(2)}, u32[]{:S(2)}) %collective-permute-start.14) | collective-permute-done | bytes 131104 | tf_op jit(solution)/shard_map/ppermute | solution.py:195
  94.2 1.5 %collective-permute-done.15.refs_2_ = bf16[128,512]{1,0:T(8,128)(2,1)S(1)} collective-permute-done((bf16[128,512]{1,0:T(8,128)(2,1)S(1)}, bf16[128,512]{1,0:T(8,128)(2,1)S(1)}, u32[]{:S(2)}, u32[]{:S(2)}) %collective-permute-start.15) | collective-permute-done | bytes 131104 | tf_op jit(solution)/shard_map/ppermute | solution.py:195
  95.7 1.6 %collective-permute-done.16.refs_3_ = bf16[128,512]{1,0:T(8,128)(2,1)S(1)} collective-permute-done((bf16[128,512]{1,0:T(8,128)(2,1)S(1)}, bf16[128,512]{1,0:T(8,128)(2,1)S(1)}, u32[]{:S(2)}, u32[]{:S(2)}) %collective-permute-start.16) | collective-permute-done | bytes 131104 | tf_op jit(solution)/shard_map/ppermute | solution.py:195
  97.3 1.3 %finish.5 = (bf16[128,1024]{1,0:T(8,128)(2,1)}, bf16[128,1024]{1,0:T(8,128)(2,1)}) custom-call(s32[4]{0:T(128)S(1)} %pad_add_fusion.place_ref, bf16[4,128,512]{2,1,0:T(8,128)(2,1)S(1)} %add_convert_fusion.3.refs_0_, bf16[128,512]{1,0:T(8,128)(2,1)S(1)} %collective-permute-done.14.refs_1_, ...), custom_call_target="tpu_custom_call", output_to_operand_aliasing={{0}: (7, {}), {1}: (8, {})} | custom-call | tf_op jit(solution)/shard_map/finish/pallas_call | solution.py:156
  (29 shorter events, 0.8 us)
Async XLA Ops:
  0.6 7.1 %copy-start.1 = (f32[8192]{0:T(1024)S(1)}, f32[8192]{0:T(1024)}, u32[]{:S(2)}) copy-start(f32[8192]{0:T(1024)} %param.11) | copy-start | bytes 98308
  2.0 54.5 %collective-permute-start.9 = (bf16[1024,512]{1,0:T(8,128)(2,1)S(1)}, bf16[1024,512]{1,0:T(8,128)(2,1)}, u32[]{:S(2)}, u32[]{:S(2)}) collective-permute-start(bf16[1024,512]{1,0:T(8,128)(2,1)S(1)} %pad_maximum_fusion.1.weights_ref), channel_id=1, source_target_pairs={{0,2},{1,3},{2,0},{3,1},{4,6},{5,7},{6,4},{7,5},{8,10},{9,11},{10,... | collective-permute-start | bytes 3145736 | tf_op jit(solution)/shard_map/ppermute | solution.py:198
  6.1 54.5 %collective-permute-start.10 = (bf16[1024,512]{1,0:T(8,128)(2,1)S(1)}, bf16[1024,512]{1,0:T(8,128)(2,1)}, u32[]{:S(2)}, u32[]{:S(2)}) collective-permute-start(bf16[1024,512]{1,0:T(8,128)(2,1)S(1)} %pad_maximum_fusion.1.weights_ref), channel_id=1, source_target_pairs={{0,1},{1,0},{2,3},{3,2},{4,5},{5,4},{6,7},{7,6},{8,9},{9,8},{10,11... | collective-permute-start | bytes 3145736 | tf_op jit(solution)/shard_map/ppermute | solution.py:198
  7.7 1.6 %copy-start = (bf16[128,8192]{1,0:T(8,128)(2,1)S(1)}, bf16[128,8192]{1,0:T(8,128)(2,1)}, u32[]{:S(2)}) copy-start(bf16[128,8192]{1,0:T(8,128)(2,1)} %tokens_ref) | copy-start | bytes 6291460
  44.4 2.0 %collective-permute-start = (bf16[4,128,512]{2,1,0:T(8,128)(2,1)S(1)}, bf16[4,128,512]{2,1,0:T(8,128)(2,1)S(1)}, u32[]{:S(2)}, u32[]{:S(2)}) collective-permute-start(bf16[4,128,512]{2,1,0:T(8,128)(2,1)S(1)} %get-tuple-element.40), channel_id=1, source_target_pairs={{0,4},{4,0},{8,12},{12,8},{16,20},{20,16},{24,28},{28,24},{1,5},{5... | collective-permute-start | bytes 1572872 | tf_op jit(solution)/shard_map/cond/branch_1_fun/ppermute | solution.py:195
  46.5 6.3 %collective-permute-start.1 = (bf16[128,512]{1,0:T(8,128)(2,1)S(1)}, bf16[128,512]{1,0:T(8,128)(2,1)S(1)}, u32[]{:S(2)}, u32[]{:S(2)}) collective-permute-start(bf16[128,512]{1,0:T(8,128)(2,1)S(1)} %get-tuple-element.101), channel_id=1, source_target_pairs={{0,16},{4,20},{8,24},{12,28},{16,0},{20,4},{24,8},{28,12},{1,17},{... | collective-permute-start | bytes 393224 | tf_op jit(solution)/shard_map/cond/branch_1_fun/ppermute | solution.py:195
  47.7 6.5 %collective-permute-start.2 = (bf16[128,512]{1,0:T(8,128)(2,1)S(1)}, bf16[128,512]{1,0:T(8,128)(2,1)S(1)}, u32[]{:S(2)}, u32[]{:S(2)}) collective-permute-start(bf16[128,512]{1,0:T(8,128)(2,1)S(1)} %get-tuple-element.100), channel_id=1, source_target_pairs={{0,8},{4,12},{8,0},{12,4},{16,24},{20,28},{24,16},{28,20},{1,9},{5... | collective-permute-start | bytes 393224 | tf_op jit(solution)/shard_map/cond/branch_1_fun/ppermute | solution.py:195
  48.7 7.2 %collective-permute-start.3 = (bf16[128,512]{1,0:T(8,128)(2,1)S(1)}, bf16[128,512]{1,0:T(8,128)(2,1)S(1)}, u32[]{:S(2)}, u32[]{:S(2)}) collective-permute-start(bf16[128,512]{1,0:T(8,128)(2,1)S(1)} %get-tuple-element.99), channel_id=1, source_target_pairs={{0,24},{4,28},{8,16},{12,20},{16,8},{20,12},{24,0},{28,4},{1,25},{... | collective-permute-start | bytes 393224 | tf_op jit(solution)/shard_map/cond/branch_1_fun/ppermute | solution.py:195
  56.5 27.0 %collective-permute-start.11 = (bf16[1024,512]{1,0:T(8,128)(2,1)}, bf16[1024,512]{1,0:T(8,128)(2,1)}, u32[]{:S(2)}, u32[]{:S(2)}) collective-permute-start(bf16[1024,512]{1,0:T(8,128)(2,1)} %collective-permute-done.9), channel_id=1, source_target_pairs={{0,1},{1,0},{2,3},{3,2},{4,5},{5,4},{6,7},{7,6},{8,9},{9,8},{10,11... | collective-permute-start | bytes 3145736 | tf_op jit(solution)/shard_map/ppermute | solution.py:198
  57.0 26.5 %collective-permute-start.12 = (bf16[1024,512]{1,0:T(8,128)(2,1)S(1)}, bf16[1024,512]{1,0:T(8,128)(2,1)}, u32[]{:S(2)}, u32[]{:S(2)}) collective-permute-start(bf16[1024,512]{1,0:T(8,128)(2,1)S(1)} %pad_maximum_fusion.1.weights_ref), channel_id=1, source_target_pairs={{1,2},{2,1},{5,6},{6,5},{9,10},{10,9},{13,14},{14,13},{17,18},{18,... | collective-permute-start | bytes 3145736 | tf_op jit(solution)/shard_map/ppermute | solution.py:198
  62.6 2.8 %copy-start.5 = (bf16[512,1024]{1,0:T(8,128)(2,1)S(1)}, bf16[512,1024]{1,0:T(8,128)(2,1)}, u32[]{:S(2)}) copy-start(bf16[512,1024]{1,0:T(8,128)(2,1)} %get-tuple-element.44) | copy-start | bytes 3145732 | tf_op jit(solution)/shard_map/cond
  62.6 4.8 %collective-permute-start.5 = (bf16[4,128,512]{2,1,0:T(8,128)(2,1)S(1)}, bf16[4,128,512]{2,1,0:T(8,128)(2,1)S(1)}, u32[]{:S(2)}, u32[]{:S(2)}) collective-permute-start(bf16[4,128,512]{2,1,0:T(8,128)(2,1)S(1)} %bitcast.45), channel_id=1, source_target_pairs={{0,4},{4,0},{8,12},{12,8},{16,20},{20,16},{24,28},{28,24},{1,5},{5... | collective-permute-start | bytes 1572872 | tf_op jit(solution)/shard_map/cond/branch_1_fun/ppermute | solution.py:195
  62.7 4.9 %collective-permute-start.4 = (bf16[4,128,512]{2,1,0:T(8,128)(2,1)S(1)}, bf16[4,128,512]{2,1,0:T(8,128)(2,1)S(1)}, u32[]{:S(2)}, u32[]{:S(2)}) collective-permute-start(bf16[4,128,512]{2,1,0:T(8,128)(2,1)S(1)} %bitcast.46), channel_id=1, source_target_pairs={{0,4},{4,0},{8,12},{12,8},{16,20},{20,16},{24,28},{28,24},{1,5},{5... | collective-permute-start | bytes 1572872 | tf_op jit(solution)/shard_map/cond/branch_1_fun/ppermute | solution.py:195
  67.9 9.2 %collective-permute-start.6 = (bf16[128,1024]{1,0:T(8,128)(2,1)S(1)}, bf16[128,1024]{1,0:T(8,128)(2,1)S(1)}, u32[]{:S(2)}, u32[]{:S(2)}) collective-permute-start(bf16[128,1024]{1,0:T(8,128)(2,1)S(1)} %get-tuple-element.103), channel_id=1, source_target_pairs={{0,16},{4,20},{8,24},{12,28},{16,0},{20,4},{24,8},{28,12},{1,17},{... | collective-permute-start | bytes 786440 | tf_op jit(solution)/shard_map/cond/branch_1_fun/ppermute | solution.py:195
  68.8 13.6 %collective-permute-start.7 = (bf16[128,1024]{1,0:T(8,128)(2,1)S(1)}, bf16[128,1024]{1,0:T(8,128)(2,1)S(1)}, u32[]{:S(2)}, u32[]{:S(2)}) collective-permute-start(bf16[128,1024]{1,0:T(8,128)(2,1)S(1)} %get-tuple-element.104), channel_id=1, source_target_pairs={{0,8},{4,12},{8,0},{12,4},{16,24},{20,28},{24,16},{28,20},{1,9},{5... | collective-permute-start | bytes 786440 | tf_op jit(solution)/shard_map/cond/branch_1_fun/ppermute | solution.py:195
  70.3 12.2 %collective-permute-start.8 = (bf16[128,1024]{1,0:T(8,128)(2,1)S(1)}, bf16[128,1024]{1,0:T(8,128)(2,1)S(1)}, u32[]{:S(2)}, u32[]{:S(2)}) collective-permute-start(bf16[128,1024]{1,0:T(8,128)(2,1)S(1)} %get-tuple-element.102), channel_id=1, source_target_pairs={{0,24},{4,28},{8,16},{12,20},{16,8},{20,12},{24,0},{28,4},{1,25},{... | collective-permute-start | bytes 786440 | tf_op jit(solution)/shard_map/cond/branch_1_fun/ppermute | solution.py:195
  83.5 2.3 %copy-start.2 = (bf16[128,1024]{1,0:T(8,128)(2,1)}, bf16[128,1024]{1,0:T(8,128)(2,1)S(1)}, u32[]{:S(2)}) copy-start(bf16[128,1024]{1,0:T(8,128)(2,1)S(1)} %get-tuple-element.97.refs_6_) | copy-start | bytes 786436
  83.5 2.3 %copy-start.3 = (bf16[128,1024]{1,0:T(8,128)(2,1)}, bf16[128,1024]{1,0:T(8,128)(2,1)S(1)}, u32[]{:S(2)}) copy-start(bf16[128,1024]{1,0:T(8,128)(2,1)S(1)} %get-tuple-element.98.refs_7_) | copy-start | bytes 786436
  85.0 1.2 %copy-start.4 = (bf16[512,1024]{1,0:T(8,128)(2,1)S(1)}, bf16[512,1024]{1,0:T(8,128)(2,1)}, u32[]{:S(2)}) copy-start(bf16[512,1024]{1,0:T(8,128)(2,1)} %get-tuple-element.87) | copy-start | bytes 3145732
  85.8 2.0 %collective-permute-start.13 = (bf16[4,128,512]{2,1,0:T(8,128)(2,1)S(1)}, bf16[4,128,512]{2,1,0:T(8,128)(2,1)S(1)}, u32[]{:S(2)}, u32[]{:S(2)}) collective-permute-start(bf16[4,128,512]{2,1,0:T(8,128)(2,1)S(1)} %bitcast.47), channel_id=1, source_target_pairs={{0,4},{4,0},{8,12},{12,8},{16,20},{20,16},{24,28},{28,24},{1,5},{5... | collective-permute-start | bytes 1572872 | tf_op jit(solution)/shard_map/ppermute | solution.py:195
  87.9 6.3 %collective-permute-start.14 = (bf16[128,512]{1,0:T(8,128)(2,1)S(1)}, bf16[128,512]{1,0:T(8,128)(2,1)S(1)}, u32[]{:S(2)}, u32[]{:S(2)}) collective-permute-start(bf16[128,512]{1,0:T(8,128)(2,1)S(1)} %get-tuple-element.107), channel_id=1, source_target_pairs={{0,16},{4,20},{8,24},{12,28},{16,0},{20,4},{24,8},{28,12},{1,17},{... | collective-permute-start | bytes 393224 | tf_op jit(solution)/shard_map/ppermute | solution.py:195
  89.2 6.5 %collective-permute-start.15 = (bf16[128,512]{1,0:T(8,128)(2,1)S(1)}, bf16[128,512]{1,0:T(8,128)(2,1)S(1)}, u32[]{:S(2)}, u32[]{:S(2)}) collective-permute-start(bf16[128,512]{1,0:T(8,128)(2,1)S(1)} %get-tuple-element.106), channel_id=1, source_target_pairs={{0,8},{4,12},{8,0},{12,4},{16,24},{20,28},{24,16},{28,20},{1,9},{5... | collective-permute-start | bytes 393224 | tf_op jit(solution)/shard_map/ppermute | solution.py:195
  90.1 7.2 %collective-permute-start.16 = (bf16[128,512]{1,0:T(8,128)(2,1)S(1)}, bf16[128,512]{1,0:T(8,128)(2,1)S(1)}, u32[]{:S(2)}, u32[]{:S(2)}) collective-permute-start(bf16[128,512]{1,0:T(8,128)(2,1)S(1)} %get-tuple-element.105), channel_id=1, source_target_pairs={{0,24},{4,28},{8,16},{12,20},{16,8},{20,12},{24,0},{28,4},{1,25},{... | collective-permute-start | bytes 393224 | tf_op jit(solution)/shard_map/ppermute | solution.py:195

commit v4 on v3

--- a/solution.py
+++ b/solution.py
@@ -97,7 +97,7 @@
     chips = count // 2
     n = weights.shape[1]
     vmem = pl.BlockSpec(memory_space=pltpu.VMEM)
-    half = jax.ShapeDtypeStruct((chips * rows, part), jnp.bfloat16)
+    half = pltpu.HBM((chips * rows, part), jnp.bfloat16)
     return pl.pallas_call(
         functools.partial(own_kernel, pair_count=pair_count, row_count=row_count),
         in_specs=[pl.BlockSpec(memory_space=pltpu.SMEM)] + [pl.BlockSpec(memory_space=pl.ANY)] * 2,
@@ -117,57 +117,111 @@
     )(place, tile, weights)
 
 
-def sum_kernel(place_ref, *refs, terms, kinds, width, outs):
+def pair_kernel(near_hbm, far_hbm, *refs, count):
+    blocks, (near_ref, far_ref) = refs[:count], refs[count : count + 2]
+    near, far, weights, sems = refs[count + 2 :]
+    n = weights.shape[2]
+    copies = [pltpu.make_async_copy(far_hbm, far, sems.at[0])]
+    copies += [
+        pltpu.make_async_copy(block, weights.at[i], sems.at[2 + i])
+        for i, block in enumerate(blocks)
+    ]
+    copies.append(pltpu.make_async_copy(near_hbm, near, sems.at[1]))
+    for copy in copies:
+        copy.start()
+
+    def write(rows, out_ref, i):
+        product = jnp.dot(rows[...], weights[i], preferred_element_type=jnp.float32)
+        shape = out_ref.shape[:2] + (n,)
+        out_ref[:, :, i * n : (i + 1) * n] = product.reshape(shape).astype(out_ref.dtype)
+
+    copies[0].wait()
+    for i in range(count):
+        copies[1 + i].wait()
+        write(far, far_ref, i)
+    copies[-1].wait()
+    for i in range(count):
+        write(near, near_ref, i)
+
+
+def project_both(near, far, blocks, rows):
+    part, n = blocks[0].shape
+    count = len(blocks)
+    chips = near.shape[0] // rows
+    vmem = pl.BlockSpec(memory_space=pltpu.VMEM)
+    out = pltpu.VMEM((chips, rows, n * count), jnp.bfloat16)
+    return pl.pallas_call(
+        functools.partial(pair_kernel, count=count),
+        in_specs=[pl.BlockSpec(memory_space=pl.ANY)] * (2 + count),
+        out_specs=[vmem, vmem],
+        out_shape=[out, out],
+        scratch_shapes=[
+            pltpu.VMEM(near.shape, jnp.bfloat16),
+            pltpu.VMEM(far.shape, jnp.bfloat16),
+            pltpu.VMEM((count, part, n), jnp.bfloat16),
+            pltpu.SemaphoreType.DMA((2 + count,)),
+        ],
+        compiler_params=pltpu.CompilerParams(vmem_limit_bytes=24 * 1024 * 1024),
+        name="project_both",
+    )(near, far, *blocks)
+
+
+def sum_kernel(place_ref, *refs, terms, slots, kinds, width, held):
     cosine_ref, sine_ref = refs[terms : terms + 2]
-    out_refs = refs[-outs:]
-    total = refs[0][0].astype(jnp.float32)
-    for ref in refs[1:terms]:
-        total = total + ref[...].astype(jnp.float32)
-    for i, kind in enumerate(kinds):
-        block = total[:, i * width : (i + 1) * width]
-        out_ref = out_refs[i]
-        if kind == "key":
-            for h in range(width // HEAD):
-                head = block[:, h * HEAD : (h + 1) * HEAD]
-                turned = head * cosine_ref[...] + pltpu.roll(
-                    head, HEAD // 2, 1
-                ) * sine_ref[...]
-                out_ref[:, h * HEAD : (h + 1) * HEAD] = turned.astype(jnp.bfloat16)
-        else:
-            out_ref[...] = block.astype(jnp.bfloat16)
+    first_out = terms + 2 + held
+    out_refs = refs[first_out : first_out + len(kinds)]
+    blocks_ref, sems = refs[first_out + len(kinds) :]
+    copies = []
+    for s, slot in enumerate(slots):
+        for i, kind in enumerate(kinds):
+            at = (s * len(kinds) + i) * width
+            block = refs[0][0, :, at : at + width].astype(jnp.float32)
+            for ref in refs[1:terms]:
+                block = block + ref[:, at : at + width].astype(jnp.float32)
+            if kind == "key":
+                turned = []
+                for h in range(0, width, HEAD):
+                    head = block[:, h : h + HEAD]
+                    other = pltpu.roll(head, HEAD // 2, 1)
+                    turned.append(head * cosine_ref[...] + other * sine_ref[...])
+                block = jnp.concatenate(turned, axis=1)
+            blocks_ref[s, i] = block.astype(jnp.bfloat16)
+            column = pl.multiple_of((place_ref[2] ^ slot) * width, width)
+            copy = pltpu.make_async_copy(
+                blocks_ref.at[s, i], out_refs[i].at[:, pl.ds(column, width)], sems.at[s, i]
+            )
+            copy.start()
+            copies.append(copy)
+    for copy in copies:
+        copy.wait()
 
 
 def finish(place, both, others, tables, held, slots, kinds, width, columns):
     rows = both.shape[1]
-    n = len(kinds) * width
-    first_slot = slots[0]
     arrays = [both, *others, *tables]
-    specs = [pl.BlockSpec((1, rows, n), lambda k, place: (0, 0, k))]
-    specs += [pl.BlockSpec((rows, n), lambda k, place: (0, k)) for o in others]
-    specs += [pl.BlockSpec((rows, HEAD), lambda k, place: (0, 0)) for t in tables]
-    aliases = {}
-    for i, h in enumerate(held):
-        aliases[1 + len(arrays)] = i
-        arrays.append(h)
-        specs.append(pl.BlockSpec(memory_space=pl.ANY))
-    out_spec = pl.BlockSpec(
-        (rows, width), lambda k, place: (0, place[2] ^ (k + first_slot))
-    )
+    vmem = pl.BlockSpec(memory_space=pltpu.VMEM)
+    specs = [pl.BlockSpec(memory_space=pltpu.SMEM)] + [vmem] * len(arrays)
+    specs += [pl.BlockSpec(memory_space=pl.ANY)] * len(held)
     return pl.pallas_call(
         functools.partial(
-            sum_kernel, terms=1 + len(others), kinds=kinds, width=width, outs=len(kinds)
+            sum_kernel,
+            terms=1 + len(others),
+            slots=slots,
+            kinds=kinds,
+            width=width,
+            held=len(held),
         ),
-        grid_spec=pltpu.PrefetchScalarGridSpec(
-            num_scalar_prefetch=1,
-            grid=(len(slots),),
-            in_specs=specs,
-            out_specs=[out_spec] * len(kinds),
-        ),
+        in_specs=specs,
+        out_specs=[pl.BlockSpec(memory_space=pl.ANY)] * len(kinds),
         out_shape=[jax.ShapeDtypeStruct((rows, columns), jnp.bfloat16)] * len(kinds),
-        input_output_aliases=aliases,
+        scratch_shapes=[
+            pltpu.VMEM((len(slots), len(kinds), rows, width), jnp.bfloat16),
+            pltpu.SemaphoreType.DMA((len(slots), len(kinds))),
+        ],
+        input_output_aliases={1 + len(arrays) + i: i for i in range(len(held))},
         compiler_params=params(),
         name="finish",
-    )(place, *arrays)
+    )(place, *arrays, *held)
 
 
 def body(tokens, norm_gain, w_key, w_value):
@@ -270,19 +324,24 @@
 
     (tile, own) = lax.optimization_barrier((tile, own))
     near, far, near0, far0 = project_own(place, tile, own, pair_count, row_count)
-    held = stage(lambda n, f: add(both_cores(n, f), [], (0,), kinds), near0, far0)
-    (near, far, held, own, slot2) = lax.optimization_barrier((near, far, held, own, slot2))
+
+    def sums(near_part, far_part):
+        both = both_cores(near_part, far_part)
+        return both[:1], second(both)
+
+    sums0 = stage(sums, near0, far0)
+    (near, far, sums0, own, slot2) = lax.optimization_barrier((near, far, sums0, own, slot2))
     outer = exchange(slot2, 1)
     middle = exchange(own, 3, (1, 2))
-
-    def middle_work(near, far12, held, slot1, slot2):
-        both12 = first(near, far12, [slot1, slot2])
-        return add(jnp.concatenate(both12, axis=2), held, (1, 2), kinds)
-
-    held = stage(middle_work, near, far_parts([slot1, slot2]), held, slot1, slot2)
-    (held, outer, middle) = lax.optimization_barrier((held, outer, middle))
+    near12, far12 = project_both(near, far, [slot1, slot2], own_rows)
+    sums12 = stage(sums, near12, far12)
+    (sums0, sums12, outer, middle) = lax.optimization_barrier((sums0, sums12, outer, middle))
     third = lax.optimization_barrier(jnp.where(inner == 1, middle, outer))
-    held = add(first(near, far_parts([third]), [third])[0], held, (3,), kinds)
+    both3 = first(near, far_parts([third]), [third])[0]
+    others3 = second(both3)
+    held = add(sums0[0], [], (0,), kinds, sums0[1])
+    held = add(sums12[0], held, (1, 2), kinds, sums12[1])
+    held = add(both3, held, (3,), kinds, others3)
     blocks = [own, slot1, slot2, third]
     while len(blocks) < col_count:
         blocks += [exchange(w, len(blocks)) for w in blocks]

time: 99 us -> 96 us (0.970)
  matrix products: 9.47 us -> 1.42 us
  Pallas kernels: 7.86 us -> 13.8 us
    dot_general x6 -> x2, matrix products: 9.47 us -> 1.42 us  [dot(): product = jnp.dot(rows, weights, preferred_element_type=jnp.float32)]
    pallas_call x3 -> x4, Pallas kernels: 2.97 us -> 9.16 us  [the longest x3 5.17 us: finish(): pl.pallas_call(functools.partial(sum_kernel, terms=1 + len(others), slots...]
    ppermute x13 -> x12, waiting for transfers between devices: 25.1 us -> 24.2 us  [swap(): return lax.ppermute(array, ('dp', 'row'), pairs)]
    ppermute x13 -> x12, starting transfers between devices: 11.4 us -> 10.9 us  [swap(): return lax.ppermute(array, ('dp', 'row'), pairs)]
  transfers between devices with their start and end apart: 17 -> 16, of which waited for: 10 -> 9; matrix products, arithmetic and copies ran while one was open for 10% -> 2% of each run, Pallas kernels for 7% -> 13%
where the time goes in v4:
time: 96 us; the launch traced here: 95.6 us
  blocking collectives  29.6 us (31%)
  waiting for transfers between devices  24.2 us (25%)
  starting transfers between devices  18.6 us (19%)
  Pallas kernels  13.8 us (14%)
  local copies, waits for them, and re-layouts  4.32 us (4%)
  other arithmetic  2.71 us (3%)
  matrix products  1.42 us (1%)
    all_to_all x1, blocking collectives, spread(): lax.all_to_all(parts, ('dp', 'row'), split_axis=0, concat_axis=0, tiled=T...  29.6 us
    ppermute x12, waiting for transfers between devices, swap(): return lax.ppermute(array, ('dp', 'row'), pairs)  24.2 us
    ppermute x12, starting transfers between devices, swap(): return lax.ppermute(array, ('dp', 'row'), pairs)  10.9 us
    ppermute x4, starting transfers between devices, exchange(): lax.ppermute(array, 'col', [(i, i ^ bits) for i in range(col_count) if i...  7.77 us
    pallas_call x3, Pallas kernels, finish(): pl.pallas_call(functools.partial(sum_kernel, terms=1 + len(others), slots...  5.17 us
    pallas_call x1, Pallas kernels, project_both(): pl.pallas_call(functools.partial(pair_kernel, count=count), in_specs=[pl....  4 us
    pallas_call x1, Pallas kernels, project_own(): pl.pallas_call(functools.partial(own_kernel, pair_count=pair_count, row_c...  3.55 us
    unnamed x10, local copies, waits for them, and re-layouts  2.91 us
  transfers between devices with their start and end apart: 16, of which 9 were waited for; matrix products, arithmetic and copies ran while one was open for 2% of the time, Pallas kernels for 13%

profile of v4, /device:TPU:0, one launch (start us, length us, event | category | flops | bytes accessed | tf_op | source)
XLA Modules:
  0.0 95.6 jit_solution(7113144479634736087)
XLA Ops:
  0.7 1.3 %constant_dynamic-slice_fusion = (bf16[1024,256]{1,0:T(8,128)(2,1)S(1)}, bf16[1024,256]{1,0:T(8,128)(2,1)S(1)}) fusion(bf16[2048,256]{1,0:T(8,128)(2,1)} %param.13, s32[]{:T(128)S(6)} %select_n.30, bf16[2048,256]{1,0:T(8,128)(2,1)} %param.12), kind=kLoop, calls=%fused_computation.23 | loop fusion | bytes 2097156 | tf_op jit(solution)/shard_map/dynamic_slice | solution.py:273
  1.9 0.1 pad_maximum_fusion.weights_ref
  2.0 4.1 %collective-permute-start.8 = (bf16[1024,512]{1,0:T(8,128)(2,1)S(1)}, bf16[1024,512]{1,0:T(8,128)(2,1)}, u32[]{:S(2)}, u32[]{:S(2)}) collective-permute-start(bf16[1024,512]{1,0:T(8,128)(2,1)S(1)} %pad_maximum_fusion.weights_ref), channel_id=1, source_target_pairs={{0,2},{1,3},{2,0},{3,1},{4,6},{5,7},{6,4},{7,5},{8,10},{9,11},{10,... | collective-permute-start | bytes 3145736 | tf_op jit(solution)/shard_map/ppermute | solution.py:252
  6.1 1.6 %collective-permute-start.9 = (bf16[1024,512]{1,0:T(8,128)(2,1)S(1)}, bf16[1024,512]{1,0:T(8,128)(2,1)}, u32[]{:S(2)}, u32[]{:S(2)}) collective-permute-start(bf16[1024,512]{1,0:T(8,128)(2,1)S(1)} %pad_maximum_fusion.weights_ref), channel_id=1, source_target_pairs={{0,1},{1,0},{2,3},{3,2},{4,5},{5,4},{6,7},{7,6},{8,9},{9,8},{10,11... | collective-permute-start | bytes 3145736 | tf_op jit(solution)/shard_map/ppermute | solution.py:252
  7.7 1.6 %copy-done = bf16[128,8192]{1,0:T(8,128)(2,1)S(1)} copy-done((bf16[128,8192]{1,0:T(8,128)(2,1)S(1)}, bf16[128,8192]{1,0:T(8,128)(2,1)}, u32[]{:S(2)}) %copy-start) | copy-done | bytes 2097176
  9.3 1.1 %norm.1 = bf16[8,128,1024]{2,1,0:T(8,128)(2,1)S(1)} custom-call(bf16[128,8192]{1,0:T(8,128)(2,1)S(1)} %copy-done, f32[1,8192]{1,0:T(1,128)S(1)} %bitcast.29), custom_call_target="tpu_custom_call" | custom-call | tf_op jit(solution)/shard_map/norm/pallas_call | solution.py:59
  10.4 29.6 %conditional.3 = (bf16[8,128,1024]{2,1,0:T(8,128)(2,1)}) conditional(s32[]{:T(128)} %convert_element_type.42, () %tuple.32, bf16[8,128,1024]{2,1,0:T(8,128)(2,1)S(1)} %norm.1), branch_computations={%region_0.1_spmd, %region_1.2_spmd} | conditional | bytes 4194312 | solution.py:269
  10.4 29.6 %all_to_all.4 = bf16[8,128,1024]{2,1,0:T(8,128)(2,1)} all-to-all(bf16[8,128,1024]{2,1,0:T(8,128)(2,1)S(1)} %param.1), channel_id=1, replica_groups=mesh['dp'=2,'row'=4,'col'=4] {'dp','row'}, dimensions={0} | all-to-all | bytes 4194304 | tf_op jit(solution)/shard_map/cond/branch_1_fun/all_to_all | solution.py:286
  40.0 0.1 pad_add_fusion.place_ref
  40.1 3.5 %project_own.1 = (bf16[512,1024]{1,0:T(8,128)(2,1)}, bf16[512,1024]{1,0:T(8,128)(2,1)}, bf16[4,128,512]{2,1,0:T(8,128)(2,1)S(1)}, bf16[4,128,512]{2,1,0:T(8,128)(2,1)S(1)}) custom-call(s32[4]{0:T(128)S(1)} %pad_add_fusion.place_ref, bf16[8,128,1024]{2,1,0:T(8,128)(2,1)} %get-tuple-element.128.tile_ref, bf16[1024,512]{1,0:T(8,128)(2,1)S(1)} %pad_maximum_fusion.weights_ref), custom_call_target="tpu_custom_call" | custom-call | tf_op jit(solution)/shard_map/project_own/pallas_call | solution.py:101
  43.7 11.6 %conditional.4 = (bf16[1,128,512]{2,1,0:T(8,128)(2,1)S(1)}, bf16[128,512]{1,0:T(8,128)(2,1)}, bf16[128,512]{1,0:T(8,128)(2,1)}, bf16[128,512]{1,0:T(8,128)(2,1)}) conditional(s32[]{:T(128)} %convert_element_type.42, () %tuple.35, (bf16[4,128,512]{2,1,0:T(8,128)(2,1)S(1)}, bf16[4,128,512]{2,1,0:T(8,128)(2,1)S(1)}) %tuple.36), branch_computations={%region_2.3_spmd, %region_3.4_spmd} | conditional | flops 1048576 | bytes 6291648 | solution.py:269
  43.8 1.9 %collective-permute-done = bf16[4,128,512]{2,1,0:T(8,128)(2,1)S(1)} collective-permute-done((bf16[4,128,512]{2,1,0:T(8,128)(2,1)S(1)}, bf16[4,128,512]{2,1,0:T(8,128)(2,1)S(1)}, u32[]{:S(2)}, u32[]{:S(2)}) %collective-permute-start) | collective-permute-done | bytes 524320 | tf_op jit(solution)/shard_map/cond/branch_1_fun/ppermute | solution.py:249
  45.7 0.1 add_convert_fusion
  45.9 1.2 %collective-permute-start.1 = (bf16[128,512]{1,0:T(8,128)(2,1)S(1)}, bf16[128,512]{1,0:T(8,128)(2,1)}, u32[]{:S(2)}, u32[]{:S(2)}) collective-permute-start(bf16[128,512]{1,0:T(8,128)(2,1)S(1)} %get-tuple-element.96), channel_id=1, source_target_pairs={{0,16},{4,20},{8,24},{12,28},{16,0},{20,4},{24,8},{28,12},{1,17},{... | collective-permute-start | bytes 393224 | tf_op jit(solution)/shard_map/cond/branch_1_fun/ppermute | solution.py:249
  47.1 0.9 collective-permute-start.2
  48.0 1.4 %collective-permute-start.3 = (bf16[128,512]{1,0:T(8,128)(2,1)S(1)}, bf16[128,512]{1,0:T(8,128)(2,1)}, u32[]{:S(2)}, u32[]{:S(2)}) collective-permute-start(bf16[128,512]{1,0:T(8,128)(2,1)S(1)} %get-tuple-element.94), channel_id=1, source_target_pairs={{0,24},{4,28},{8,16},{12,20},{16,8},{20,12},{24,0},{28,4},{1,25},{... | collective-permute-start | bytes 393224 | tf_op jit(solution)/shard_map/cond/branch_1_fun/ppermute | solution.py:249
  49.4 2.9 %collective-permute-done.1 = bf16[128,512]{1,0:T(8,128)(2,1)} collective-permute-done((bf16[128,512]{1,0:T(8,128)(2,1)S(1)}, bf16[128,512]{1,0:T(8,128)(2,1)}, u32[]{:S(2)}, u32[]{:S(2)}) %collective-permute-start.1) | collective-permute-done | bytes 131104 | tf_op jit(solution)/shard_map/cond/branch_1_fun/ppermute | solution.py:249
  52.3 1.3 %collective-permute-done.2 = bf16[128,512]{1,0:T(8,128)(2,1)} collective-permute-done((bf16[128,512]{1,0:T(8,128)(2,1)S(1)}, bf16[128,512]{1,0:T(8,128)(2,1)}, u32[]{:S(2)}, u32[]{:S(2)}) %collective-permute-start.2) | collective-permute-done | bytes 131104 | tf_op jit(solution)/shard_map/cond/branch_1_fun/ppermute | solution.py:249
  53.6 1.7 %collective-permute-done.3 = bf16[128,512]{1,0:T(8,128)(2,1)} collective-permute-done((bf16[128,512]{1,0:T(8,128)(2,1)S(1)}, bf16[128,512]{1,0:T(8,128)(2,1)}, u32[]{:S(2)}, u32[]{:S(2)}) %collective-permute-start.3) | collective-permute-done | bytes 131104 | tf_op jit(solution)/shard_map/cond/branch_1_fun/ppermute | solution.py:249
  55.3 0.5 collective-permute-start.10
  55.7 1.6 %collective-permute-start.11 = (bf16[1024,512]{1,0:T(8,128)(2,1)S(1)}, bf16[1024,512]{1,0:T(8,128)(2,1)}, u32[]{:S(2)}, u32[]{:S(2)}) collective-permute-start(bf16[1024,512]{1,0:T(8,128)(2,1)S(1)} %pad_maximum_fusion.weights_ref), channel_id=1, source_target_pairs={{1,2},{2,1},{5,6},{6,5},{9,10},{10,9},{13,14},{14,13},{17,18},{18,... | collective-permute-start | bytes 3145736 | tf_op jit(solution)/shard_map/ppermute | solution.py:252
  57.4 1.2 %copy-done.2 = bf16[512,1024]{1,0:T(8,128)(2,1)S(1)} copy-done((bf16[512,1024]{1,0:T(8,128)(2,1)S(1)}, bf16[512,1024]{1,0:T(8,128)(2,1)}, u32[]{:S(2)}) %copy-start.2) | copy-done | bytes 1048600
  58.6 4.0 %project_both.1 = (bf16[4,128,1024]{2,1,0:T(8,128)(2,1)S(1)}, bf16[4,128,1024]{2,1,0:T(8,128)(2,1)S(1)}) custom-call(bf16[512,1024]{1,0:T(8,128)(2,1)S(1)} %copy-done.1, bf16[512,1024]{1,0:T(8,128)(2,1)S(1)} %copy-done.2, bf16[1024,512]{1,0:T(8,128)(2,1)} %collective-permute-done.9.refs_0_, bf16[1024,512]{1,0:T(8,128)(2,1)} %collective-permute-done.8.refs_1_), custom_call_target="tpu_custom_call" | custom-call | tf_op jit(solution)/shard_map/project_both/pallas_call | solution.py:153
  62.6 17.9 %conditional.5 = (bf16[1,128,1024]{2,1,0:T(8,128)(2,1)S(1)}, bf16[128,1024]{1,0:T(8,128)(2,1)}, bf16[128,1024]{1,0:T(8,128)(2,1)}, bf16[128,1024]{1,0:T(8,128)(2,1)}) conditional(s32[]{:T(128)} %convert_element_type.42, () %tuple.38, (bf16[4,128,1024]{2,1,0:T(8,128)(2,1)S(1)}, bf16[4,128,1024]{2,1,0:T(8,128)(2,1)S(1)}) %project_both.1), branch_computations={%region_4.5_spmd, %region_5.6_spmd} | conditional | flops 2097152 | bytes 12583104 | solution.py:269
  62.6 0.1 collective-permute-start.4
  62.7 2.6 %collective-permute-done.4 = bf16[4,128,1024]{2,1,0:T(8,128)(2,1)S(1)} collective-permute-done((bf16[4,128,1024]{2,1,0:T(8,128)(2,1)S(1)}, bf16[4,128,1024]{2,1,0:T(8,128)(2,1)S(1)}, u32[]{:S(2)}, u32[]{:S(2)}) %collective-permute-start.4) | collective-permute-done | bytes 1048608 | tf_op jit(solution)/shard_map/cond/branch_1_fun/ppermute | solution.py:249
  65.3 0.4 add_convert_fusion.1
  65.8 0.1 slice_bitcast_fusion.3
  65.8 0.9 collective-permute-start.5
  66.7 1.5 %collective-permute-start.6 = (bf16[128,1024]{1,0:T(8,128)(2,1)S(1)}, bf16[128,1024]{1,0:T(8,128)(2,1)}, u32[]{:S(2)}, u32[]{:S(2)}) collective-permute-start(bf16[128,1024]{1,0:T(8,128)(2,1)S(1)} %get-tuple-element.99), channel_id=1, source_target_pairs={{0,8},{4,12},{8,0},{12,4},{16,24},{20,28},{24,16},{28,20},{1,9},{5... | collective-permute-start | bytes 786440 | tf_op jit(solution)/shard_map/cond/branch_1_fun/ppermute | solution.py:249
  68.2 1.2 %collective-permute-start.7 = (bf16[128,1024]{1,0:T(8,128)(2,1)S(1)}, bf16[128,1024]{1,0:T(8,128)(2,1)}, u32[]{:S(2)}, u32[]{:S(2)}) collective-permute-start(bf16[128,1024]{1,0:T(8,128)(2,1)S(1)} %get-tuple-element.98), channel_id=1, source_target_pairs={{0,24},{4,28},{8,16},{12,20},{16,8},{20,12},{24,0},{28,4},{1,25},{... | collective-permute-start | bytes 786440 | tf_op jit(solution)/shard_map/cond/branch_1_fun/ppermute | solution.py:249
  69.4 5.8 %collective-permute-done.5 = bf16[128,1024]{1,0:T(8,128)(2,1)} collective-permute-done((bf16[128,1024]{1,0:T(8,128)(2,1)S(1)}, bf16[128,1024]{1,0:T(8,128)(2,1)}, u32[]{:S(2)}, u32[]{:S(2)}) %collective-permute-start.5) | collective-permute-done | bytes 262176 | tf_op jit(solution)/shard_map/cond/branch_1_fun/ppermute | solution.py:249
  75.2 5.4 %collective-permute-done.6 = bf16[128,1024]{1,0:T(8,128)(2,1)} collective-permute-done((bf16[128,1024]{1,0:T(8,128)(2,1)S(1)}, bf16[128,1024]{1,0:T(8,128)(2,1)}, u32[]{:S(2)}, u32[]{:S(2)}) %collective-permute-start.6) | collective-permute-done | bytes 262176 | tf_op jit(solution)/shard_map/cond/branch_1_fun/ppermute | solution.py:249
  80.6 1.4 %broadcast_select_fusion = bf16[1024,512]{1,0:T(8,128)(2,1)S(1)} fusion(bf16[1024,512]{1,0:T(8,128)(2,1)} %collective-permute-done.11, bf16[1024,512]{1,0:T(8,128)(2,1)} %collective-permute-done.10, pred[]{:T(512)S(6)} %eq.6), kind=kLoop, calls=%fused_computation.11 | loop fusion | flops 524288 | bytes 3145729 | tf_op jit(solution)/shard_map/jit(_where)/select_n | solution.py:339
  82.0 0.1 copy-done.3
  82.1 0.7 convolution_convert_fusion
  82.9 0.7 fusion.1
  83.6 1.2 %collective-permute-done.12 = bf16[4,128,512]{2,1,0:T(8,128)(2,1)S(1)} collective-permute-done((bf16[4,128,512]{2,1,0:T(8,128)(2,1)S(1)}, bf16[4,128,512]{2,1,0:T(8,128)(2,1)S(1)}, u32[]{:S(2)}, u32[]{:S(2)}) %collective-permute-start.12) | collective-permute-done | bytes 524320 | tf_op jit(solution)/shard_map/ppermute | solution.py:249
  84.8 0.2 add_convert_fusion.2.refs_0_
  85.0 1.2 %collective-permute-start.13 = (bf16[128,512]{1,0:T(8,128)(2,1)S(1)}, bf16[128,512]{1,0:T(8,128)(2,1)S(1)}, u32[]{:S(2)}, u32[]{:S(2)}) collective-permute-start(bf16[128,512]{1,0:T(8,128)(2,1)S(1)} %get-tuple-element.104), channel_id=1, source_target_pairs={{0,16},{4,20},{8,24},{12,28},{16,0},{20,4},{24,8},{28,12},{1,17},{... | collective-permute-start | bytes 393224 | tf_op jit(solution)/shard_map/ppermute | solution.py:249
  86.2 0.9 collective-permute-start.14
  87.1 1.4 %collective-permute-start.15 = (bf16[128,512]{1,0:T(8,128)(2,1)S(1)}, bf16[128,512]{1,0:T(8,128)(2,1)S(1)}, u32[]{:S(2)}, u32[]{:S(2)}) collective-permute-start(bf16[128,512]{1,0:T(8,128)(2,1)S(1)} %get-tuple-element.102), channel_id=1, source_target_pairs={{0,24},{4,28},{8,16},{12,20},{16,8},{20,12},{24,0},{28,4},{1,25},{... | collective-permute-start | bytes 393224 | tf_op jit(solution)/shard_map/ppermute | solution.py:249
  88.5 0.3 fusion
  88.8 0.1 pad_maximum_fusion.1
  89.0 1.8 %finish.3 = (bf16[128,1024]{1,0:T(8,128)(2,1)}, bf16[128,1024]{1,0:T(8,128)(2,1)}) custom-call(s32[4]{0:T(128)S(1)} %pad_add_fusion.place_ref, bf16[1,128,512]{2,1,0:T(8,128)(2,1)S(1)} %get-tuple-element.86.refs_0_, bf16[128,512]{1,0:T(8,128)(2,1)} %get-tuple-element.87.refs_1_, bf16[128,512]{1,0:T(8,128)(2,1)} %get-tuple-element.88.refs_2_, ...), custom_call_target="tpu_custom_call" | custom-call | tf_op jit(solution)/shard_map/finish/pallas_call | solution.py:205
  90.8 2.0 %finish.4 = (bf16[128,1024]{1,0:T(8,128)(2,1)}, bf16[128,1024]{1,0:T(8,128)(2,1)}) custom-call(s32[4]{0:T(128)S(1)} %pad_add_fusion.place_ref, bf16[1,128,1024]{2,1,0:T(8,128)(2,1)S(1)} %get-tuple-element.82.refs_0_, bf16[128,1024]{1,0:T(8,128)(2,1)} %get-tuple-element.83.refs_1_, ...), custom_call_target="tpu_custom_call", output_to_operand_aliasing={{0}: (7, {}), {1}: (8, {})} | custom-call | tf_op jit(solution)/shard_map/finish/pallas_call | solution.py:205
  92.8 1.5 %collective-permute-done.15.refs_3_ = bf16[128,512]{1,0:T(8,128)(2,1)S(1)} collective-permute-done((bf16[128,512]{1,0:T(8,128)(2,1)S(1)}, bf16[128,512]{1,0:T(8,128)(2,1)S(1)}, u32[]{:S(2)}, u32[]{:S(2)}) %collective-permute-start.15) | collective-permute-done | bytes 131104 | tf_op jit(solution)/shard_map/ppermute | solution.py:249
  94.3 1.3 %finish.5 = (bf16[128,1024]{1,0:T(8,128)(2,1)}, bf16[128,1024]{1,0:T(8,128)(2,1)}) custom-call(s32[4]{0:T(128)S(1)} %pad_add_fusion.place_ref, bf16[4,128,512]{2,1,0:T(8,128)(2,1)S(1)} %add_convert_fusion.2.refs_0_, bf16[128,512]{1,0:T(8,128)(2,1)S(1)} %collective-permute-done.13.refs_1_, ...), custom_call_target="tpu_custom_call", output_to_operand_aliasing={{0}: (7, {}), {1}: (8, {})} | custom-call | tf_op jit(solution)/shard_map/finish/pallas_call | solution.py:205
  (20 shorter events, 0.3 us)
Async XLA Ops:
  0.6 7.1 %copy-start.4 = (f32[8192]{0:T(1024)S(1)}, f32[8192]{0:T(1024)}, u32[]{:S(2)}) copy-start(f32[8192]{0:T(1024)} %param.11) | copy-start | bytes 98308
  2.0 53.3 %collective-permute-start.8 = (bf16[1024,512]{1,0:T(8,128)(2,1)S(1)}, bf16[1024,512]{1,0:T(8,128)(2,1)}, u32[]{:S(2)}, u32[]{:S(2)}) collective-permute-start(bf16[1024,512]{1,0:T(8,128)(2,1)S(1)} %pad_maximum_fusion.weights_ref), channel_id=1, source_target_pairs={{0,2},{1,3},{2,0},{3,1},{4,6},{5,7},{6,4},{7,5},{8,10},{9,11},{10,... | collective-permute-start | bytes 3145736 | tf_op jit(solution)/shard_map/ppermute | solution.py:252
  6.1 51.3 %collective-permute-start.9 = (bf16[1024,512]{1,0:T(8,128)(2,1)S(1)}, bf16[1024,512]{1,0:T(8,128)(2,1)}, u32[]{:S(2)}, u32[]{:S(2)}) collective-permute-start(bf16[1024,512]{1,0:T(8,128)(2,1)S(1)} %pad_maximum_fusion.weights_ref), channel_id=1, source_target_pairs={{0,1},{1,0},{2,3},{3,2},{4,5},{5,4},{6,7},{7,6},{8,9},{9,8},{10,11... | collective-permute-start | bytes 3145736 | tf_op jit(solution)/shard_map/ppermute | solution.py:252
  7.7 1.6 %copy-start = (bf16[128,8192]{1,0:T(8,128)(2,1)S(1)}, bf16[128,8192]{1,0:T(8,128)(2,1)}, u32[]{:S(2)}) copy-start(bf16[128,8192]{1,0:T(8,128)(2,1)} %tokens_ref) | copy-start | bytes 6291460
  43.7 13.7 %copy-start.1 = (bf16[512,1024]{1,0:T(8,128)(2,1)S(1)}, bf16[512,1024]{1,0:T(8,128)(2,1)}, u32[]{:S(2)}) copy-start(bf16[512,1024]{1,0:T(8,128)(2,1)} %get-tuple-element.68.near_hbm) | copy-start | bytes 3145732
  43.7 2.0 %collective-permute-start = (bf16[4,128,512]{2,1,0:T(8,128)(2,1)S(1)}, bf16[4,128,512]{2,1,0:T(8,128)(2,1)S(1)}, u32[]{:S(2)}, u32[]{:S(2)}) collective-permute-start(bf16[4,128,512]{2,1,0:T(8,128)(2,1)S(1)} %get-tuple-element.13), channel_id=1, source_target_pairs={{0,4},{4,0},{8,12},{12,8},{16,20},{20,16},{24,28},{28,24},{1,5},{5... | collective-permute-start | bytes 1572872 | tf_op jit(solution)/shard_map/cond/branch_1_fun/ppermute | solution.py:249
  45.9 6.4 %collective-permute-start.1 = (bf16[128,512]{1,0:T(8,128)(2,1)S(1)}, bf16[128,512]{1,0:T(8,128)(2,1)}, u32[]{:S(2)}, u32[]{:S(2)}) collective-permute-start(bf16[128,512]{1,0:T(8,128)(2,1)S(1)} %get-tuple-element.96), channel_id=1, source_target_pairs={{0,16},{4,20},{8,24},{12,28},{16,0},{20,4},{24,8},{28,12},{1,17},{... | collective-permute-start | bytes 393224 | tf_op jit(solution)/shard_map/cond/branch_1_fun/ppermute | solution.py:249
  47.1 6.5 %collective-permute-start.2 = (bf16[128,512]{1,0:T(8,128)(2,1)S(1)}, bf16[128,512]{1,0:T(8,128)(2,1)}, u32[]{:S(2)}, u32[]{:S(2)}) collective-permute-start(bf16[128,512]{1,0:T(8,128)(2,1)S(1)} %get-tuple-element.95), channel_id=1, source_target_pairs={{0,8},{4,12},{8,0},{12,4},{16,24},{20,28},{24,16},{28,20},{1,9},{5... | collective-permute-start | bytes 393224 | tf_op jit(solution)/shard_map/cond/branch_1_fun/ppermute | solution.py:249
  48.0 7.3 %collective-permute-start.3 = (bf16[128,512]{1,0:T(8,128)(2,1)S(1)}, bf16[128,512]{1,0:T(8,128)(2,1)}, u32[]{:S(2)}, u32[]{:S(2)}) collective-permute-start(bf16[128,512]{1,0:T(8,128)(2,1)S(1)} %get-tuple-element.94), channel_id=1, source_target_pairs={{0,24},{4,28},{8,16},{12,20},{16,8},{20,12},{24,0},{28,4},{1,25},{... | collective-permute-start | bytes 393224 | tf_op jit(solution)/shard_map/cond/branch_1_fun/ppermute | solution.py:249
  55.3 25.3 %collective-permute-start.10 = (bf16[1024,512]{1,0:T(8,128)(2,1)}, bf16[1024,512]{1,0:T(8,128)(2,1)}, u32[]{:S(2)}, u32[]{:S(2)}) collective-permute-start(bf16[1024,512]{1,0:T(8,128)(2,1)} %collective-permute-done.8.refs_1_), channel_id=1, source_target_pairs={{0,1},{1,0},{2,3},{3,2},{4,5},{5,4},{6,7},{7,6},{8,9},{9,8},{10,11... | collective-permute-start | bytes 3145736 | tf_op jit(solution)/shard_map/ppermute | solution.py:252
  55.7 24.8 %collective-permute-start.11 = (bf16[1024,512]{1,0:T(8,128)(2,1)S(1)}, bf16[1024,512]{1,0:T(8,128)(2,1)}, u32[]{:S(2)}, u32[]{:S(2)}) collective-permute-start(bf16[1024,512]{1,0:T(8,128)(2,1)S(1)} %pad_maximum_fusion.weights_ref), channel_id=1, source_target_pairs={{1,2},{2,1},{5,6},{6,5},{9,10},{10,9},{13,14},{14,13},{17,18},{18,... | collective-permute-start | bytes 3145736 | tf_op jit(solution)/shard_map/ppermute | solution.py:252
  57.4 1.2 %copy-start.2 = (bf16[512,1024]{1,0:T(8,128)(2,1)S(1)}, bf16[512,1024]{1,0:T(8,128)(2,1)}, u32[]{:S(2)}) copy-start(bf16[512,1024]{1,0:T(8,128)(2,1)} %get-tuple-element.73.far_hbm) | copy-start | bytes 3145732
  62.6 2.7 %collective-permute-start.4 = (bf16[4,128,1024]{2,1,0:T(8,128)(2,1)S(1)}, bf16[4,128,1024]{2,1,0:T(8,128)(2,1)S(1)}, u32[]{:S(2)}, u32[]{:S(2)}) collective-permute-start(bf16[4,128,1024]{2,1,0:T(8,128)(2,1)S(1)} %get-tuple-element.15), channel_id=1, source_target_pairs={{0,4},{4,0},{8,12},{12,8},{16,20},{20,16},{24,28},{28,24},{1,5},{5... | collective-permute-start | bytes 3145736 | tf_op jit(solution)/shard_map/cond/branch_1_fun/ppermute | solution.py:249
  65.8 9.3 %collective-permute-start.5 = (bf16[128,1024]{1,0:T(8,128)(2,1)S(1)}, bf16[128,1024]{1,0:T(8,128)(2,1)}, u32[]{:S(2)}, u32[]{:S(2)}) collective-permute-start(bf16[128,1024]{1,0:T(8,128)(2,1)S(1)} %get-tuple-element.100), channel_id=1, source_target_pairs={{0,16},{4,20},{8,24},{12,28},{16,0},{20,4},{24,8},{28,12},{1,17},{... | collective-permute-start | bytes 786440 | tf_op jit(solution)/shard_map/cond/branch_1_fun/ppermute | solution.py:249
  66.7 13.8 %collective-permute-start.6 = (bf16[128,1024]{1,0:T(8,128)(2,1)S(1)}, bf16[128,1024]{1,0:T(8,128)(2,1)}, u32[]{:S(2)}, u32[]{:S(2)}) collective-permute-start(bf16[128,1024]{1,0:T(8,128)(2,1)S(1)} %get-tuple-element.99), channel_id=1, source_target_pairs={{0,8},{4,12},{8,0},{12,4},{16,24},{20,28},{24,16},{28,20},{1,9},{5... | collective-permute-start | bytes 786440 | tf_op jit(solution)/shard_map/cond/branch_1_fun/ppermute | solution.py:249
  68.2 12.3 %collective-permute-start.7 = (bf16[128,1024]{1,0:T(8,128)(2,1)S(1)}, bf16[128,1024]{1,0:T(8,128)(2,1)}, u32[]{:S(2)}, u32[]{:S(2)}) collective-permute-start(bf16[128,1024]{1,0:T(8,128)(2,1)S(1)} %get-tuple-element.98), channel_id=1, source_target_pairs={{0,24},{4,28},{8,16},{12,20},{16,8},{20,12},{24,0},{28,4},{1,25},{... | collective-permute-start | bytes 786440 | tf_op jit(solution)/shard_map/cond/branch_1_fun/ppermute | solution.py:249
  80.5 1.5 %copy-start.3 = (bf16[512,1024]{1,0:T(8,128)(2,1)S(1)}, bf16[512,1024]{1,0:T(8,128)(2,1)}, u32[]{:S(2)}) copy-start(bf16[512,1024]{1,0:T(8,128)(2,1)} %get-tuple-element.73.far_hbm) | copy-start | bytes 3145732
  82.8 2.0 %collective-permute-start.12 = (bf16[4,128,512]{2,1,0:T(8,128)(2,1)S(1)}, bf16[4,128,512]{2,1,0:T(8,128)(2,1)S(1)}, u32[]{:S(2)}, u32[]{:S(2)}) collective-permute-start(bf16[4,128,512]{2,1,0:T(8,128)(2,1)S(1)} %bitcast.31), channel_id=1, source_target_pairs={{0,4},{4,0},{8,12},{12,8},{16,20},{20,16},{24,28},{28,24},{1,5},{5... | collective-permute-start | bytes 1572872 | tf_op jit(solution)/shard_map/ppermute | solution.py:249
  85.0 7.8 %collective-permute-start.13 = (bf16[128,512]{1,0:T(8,128)(2,1)S(1)}, bf16[128,512]{1,0:T(8,128)(2,1)S(1)}, u32[]{:S(2)}, u32[]{:S(2)}) collective-permute-start(bf16[128,512]{1,0:T(8,128)(2,1)S(1)} %get-tuple-element.104), channel_id=1, source_target_pairs={{0,16},{4,20},{8,24},{12,28},{16,0},{20,4},{24,8},{28,12},{1,17},{... | collective-permute-start | bytes 393224 | tf_op jit(solution)/shard_map/ppermute | solution.py:249
  86.2 6.6 %collective-permute-start.14 = (bf16[128,512]{1,0:T(8,128)(2,1)S(1)}, bf16[128,512]{1,0:T(8,128)(2,1)S(1)}, u32[]{:S(2)}, u32[]{:S(2)}) collective-permute-start(bf16[128,512]{1,0:T(8,128)(2,1)S(1)} %get-tuple-element.103), channel_id=1, source_target_pairs={{0,8},{4,12},{8,0},{12,4},{16,24},{20,28},{24,16},{28,20},{1,9},{5... | collective-permute-start | bytes 393224 | tf_op jit(solution)/shard_map/ppermute | solution.py:249
  87.1 7.2 %collective-permute-start.15 = (bf16[128,512]{1,0:T(8,128)(2,1)S(1)}, bf16[128,512]{1,0:T(8,128)(2,1)S(1)}, u32[]{:S(2)}, u32[]{:S(2)}) collective-permute-start(bf16[128,512]{1,0:T(8,128)(2,1)S(1)} %get-tuple-element.102), channel_id=1, source_target_pairs={{0,24},{4,28},{8,16},{12,20},{16,8},{20,12},{24,0},{28,4},{1,25},{... | collective-permute-start | bytes 393224 | tf_op jit(solution)/shard_map/ppermute | solution.py:249

commit v5 on v4

--- a/solution.py
+++ b/solution.py
@@ -29,40 +29,60 @@
     return pltpu.CompilerParams(vmem_limit_bytes=24 * 1024 * 1024)
 
 
-def norm_kernel(tokens_ref, gain_ref, out_ref, *, row_count, pair_count, part):
-    step = 32
-    blocks = [(d * row_count + r, r * pair_count + d) for r in range(row_count) for d in range(pair_count)]
-    count = len(blocks) * part
-
-    @pl.loop(0, tokens_ref.shape[0], step=step)
-    def _(at):
-        rows = pl.ds(pl.multiple_of(at, step), step)
+def norm_kernel(tokens_hbm, gain_hbm, out_ref, tokens, gain, sems, *, row_count, pair_count, part):
+    step = sems_step(tokens_hbm.shape[0])
+    blocks = [
+        (d * row_count + r, r * pair_count + d)
+        for r in range(row_count)
+        for d in range(pair_count)
+    ]
+    copies = [pltpu.make_async_copy(gain_hbm, gain, sems.at[0])]
+    for i in range(tokens_hbm.shape[0] // step):
+        rows = pl.ds(i * step, step)
+        copies.append(
+            pltpu.make_async_copy(tokens_hbm.at[rows], tokens.at[rows], sems.at[1 + i])
+        )
+    for copy in copies:
+        copy.start()
+    copies[0].wait()
+    for i, copy in enumerate(copies[1:]):
+        copy.wait()
+        rows = pl.ds(i * step, step)
 
         def piece(k):
-            return tokens_ref[rows, k * part : (k + 1) * part].astype(jnp.float32)
+            return tokens[rows, k * part : (k + 1) * part].astype(jnp.float32)
 
         squares = jnp.zeros((step, 128), jnp.float32)
         for _, k in blocks:
             square = piece(k) * piece(k)
             for j in range(0, part, 128):
                 squares = squares + square[:, j : j + 128]
-        mean = jnp.sum(squares, axis=1, keepdims=True) / count
+        mean = jnp.sum(squares, axis=1, keepdims=True) / (len(blocks) * part)
         inverse_rms = lax.rsqrt(mean + 1e-05)
         for place, k in blocks:
-            gain = gain_ref[:, k * part : (k + 1) * part]
-            out_ref[place, rows, :] = (piece(k) * inverse_rms * gain).astype(jnp.bfloat16)
+            scaled = piece(k) * inverse_rms * gain[:, k * part : (k + 1) * part]
+            out_ref[place, rows, :] = scaled.astype(jnp.bfloat16)
+
+
+def sems_step(rows):
+    return min(32, rows)
 
 
 def normalise(tokens, norm_gain, row_count, pair_count, part):
-    rows = tokens.shape[0]
-    vmem = pl.BlockSpec(memory_space=pltpu.VMEM)
+    rows, features = tokens.shape
+    anywhere = pl.BlockSpec(memory_space=pl.ANY)
     return pl.pallas_call(
         functools.partial(
             norm_kernel, row_count=row_count, pair_count=pair_count, part=part
         ),
-        in_specs=[vmem, vmem],
-        out_specs=vmem,
+        in_specs=[anywhere, anywhere],
+        out_specs=pl.BlockSpec(memory_space=pltpu.VMEM),
         out_shape=pltpu.VMEM((row_count * pair_count, rows, part), jnp.bfloat16),
+        scratch_shapes=[
+            pltpu.VMEM((rows, features), jnp.bfloat16),
+            pltpu.VMEM((1, features), jnp.float32),
+            pltpu.SemaphoreType.DMA((1 + rows // sems_step(rows),)),
+        ],
         compiler_params=params(),
         name="norm",
     )(tokens, norm_gain[None, :])
@@ -161,7 +181,7 @@
             pltpu.VMEM((count, part, n), jnp.bfloat16),
             pltpu.SemaphoreType.DMA((2 + count,)),
         ],
-        compiler_params=pltpu.CompilerParams(vmem_limit_bytes=24 * 1024 * 1024),
+        compiler_params=pltpu.CompilerParams(vmem_limit_bytes=58 * 1024 * 1024),
         name="project_both",
     )(near, far, *blocks)
 
@@ -276,9 +296,8 @@
     slot1 = exchange(own, 1)
     chips = [(r, d) for r in range(0, row_count, 2) for d in range(pair_count)]
     (tokens, own) = lax.optimization_barrier((tokens, own))
-    parts = normalise(tokens, norm_gain, row_count, pair_count, part)
-
-    def spread(parts):
+    def spread(tokens):
+        parts = normalise(tokens, norm_gain, row_count, pair_count, part)
         groups = [
             [(g * pair_count + d) * row_count + r for d in range(pair_count) for r in range(row_count)]
             for g in range(dp_count // pair_count)
@@ -292,7 +311,7 @@
             axis_index_groups=groups if len(groups) > 1 else None,
         )
 
-    tile = stage(spread, parts)
+    tile = stage(spread, tokens)
 
     shape = (len(chips), own_rows, -1)
 

time: 96 us -> 93.4 us (0.973)
  the two profiles are of different devices: /device:TPU:0 before, /device:TPU:8 now
where the time goes in v5:
time: 93.4 us; the launch traced here: 93.1 us
  blocking collectives  29.5 us (32%)
  waiting for transfers between devices  24.7 us (26%)
  starting transfers between devices  18.6 us (20%)
  Pallas kernels  13.8 us (15%)
  local copies, waits for them, and re-layouts  2.73 us (3%)
  matrix products  1.42 us (2%)
  other arithmetic  1.4 us (1%)
    all_to_all x1, blocking collectives, spread(): lax.all_to_all(parts, ('dp', 'row'), split_axis=0, concat_axis=0, tiled=T...  29.5 us
    ppermute x12, waiting for transfers between devices, swap(): return lax.ppermute(array, ('dp', 'row'), pairs)  24.5 us
    ppermute x12, starting transfers between devices, swap(): return lax.ppermute(array, ('dp', 'row'), pairs)  10.9 us
    ppermute x4, starting transfers between devices, exchange(): lax.ppermute(array, 'col', [(i, i ^ bits) for i in range(col_count) if i...  7.75 us
    pallas_call x3, Pallas kernels, finish(): pl.pallas_call(functools.partial(sum_kernel, terms=1 + len(others), slots...  5.16 us
    pallas_call x1, Pallas kernels, project_both(): pl.pallas_call(functools.partial(pair_kernel, count=count), in_specs=[pl....  4.25 us
    pallas_call x1, Pallas kernels, project_own(): pl.pallas_call(functools.partial(own_kernel, pair_count=pair_count, row_c...  2.2 us
    pallas_call x1, Pallas kernels, normalise(): pl.pallas_call(functools.partial(norm_kernel, row_count=row_count, pair_c...  2.2 us
  transfers between devices with their start and end apart: 16, of which 10 were waited for; matrix products, arithmetic and copies ran while one was open for 2% of the time, Pallas kernels for 13%

profile of v5, /device:TPU:8, one launch (start us, length us, event | category | flops | bytes accessed | tf_op | source)
XLA Modules:
  0.0 93.1 jit_solution(4259019741330620979)
XLA Ops:
  0.7 1.3 %constant_dynamic-slice_fusion = (bf16[1024,256]{1,0:T(8,128)(2,1)S(1)}, bf16[1024,256]{1,0:T(8,128)(2,1)S(1)}) fusion(bf16[2048,256]{1,0:T(8,128)(2,1)} %param.13, s32[]{:T(128)S(6)} %select_n.30, bf16[2048,256]{1,0:T(8,128)(2,1)} %param.12), kind=kLoop, calls=%fused_computation.23 | loop fusion | bytes 2097156 | tf_op jit(solution)/shard_map/dynamic_slice | solution.py:293
  1.9 0.1 pad_maximum_fusion.weights_ref
  2.0 2.7 %collective-permute-start.8 = (bf16[1024,512]{1,0:T(8,128)(2,1)S(1)}, bf16[1024,512]{1,0:T(8,128)(2,1)}, u32[]{:S(2)}, u32[]{:S(2)}) collective-permute-start(bf16[1024,512]{1,0:T(8,128)(2,1)S(1)} %pad_maximum_fusion.weights_ref), channel_id=1, source_target_pairs={{0,2},{1,3},{2,0},{3,1},{4,6},{5,7},{6,4},{7,5},{8,10},{9,11},{10,... | collective-permute-start | bytes 3145736 | tf_op jit(solution)/shard_map/ppermute | solution.py:272
  4.7 0.4 collective-permute-start.9
  5.1 31.7 %conditional.3 = (bf16[8,128,1024]{2,1,0:T(8,128)(2,1)S(1)}) conditional(s32[]{:T(128)} %convert_element_type.42, () %tuple.32, (f32[8192]{0:T(1024)S(1)}, bf16[128,8192]{1,0:T(8,128)(2,1)}) %tuple.59), branch_computations={%region_0.1_spmd, %region_1.2_spmd} | conditional | bytes 4194312 | solution.py:289
  5.1 2.2 %norm.1 = bf16[8,128,1024]{2,1,0:T(8,128)(2,1)S(1)} custom-call(bf16[128,8192]{1,0:T(8,128)(2,1)} %get-tuple-element.13.tokens_hbm, f32[1,8192]{1,0:T(1,128)S(1)} %bitcast.30), custom_call_target="tpu_custom_call" | custom-call | tf_op jit(solution)/shard_map/cond/branch_1_fun/norm/pallas_call | solution.py:74
  7.3 29.5 %all_to_all.4 = bf16[8,128,1024]{2,1,0:T(8,128)(2,1)S(1)} all-to-all(bf16[8,128,1024]{2,1,0:T(8,128)(2,1)S(1)} %norm.1), channel_id=1, replica_groups=mesh['dp'=2,'row'=4,'col'=4] {'dp','row'}, dimensions={0} | all-to-all | bytes 4194304 | tf_op jit(solution)/shard_map/cond/branch_1_fun/all_to_all | solution.py:305
  36.9 0.1 pad_add_fusion.place_ref
  36.9 2.2 %project_own.1 = (bf16[512,1024]{1,0:T(8,128)(2,1)}, bf16[512,1024]{1,0:T(8,128)(2,1)}, bf16[4,128,512]{2,1,0:T(8,128)(2,1)S(1)}, bf16[4,128,512]{2,1,0:T(8,128)(2,1)S(1)}) custom-call(s32[4]{0:T(128)S(1)} %pad_add_fusion.place_ref, bf16[8,128,1024]{2,1,0:T(8,128)(2,1)S(1)} %get-tuple-element.135.tile_ref, bf16[1024,512]{1,0:T(8,128)(2,1)S(1)} %pad_maximum_fusion.weights_ref), custom_call_target="tpu_custom_call" | custom-call | tf_op jit(solution)/shard_map/project_own/pallas_call | solution.py:121
  39.1 11.6 %conditional.4 = (bf16[1,128,512]{2,1,0:T(8,128)(2,1)S(1)}, bf16[128,512]{1,0:T(8,128)(2,1)}, bf16[128,512]{1,0:T(8,128)(2,1)}, bf16[128,512]{1,0:T(8,128)(2,1)}) conditional(s32[]{:T(128)} %convert_element_type.42, () %tuple.36, (bf16[4,128,512]{2,1,0:T(8,128)(2,1)S(1)}, bf16[4,128,512]{2,1,0:T(8,128)(2,1)S(1)}) %tuple.37), branch_computations={%region_2.3_spmd, %region_3.4_spmd} | conditional | flops 1048576 | bytes 6291648 | solution.py:289
  39.2 1.9 %collective-permute-done = bf16[4,128,512]{2,1,0:T(8,128)(2,1)S(1)} collective-permute-done((bf16[4,128,512]{2,1,0:T(8,128)(2,1)S(1)}, bf16[4,128,512]{2,1,0:T(8,128)(2,1)S(1)}, u32[]{:S(2)}, u32[]{:S(2)}) %collective-permute-start) | collective-permute-done | bytes 524320 | tf_op jit(solution)/shard_map/cond/branch_1_fun/ppermute | solution.py:269
  41.1 0.1 add_convert_fusion
  41.3 1.2 %collective-permute-start.1 = (bf16[128,512]{1,0:T(8,128)(2,1)S(1)}, bf16[128,512]{1,0:T(8,128)(2,1)}, u32[]{:S(2)}, u32[]{:S(2)}) collective-permute-start(bf16[128,512]{1,0:T(8,128)(2,1)S(1)} %get-tuple-element.103), channel_id=1, source_target_pairs={{0,16},{4,20},{8,24},{12,28},{16,0},{20,4},{24,8},{28,12},{1,17},{... | collective-permute-start | bytes 393224 | tf_op jit(solution)/shard_map/cond/branch_1_fun/ppermute | solution.py:269
  42.5 0.9 collective-permute-start.2
  43.5 1.4 %collective-permute-start.3 = (bf16[128,512]{1,0:T(8,128)(2,1)S(1)}, bf16[128,512]{1,0:T(8,128)(2,1)}, u32[]{:S(2)}, u32[]{:S(2)}) collective-permute-start(bf16[128,512]{1,0:T(8,128)(2,1)S(1)} %get-tuple-element.101), channel_id=1, source_target_pairs={{0,24},{4,28},{8,16},{12,20},{16,8},{20,12},{24,0},{28,4},{1,25},{... | collective-permute-start | bytes 393224 | tf_op jit(solution)/shard_map/cond/branch_1_fun/ppermute | solution.py:269
  44.9 2.9 %collective-permute-done.1 = bf16[128,512]{1,0:T(8,128)(2,1)} collective-permute-done((bf16[128,512]{1,0:T(8,128)(2,1)S(1)}, bf16[128,512]{1,0:T(8,128)(2,1)}, u32[]{:S(2)}, u32[]{:S(2)}) %collective-permute-start.1) | collective-permute-done | bytes 131104 | tf_op jit(solution)/shard_map/cond/branch_1_fun/ppermute | solution.py:269
  47.7 1.3 %collective-permute-done.2 = bf16[128,512]{1,0:T(8,128)(2,1)} collective-permute-done((bf16[128,512]{1,0:T(8,128)(2,1)S(1)}, bf16[128,512]{1,0:T(8,128)(2,1)}, u32[]{:S(2)}, u32[]{:S(2)}) %collective-permute-start.2) | collective-permute-done | bytes 131104 | tf_op jit(solution)/shard_map/cond/branch_1_fun/ppermute | solution.py:269
  49.1 1.7 %collective-permute-done.3 = bf16[128,512]{1,0:T(8,128)(2,1)} collective-permute-done((bf16[128,512]{1,0:T(8,128)(2,1)S(1)}, bf16[128,512]{1,0:T(8,128)(2,1)}, u32[]{:S(2)}, u32[]{:S(2)}) %collective-permute-start.3) | collective-permute-done | bytes 131104 | tf_op jit(solution)/shard_map/cond/branch_1_fun/ppermute | solution.py:269
  50.7 1.6 %collective-permute-start.10 = (bf16[1024,512]{1,0:T(8,128)(2,1)}, bf16[1024,512]{1,0:T(8,128)(2,1)S(1)}, u32[]{:S(2)}, u32[]{:S(2)}) collective-permute-start(bf16[1024,512]{1,0:T(8,128)(2,1)} %collective-permute-done.8.refs_1_), channel_id=1, source_target_pairs={{0,1},{1,0},{2,3},{3,2},{4,5},{5,4},{6,7},{7,6},{8,9},{9,8},{10,11... | collective-permute-start | bytes 3145736 | tf_op jit(solution)/shard_map/ppermute | solution.py:272
  52.3 3.1 %collective-permute-start.11 = (bf16[1024,512]{1,0:T(8,128)(2,1)S(1)}, bf16[1024,512]{1,0:T(8,128)(2,1)S(1)}, u32[]{:S(2)}, u32[]{:S(2)}) collective-permute-start(bf16[1024,512]{1,0:T(8,128)(2,1)S(1)} %pad_maximum_fusion.weights_ref), channel_id=1, source_target_pairs={{1,2},{2,1},{5,6},{6,5},{9,10},{10,9},{13,14},{14,13},{17,18},{18,... | collective-permute-start | bytes 3145736 | tf_op jit(solution)/shard_map/ppermute | solution.py:272
  55.4 4.2 %project_both.1 = (bf16[4,128,1024]{2,1,0:T(8,128)(2,1)S(1)}, bf16[4,128,1024]{2,1,0:T(8,128)(2,1)S(1)}) custom-call(bf16[512,1024]{1,0:T(8,128)(2,1)} %get-tuple-element.73.near_hbm, bf16[512,1024]{1,0:T(8,128)(2,1)} %get-tuple-element.78.far_hbm, bf16[1024,512]{1,0:T(8,128)(2,1)} %collective-permute-done.9.refs_0_, ...), custom_call_target="tpu_custom_call" | custom-call | tf_op jit(solution)/shard_map/project_both/pallas_call | solution.py:173
  59.7 18.6 %conditional.5 = (bf16[1,128,1024]{2,1,0:T(8,128)(2,1)S(1)}, bf16[128,1024]{1,0:T(8,128)(2,1)}, bf16[128,1024]{1,0:T(8,128)(2,1)}, bf16[128,1024]{1,0:T(8,128)(2,1)}) conditional(s32[]{:T(128)} %convert_element_type.42, () %tuple.39, (bf16[4,128,1024]{2,1,0:T(8,128)(2,1)S(1)}, bf16[4,128,1024]{2,1,0:T(8,128)(2,1)S(1)}) %project_both.1), branch_computations={%region_4.5_spmd, %region_5.6_spmd} | conditional | flops 2097152 | bytes 12583104 | solution.py:289
  59.8 2.6 %collective-permute-done.4 = bf16[4,128,1024]{2,1,0:T(8,128)(2,1)S(1)} collective-permute-done((bf16[4,128,1024]{2,1,0:T(8,128)(2,1)S(1)}, bf16[4,128,1024]{2,1,0:T(8,128)(2,1)S(1)}, u32[]{:S(2)}, u32[]{:S(2)}) %collective-permute-start.4) | collective-permute-done | bytes 1048608 | tf_op jit(solution)/shard_map/cond/branch_1_fun/ppermute | solution.py:269
  62.4 0.4 add_convert_fusion.1
  62.8 0.1 slice_bitcast_fusion.3
  62.9 1.6 %collective-permute-start.5 = (bf16[128,1024]{1,0:T(8,128)(2,1)S(1)}, bf16[128,1024]{1,0:T(8,128)(2,1)}, u32[]{:S(2)}, u32[]{:S(2)}) collective-permute-start(bf16[128,1024]{1,0:T(8,128)(2,1)S(1)} %get-tuple-element.107), channel_id=1, source_target_pairs={{0,16},{4,20},{8,24},{12,28},{16,0},{20,4},{24,8},{28,12},{1,17},{... | collective-permute-start | bytes 786440 | tf_op jit(solution)/shard_map/cond/branch_1_fun/ppermute | solution.py:269
  64.5 1.5 %collective-permute-start.6 = (bf16[128,1024]{1,0:T(8,128)(2,1)S(1)}, bf16[128,1024]{1,0:T(8,128)(2,1)}, u32[]{:S(2)}, u32[]{:S(2)}) collective-permute-start(bf16[128,1024]{1,0:T(8,128)(2,1)S(1)} %get-tuple-element.106), channel_id=1, source_target_pairs={{0,8},{4,12},{8,0},{12,4},{16,24},{20,28},{24,16},{28,20},{1,9},{5... | collective-permute-start | bytes 786440 | tf_op jit(solution)/shard_map/cond/branch_1_fun/ppermute | solution.py:269
  66.0 0.5 collective-permute-start.7
  66.5 5.8 %collective-permute-done.5 = bf16[128,1024]{1,0:T(8,128)(2,1)} collective-permute-done((bf16[128,1024]{1,0:T(8,128)(2,1)S(1)}, bf16[128,1024]{1,0:T(8,128)(2,1)}, u32[]{:S(2)}, u32[]{:S(2)}) %collective-permute-start.5) | collective-permute-done | bytes 262176 | tf_op jit(solution)/shard_map/cond/branch_1_fun/ppermute | solution.py:269
  72.2 6.0 %collective-permute-done.6 = bf16[128,1024]{1,0:T(8,128)(2,1)} collective-permute-done((bf16[128,1024]{1,0:T(8,128)(2,1)S(1)}, bf16[128,1024]{1,0:T(8,128)(2,1)}, u32[]{:S(2)}, u32[]{:S(2)}) %collective-permute-start.6) | collective-permute-done | bytes 262176 | tf_op jit(solution)/shard_map/cond/branch_1_fun/ppermute | solution.py:269
  78.3 0.2 collective-permute-done.11
  78.4 0.1 broadcast_select_fusion
  78.6 0.9 copy-done.1
  79.5 0.7 convolution_convert_fusion
  80.2 0.1 collective-permute-start.12
  80.3 0.4 copy-done
  80.7 0.7 fusion.1
  81.4 0.7 collective-permute-done.12
  82.2 0.2 add_convert_fusion.2.refs_0_
  82.4 1.3 %collective-permute-start.13 = (bf16[128,512]{1,0:T(8,128)(2,1)S(1)}, bf16[128,512]{1,0:T(8,128)(2,1)S(1)}, u32[]{:S(2)}, u32[]{:S(2)}) collective-permute-start(bf16[128,512]{1,0:T(8,128)(2,1)S(1)} %get-tuple-element.111), channel_id=1, source_target_pairs={{0,16},{4,20},{8,24},{12,28},{16,0},{20,4},{24,8},{28,12},{1,17},{... | collective-permute-start | bytes 393224 | tf_op jit(solution)/shard_map/ppermute | solution.py:269
  83.7 0.9 collective-permute-start.14
  84.6 1.4 %collective-permute-start.15 = (bf16[128,512]{1,0:T(8,128)(2,1)S(1)}, bf16[128,512]{1,0:T(8,128)(2,1)S(1)}, u32[]{:S(2)}, u32[]{:S(2)}) collective-permute-start(bf16[128,512]{1,0:T(8,128)(2,1)S(1)} %get-tuple-element.109), channel_id=1, source_target_pairs={{0,24},{4,28},{8,16},{12,20},{16,8},{20,12},{24,0},{28,4},{1,25},{... | collective-permute-start | bytes 393224 | tf_op jit(solution)/shard_map/ppermute | solution.py:269
  85.9 0.3 fusion
  86.2 0.1 pad_maximum_fusion.1
  86.3 1.8 %finish.3 = (bf16[128,1024]{1,0:T(8,128)(2,1)}, bf16[128,1024]{1,0:T(8,128)(2,1)}) custom-call(s32[4]{0:T(128)S(1)} %pad_add_fusion.place_ref, bf16[1,128,512]{2,1,0:T(8,128)(2,1)S(1)} %get-tuple-element.91.refs_0_, bf16[128,512]{1,0:T(8,128)(2,1)} %get-tuple-element.92.refs_1_, bf16[128,512]{1,0:T(8,128)(2,1)} %get-tuple-element.93.refs_2_, ...), custom_call_target="tpu_custom_call" | custom-call | tf_op jit(solution)/shard_map/finish/pallas_call | solution.py:225
  88.2 2.0 %finish.4 = (bf16[128,1024]{1,0:T(8,128)(2,1)}, bf16[128,1024]{1,0:T(8,128)(2,1)}) custom-call(s32[4]{0:T(128)S(1)} %pad_add_fusion.place_ref, bf16[1,128,1024]{2,1,0:T(8,128)(2,1)S(1)} %get-tuple-element.87.refs_0_, bf16[128,1024]{1,0:T(8,128)(2,1)} %get-tuple-element.88.refs_1_, ...), custom_call_target="tpu_custom_call", output_to_operand_aliasing={{0}: (7, {}), {1}: (8, {})} | custom-call | tf_op jit(solution)/shard_map/finish/pallas_call | solution.py:225
  90.2 1.5 %collective-permute-done.15.refs_3_ = bf16[128,512]{1,0:T(8,128)(2,1)S(1)} collective-permute-done((bf16[128,512]{1,0:T(8,128)(2,1)S(1)}, bf16[128,512]{1,0:T(8,128)(2,1)S(1)}, u32[]{:S(2)}, u32[]{:S(2)}) %collective-permute-start.15) | collective-permute-done | bytes 131104 | tf_op jit(solution)/shard_map/ppermute | solution.py:269
  91.7 1.3 %finish.5 = (bf16[128,1024]{1,0:T(8,128)(2,1)}, bf16[128,1024]{1,0:T(8,128)(2,1)}) custom-call(s32[4]{0:T(128)S(1)} %pad_add_fusion.place_ref, bf16[4,128,512]{2,1,0:T(8,128)(2,1)S(1)} %add_convert_fusion.2.refs_0_, bf16[128,512]{1,0:T(8,128)(2,1)S(1)} %collective-permute-done.13.refs_1_, ...), custom_call_target="tpu_custom_call", output_to_operand_aliasing={{0}: (7, {}), {1}: (8, {})} | custom-call | tf_op jit(solution)/shard_map/finish/pallas_call | solution.py:225
  (16 shorter events, 0.2 us)
Async XLA Ops:
  0.6 4.5 %copy-start.2 = (f32[8192]{0:T(1024)S(1)}, f32[8192]{0:T(1024)}, u32[]{:S(2)}) copy-start(f32[8192]{0:T(1024)} %param.11) | copy-start | bytes 98308
  2.0 48.7 %collective-permute-start.8 = (bf16[1024,512]{1,0:T(8,128)(2,1)S(1)}, bf16[1024,512]{1,0:T(8,128)(2,1)}, u32[]{:S(2)}, u32[]{:S(2)}) collective-permute-start(bf16[1024,512]{1,0:T(8,128)(2,1)S(1)} %pad_maximum_fusion.weights_ref), channel_id=1, source_target_pairs={{0,2},{1,3},{2,0},{3,1},{4,6},{5,7},{6,4},{7,5},{8,10},{9,11},{10,... | collective-permute-start | bytes 3145736 | tf_op jit(solution)/shard_map/ppermute | solution.py:272
  4.7 50.7 %collective-permute-start.9 = (bf16[1024,512]{1,0:T(8,128)(2,1)S(1)}, bf16[1024,512]{1,0:T(8,128)(2,1)}, u32[]{:S(2)}, u32[]{:S(2)}) collective-permute-start(bf16[1024,512]{1,0:T(8,128)(2,1)S(1)} %pad_maximum_fusion.weights_ref), channel_id=1, source_target_pairs={{0,1},{1,0},{2,3},{3,2},{4,5},{5,4},{6,7},{7,6},{8,9},{9,8},{10,11... | collective-permute-start | bytes 3145736 | tf_op jit(solution)/shard_map/ppermute | solution.py:272
  39.2 2.0 %collective-permute-start = (bf16[4,128,512]{2,1,0:T(8,128)(2,1)S(1)}, bf16[4,128,512]{2,1,0:T(8,128)(2,1)S(1)}, u32[]{:S(2)}, u32[]{:S(2)}) collective-permute-start(bf16[4,128,512]{2,1,0:T(8,128)(2,1)S(1)} %get-tuple-element.18), channel_id=1, source_target_pairs={{0,4},{4,0},{8,12},{12,8},{16,20},{20,16},{24,28},{28,24},{1,5},{5... | collective-permute-start | bytes 1572872 | tf_op jit(solution)/shard_map/cond/branch_1_fun/ppermute | solution.py:269
  41.3 6.4 %collective-permute-start.1 = (bf16[128,512]{1,0:T(8,128)(2,1)S(1)}, bf16[128,512]{1,0:T(8,128)(2,1)}, u32[]{:S(2)}, u32[]{:S(2)}) collective-permute-start(bf16[128,512]{1,0:T(8,128)(2,1)S(1)} %get-tuple-element.103), channel_id=1, source_target_pairs={{0,16},{4,20},{8,24},{12,28},{16,0},{20,4},{24,8},{28,12},{1,17},{... | collective-permute-start | bytes 393224 | tf_op jit(solution)/shard_map/cond/branch_1_fun/ppermute | solution.py:269
  42.5 6.5 %collective-permute-start.2 = (bf16[128,512]{1,0:T(8,128)(2,1)S(1)}, bf16[128,512]{1,0:T(8,128)(2,1)}, u32[]{:S(2)}, u32[]{:S(2)}) collective-permute-start(bf16[128,512]{1,0:T(8,128)(2,1)S(1)} %get-tuple-element.102), channel_id=1, source_target_pairs={{0,8},{4,12},{8,0},{12,4},{16,24},{20,28},{24,16},{28,20},{1,9},{5... | collective-permute-start | bytes 393224 | tf_op jit(solution)/shard_map/cond/branch_1_fun/ppermute | solution.py:269
  43.5 7.3 %collective-permute-start.3 = (bf16[128,512]{1,0:T(8,128)(2,1)S(1)}, bf16[128,512]{1,0:T(8,128)(2,1)}, u32[]{:S(2)}, u32[]{:S(2)}) collective-permute-start(bf16[128,512]{1,0:T(8,128)(2,1)S(1)} %get-tuple-element.101), channel_id=1, source_target_pairs={{0,24},{4,28},{8,16},{12,20},{16,8},{20,12},{24,0},{28,4},{1,25},{... | collective-permute-start | bytes 393224 | tf_op jit(solution)/shard_map/cond/branch_1_fun/ppermute | solution.py:269
  50.7 27.5 %collective-permute-start.10 = (bf16[1024,512]{1,0:T(8,128)(2,1)}, bf16[1024,512]{1,0:T(8,128)(2,1)S(1)}, u32[]{:S(2)}, u32[]{:S(2)}) collective-permute-start(bf16[1024,512]{1,0:T(8,128)(2,1)} %collective-permute-done.8.refs_1_), channel_id=1, source_target_pairs={{0,1},{1,0},{2,3},{3,2},{4,5},{5,4},{6,7},{7,6},{8,9},{9,8},{10,11... | collective-permute-start | bytes 3145736 | tf_op jit(solution)/shard_map/ppermute | solution.py:272
  52.3 26.1 %collective-permute-start.11 = (bf16[1024,512]{1,0:T(8,128)(2,1)S(1)}, bf16[1024,512]{1,0:T(8,128)(2,1)S(1)}, u32[]{:S(2)}, u32[]{:S(2)}) collective-permute-start(bf16[1024,512]{1,0:T(8,128)(2,1)S(1)} %pad_maximum_fusion.weights_ref), channel_id=1, source_target_pairs={{1,2},{2,1},{5,6},{6,5},{9,10},{10,9},{13,14},{14,13},{17,18},{18,... | collective-permute-start | bytes 3145736 | tf_op jit(solution)/shard_map/ppermute | solution.py:272
  59.7 2.7 %collective-permute-start.4 = (bf16[4,128,1024]{2,1,0:T(8,128)(2,1)S(1)}, bf16[4,128,1024]{2,1,0:T(8,128)(2,1)S(1)}, u32[]{:S(2)}, u32[]{:S(2)}) collective-permute-start(bf16[4,128,1024]{2,1,0:T(8,128)(2,1)S(1)} %get-tuple-element.20), channel_id=1, source_target_pairs={{0,4},{4,0},{8,12},{12,8},{16,20},{20,16},{24,28},{28,24},{1,5},{5... | collective-permute-start | bytes 3145736 | tf_op jit(solution)/shard_map/cond/branch_1_fun/ppermute | solution.py:269
  62.9 9.3 %collective-permute-start.5 = (bf16[128,1024]{1,0:T(8,128)(2,1)S(1)}, bf16[128,1024]{1,0:T(8,128)(2,1)}, u32[]{:S(2)}, u32[]{:S(2)}) collective-permute-start(bf16[128,1024]{1,0:T(8,128)(2,1)S(1)} %get-tuple-element.107), channel_id=1, source_target_pairs={{0,16},{4,20},{8,24},{12,28},{16,0},{20,4},{24,8},{28,12},{1,17},{... | collective-permute-start | bytes 786440 | tf_op jit(solution)/shard_map/cond/branch_1_fun/ppermute | solution.py:269
  64.5 13.8 %collective-permute-start.6 = (bf16[128,1024]{1,0:T(8,128)(2,1)S(1)}, bf16[128,1024]{1,0:T(8,128)(2,1)}, u32[]{:S(2)}, u32[]{:S(2)}) collective-permute-start(bf16[128,1024]{1,0:T(8,128)(2,1)S(1)} %get-tuple-element.106), channel_id=1, source_target_pairs={{0,8},{4,12},{8,0},{12,4},{16,24},{20,28},{24,16},{28,20},{1,9},{5... | collective-permute-start | bytes 786440 | tf_op jit(solution)/shard_map/cond/branch_1_fun/ppermute | solution.py:269
  66.0 12.3 %collective-permute-start.7 = (bf16[128,1024]{1,0:T(8,128)(2,1)S(1)}, bf16[128,1024]{1,0:T(8,128)(2,1)}, u32[]{:S(2)}, u32[]{:S(2)}) collective-permute-start(bf16[128,1024]{1,0:T(8,128)(2,1)S(1)} %get-tuple-element.105), channel_id=1, source_target_pairs={{0,24},{4,28},{8,16},{12,20},{16,8},{20,12},{24,0},{28,4},{1,25},{... | collective-permute-start | bytes 786440 | tf_op jit(solution)/shard_map/cond/branch_1_fun/ppermute | solution.py:269
  78.2 1.2 %copy-start.1 = (bf16[512,1024]{1,0:T(8,128)(2,1)S(1)}, bf16[512,1024]{1,0:T(8,128)(2,1)}, u32[]{:S(2)}) copy-start(bf16[512,1024]{1,0:T(8,128)(2,1)} %get-tuple-element.78.far_hbm) | copy-start | bytes 3145732
  79.5 1.2 %copy-start = (bf16[512,1024]{1,0:T(8,128)(2,1)S(1)}, bf16[512,1024]{1,0:T(8,128)(2,1)}, u32[]{:S(2)}) copy-start(bf16[512,1024]{1,0:T(8,128)(2,1)} %get-tuple-element.73.near_hbm) | copy-start | bytes 3145732
  80.2 2.0 %collective-permute-start.12 = (bf16[4,128,512]{2,1,0:T(8,128)(2,1)S(1)}, bf16[4,128,512]{2,1,0:T(8,128)(2,1)S(1)}, u32[]{:S(2)}, u32[]{:S(2)}) collective-permute-start(bf16[4,128,512]{2,1,0:T(8,128)(2,1)S(1)} %bitcast.31), channel_id=1, source_target_pairs={{0,4},{4,0},{8,12},{12,8},{16,20},{20,16},{24,28},{28,24},{1,5},{5... | collective-permute-start | bytes 1572872 | tf_op jit(solution)/shard_map/ppermute | solution.py:269
  82.4 7.8 %collective-permute-start.13 = (bf16[128,512]{1,0:T(8,128)(2,1)S(1)}, bf16[128,512]{1,0:T(8,128)(2,1)S(1)}, u32[]{:S(2)}, u32[]{:S(2)}) collective-permute-start(bf16[128,512]{1,0:T(8,128)(2,1)S(1)} %get-tuple-element.111), channel_id=1, source_target_pairs={{0,16},{4,20},{8,24},{12,28},{16,0},{20,4},{24,8},{28,12},{1,17},{... | collective-permute-start | bytes 393224 | tf_op jit(solution)/shard_map/ppermute | solution.py:269
  83.7 6.6 %collective-permute-start.14 = (bf16[128,512]{1,0:T(8,128)(2,1)S(1)}, bf16[128,512]{1,0:T(8,128)(2,1)S(1)}, u32[]{:S(2)}, u32[]{:S(2)}) collective-permute-start(bf16[128,512]{1,0:T(8,128)(2,1)S(1)} %get-tuple-element.110), channel_id=1, source_target_pairs={{0,8},{4,12},{8,0},{12,4},{16,24},{20,28},{24,16},{28,20},{1,9},{5... | collective-permute-start | bytes 393224 | tf_op jit(solution)/shard_map/ppermute | solution.py:269
  84.6 7.2 %collective-permute-start.15 = (bf16[128,512]{1,0:T(8,128)(2,1)S(1)}, bf16[128,512]{1,0:T(8,128)(2,1)S(1)}, u32[]{:S(2)}, u32[]{:S(2)}) collective-permute-start(bf16[128,512]{1,0:T(8,128)(2,1)S(1)} %get-tuple-element.109), channel_id=1, source_target_pairs={{0,24},{4,28},{8,16},{12,20},{16,8},{20,12},{24,0},{28,4},{1,25},{... | collective-permute-start | bytes 393224 | tf_op jit(solution)/shard_map/ppermute | solution.py:269

commit v6 on v5

--- a/solution.py
+++ b/solution.py
@@ -30,7 +30,7 @@
 
 
 def norm_kernel(tokens_hbm, gain_hbm, out_ref, tokens, gain, sems, *, row_count, pair_count, part):
-    step = sems_step(tokens_hbm.shape[0])
+    step = norm_step(tokens_hbm.shape[0])
     blocks = [
         (d * row_count + r, r * pair_count + d)
         for r in range(row_count)
@@ -64,7 +64,7 @@
             out_ref[place, rows, :] = scaled.astype(jnp.bfloat16)
 
 
-def sems_step(rows):
+def norm_step(rows):
     return min(32, rows)
 
 
@@ -81,21 +81,21 @@
         scratch_shapes=[
             pltpu.VMEM((rows, features), jnp.bfloat16),
             pltpu.VMEM((1, features), jnp.float32),
-            pltpu.SemaphoreType.DMA((1 + rows // sems_step(rows),)),
+            pltpu.SemaphoreType.DMA((1 + rows // norm_step(rows),)),
         ],
         compiler_params=params(),
         name="norm",
     )(tokens, norm_gain[None, :])
 
 
-def own_kernel(place_ref, tile_ref, weights_ref, near_rows, far_rows, near_ref, far_ref, weights, sems, *, pair_count, row_count):
+def own_kernel(tile_ref, weights_ref, near_rows, far_rows, near_ref, far_ref, weights, sems, *, pair_count, row_count):
     rows = tile_ref.shape[1]
     copies = [pltpu.make_async_copy(weights_ref, weights, sems.at[2, 0])]
     halves = (near_rows, far_rows)
     for odd in (1, 0):
         for k in range(row_count // 2 * pair_count):
-            pair = place_ref[0] ^ (k % pair_count)
-            row = place_ref[1] ^ ((k // pair_count) * 2 + odd)
+            pair = lax.rem(lax.axis_index("dp"), pair_count) ^ (k % pair_count)
+            row = lax.axis_index("row") ^ ((k // pair_count) * 2 + odd)
             copies.append(
                 pltpu.make_async_copy(
                     tile_ref.at[pair * row_count + row],
@@ -112,7 +112,7 @@
         out_ref[...] = product.reshape(out_ref.shape).astype(out_ref.dtype)
 
 
-def project_own(place, tile, weights, pair_count, row_count):
+def project_own(tile, weights, pair_count, row_count):
     count, rows, part = tile.shape
     chips = count // 2
     n = weights.shape[1]
@@ -120,7 +120,7 @@
     half = pltpu.HBM((chips * rows, part), jnp.bfloat16)
     return pl.pallas_call(
         functools.partial(own_kernel, pair_count=pair_count, row_count=row_count),
-        in_specs=[pl.BlockSpec(memory_space=pltpu.SMEM)] + [pl.BlockSpec(memory_space=pl.ANY)] * 2,
+        in_specs=[pl.BlockSpec(memory_space=pl.ANY)] * 2,
         out_specs=[vmem] * 4,
         out_shape=[
             half,
@@ -134,7 +134,7 @@
         ],
         compiler_params=params(),
         name="project_own",
-    )(place, tile, weights)
+    )(tile, weights)
 
 
 def pair_kernel(near_hbm, far_hbm, *refs, count):
@@ -186,7 +186,7 @@
     )(near, far, *blocks)
 
 
-def sum_kernel(place_ref, *refs, terms, slots, kinds, width, held):
+def sum_kernel(*refs, terms, slots, kinds, width, held):
     cosine_ref, sine_ref = refs[terms : terms + 2]
     first_out = terms + 2 + held
     out_refs = refs[first_out : first_out + len(kinds)]
@@ -206,7 +206,7 @@
                     turned.append(head * cosine_ref[...] + other * sine_ref[...])
                 block = jnp.concatenate(turned, axis=1)
             blocks_ref[s, i] = block.astype(jnp.bfloat16)
-            column = pl.multiple_of((place_ref[2] ^ slot) * width, width)
+            column = pl.multiple_of((lax.axis_index("col") ^ slot) * width, width)
             copy = pltpu.make_async_copy(
                 blocks_ref.at[s, i], out_refs[i].at[:, pl.ds(column, width)], sems.at[s, i]
             )
@@ -216,12 +216,11 @@
         copy.wait()
 
 
-def finish(place, both, others, tables, held, slots, kinds, width, columns):
+def finish(both, others, tables, held, slots, kinds, width, columns):
     rows = both.shape[1]
     arrays = [both, *others, *tables]
     vmem = pl.BlockSpec(memory_space=pltpu.VMEM)
-    specs = [pl.BlockSpec(memory_space=pltpu.SMEM)] + [vmem] * len(arrays)
-    specs += [pl.BlockSpec(memory_space=pl.ANY)] * len(held)
+    specs = [vmem] * len(arrays) + [pl.BlockSpec(memory_space=pl.ANY)] * len(held)
     return pl.pallas_call(
         functools.partial(
             sum_kernel,
@@ -238,10 +237,10 @@
             pltpu.VMEM((len(slots), len(kinds), rows, width), jnp.bfloat16),
             pltpu.SemaphoreType.DMA((len(slots), len(kinds))),
         ],
-        input_output_aliases={1 + len(arrays) + i: i for i in range(len(held))},
+        input_output_aliases={len(arrays) + i: i for i in range(len(held))},
         compiler_params=params(),
         name="finish",
-    )(place, *arrays, *held)
+    )(*arrays, *held)
 
 
 def body(tokens, norm_gain, w_key, w_value):
@@ -258,7 +257,6 @@
     pair_index = dp_index % pair_count
     part = block // pair_count
     inner = ((col_index + 1) % 4) // 2
-    place = jnp.stack([pair_index, row_index, col_index, inner]).astype(jnp.int32)
 
     def swap(array, row_bits, pair_bits):
         pairs = []
@@ -334,7 +332,7 @@
 
     def add(both, held, slots, kinds, others=None):
         others = second(both) if others is None else others
-        return finish(place, both, others, tables, held, slots, kinds, width, columns)
+        return finish(both, others, tables, held, slots, kinds, width, columns)
 
     kinds = ("key", "value")
     def both_cores(near_part, far_part):
@@ -342,7 +340,7 @@
         return (near_part.astype(jnp.float32) + other.astype(jnp.float32)).astype(jnp.bfloat16)
 
     (tile, own) = lax.optimization_barrier((tile, own))
-    near, far, near0, far0 = project_own(place, tile, own, pair_count, row_count)
+    near, far, near0, far0 = project_own(tile, own, pair_count, row_count)
 
     def sums(near_part, far_part):
         both = both_cores(near_part, far_part)
@@ -350,11 +348,12 @@
 
     sums0 = stage(sums, near0, far0)
     (near, far, sums0, own, slot2) = lax.optimization_barrier((near, far, sums0, own, slot2))
+    middle = exchange(own, 3, (1, 2))
     outer = exchange(slot2, 1)
-    middle = exchange(own, 3, (1, 2))
     near12, far12 = project_both(near, far, [slot1, slot2], own_rows)
     sums12 = stage(sums, near12, far12)
-    (sums0, sums12, outer, middle) = lax.optimization_barrier((sums0, sums12, outer, middle))
+    (sums0, sums12, middle) = lax.optimization_barrier((sums0, sums12, middle))
+    (outer, middle) = lax.optimization_barrier((outer, middle))
     third = lax.optimization_barrier(jnp.where(inner == 1, middle, outer))
     both3 = first(near, far_parts([third]), [third])[0]
     others3 = second(both3)

time: 93.4 us -> 92.3 us (0.988)
  the two profiles are of different devices: /device:TPU:8 before, /device:TPU:0 now
where the time goes in v6:
time: 92.3 us; the launch traced here: 92 us
  blocking collectives  29.5 us (32%)
  waiting for transfers between devices  24.2 us (26%)
  starting transfers between devices  19.4 us (21%)
  Pallas kernels  12.7 us (14%)
  local copies, waits for them, and re-layouts  2.54 us (3%)
  matrix products  1.42 us (2%)
  other arithmetic  1.31 us (1%)
    all_to_all x1, blocking collectives, spread(): lax.all_to_all(parts, ('dp', 'row'), split_axis=0, concat_axis=0, tiled=T...  29.5 us
    ppermute x12, waiting for transfers between devices, swap(): return lax.ppermute(array, ('dp', 'row'), pairs)  23.8 us
    ppermute x12, starting transfers between devices, swap(): return lax.ppermute(array, ('dp', 'row'), pairs)  10.9 us
    ppermute x4, starting transfers between devices, exchange(): lax.ppermute(array, 'col', [(i, i ^ bits) for i in range(col_count) if i...  8.54 us
    pallas_call x3, Pallas kernels, finish(): pl.pallas_call(functools.partial(sum_kernel, terms=1 + len(others), slots...  4.59 us
    pallas_call x1, Pallas kernels, project_both(): pl.pallas_call(functools.partial(pair_kernel, count=count), in_specs=[pl....  4.24 us
    pallas_call x1, Pallas kernels, normalise(): pl.pallas_call(functools.partial(norm_kernel, row_count=row_count, pair_c...  2.2 us
  transfers between devices with their start and end apart: 16, of which 11 were waited for; matrix products, arithmetic and copies ran while one was open for 2% of the time, Pallas kernels for 13%

profile of v6, /device:TPU:0, one launch (start us, length us, event | category | flops | bytes accessed | tf_op | source)
XLA Modules:
  0.0 92.0 jit_solution(16824478385783059276)
XLA Ops:
  0.7 1.3 %constant_dynamic-slice_fusion = (bf16[1024,256]{1,0:T(8,128)(2,1)S(1)}, bf16[1024,256]{1,0:T(8,128)(2,1)S(1)}) fusion(bf16[2048,256]{1,0:T(8,128)(2,1)} %param.13, s32[]{:T(128)S(6)} %select_n.28, bf16[2048,256]{1,0:T(8,128)(2,1)} %param.12), kind=kLoop, calls=%fused_computation.22 | loop fusion | bytes 2097156 | tf_op jit(solution)/shard_map/dynamic_slice | solution.py:291
  1.9 0.1 pad_maximum_fusion.weights_ref
  2.0 4.1 %collective-permute-start.8 = (bf16[1024,512]{1,0:T(8,128)(2,1)S(1)}, bf16[1024,512]{1,0:T(8,128)(2,1)}, u32[]{:S(2)}, u32[]{:S(2)}) collective-permute-start(bf16[1024,512]{1,0:T(8,128)(2,1)S(1)} %pad_maximum_fusion.weights_ref), channel_id=1, source_target_pairs={{0,2},{1,3},{2,0},{3,1},{4,6},{5,7},{6,4},{7,5},{8,10},{9,11},{10,... | collective-permute-start | bytes 3145736 | tf_op jit(solution)/shard_map/ppermute | solution.py:270
  6.1 1.6 %collective-permute-start.10 = (bf16[1024,512]{1,0:T(8,128)(2,1)S(1)}, bf16[1024,512]{1,0:T(8,128)(2,1)}, u32[]{:S(2)}, u32[]{:S(2)}) collective-permute-start(bf16[1024,512]{1,0:T(8,128)(2,1)S(1)} %pad_maximum_fusion.weights_ref), channel_id=1, source_target_pairs={{0,1},{1,0},{2,3},{3,2},{4,5},{5,4},{6,7},{7,6},{8,9},{9,8},{10,11... | collective-permute-start | bytes 3145736 | tf_op jit(solution)/shard_map/ppermute | solution.py:270
  7.7 31.7 %conditional.3 = (bf16[8,128,1024]{2,1,0:T(8,128)(2,1)S(1)}) conditional(s32[]{:T(128)} %convert_element_type.42, () %tuple.33, (f32[8192]{0:T(1024)S(1)}, bf16[128,8192]{1,0:T(8,128)(2,1)}) %tuple.61), branch_computations={%region_0.1_spmd, %region_1.2_spmd} | conditional | bytes 4194312 | solution.py:287
  7.7 2.2 %norm.1 = bf16[8,128,1024]{2,1,0:T(8,128)(2,1)S(1)} custom-call(bf16[128,8192]{1,0:T(8,128)(2,1)} %get-tuple-element.13.tokens_hbm, f32[1,8192]{1,0:T(1,128)S(1)} %bitcast.26), custom_call_target="tpu_custom_call" | custom-call | tf_op jit(solution)/shard_map/cond/branch_1_fun/norm/pallas_call | solution.py:74
  9.9 29.5 %all_to_all.4 = bf16[8,128,1024]{2,1,0:T(8,128)(2,1)S(1)} all-to-all(bf16[8,128,1024]{2,1,0:T(8,128)(2,1)S(1)} %norm.1), channel_id=1, replica_groups=mesh['dp'=2,'row'=4,'col'=4] {'dp','row'}, dimensions={0} | all-to-all | bytes 4194304 | tf_op jit(solution)/shard_map/cond/branch_1_fun/all_to_all | solution.py:303
  39.4 1.7 %project_own.1 = (bf16[512,1024]{1,0:T(8,128)(2,1)}, bf16[512,1024]{1,0:T(8,128)(2,1)}, bf16[4,128,512]{2,1,0:T(8,128)(2,1)S(1)}, bf16[4,128,512]{2,1,0:T(8,128)(2,1)S(1)}) custom-call(bf16[8,128,1024]{2,1,0:T(8,128)(2,1)S(1)} %get-tuple-element.137.tile_ref, bf16[1024,512]{1,0:T(8,128)(2,1)S(1)} %pad_maximum_fusion.weights_ref), custom_call_target="tpu_custom_call" | custom-call | tf_op jit(solution)/shard_map/project_own/pallas_call | solution.py:121
  41.1 11.6 %conditional.4 = (bf16[1,128,512]{2,1,0:T(8,128)(2,1)S(1)}, bf16[128,512]{1,0:T(8,128)(2,1)}, bf16[128,512]{1,0:T(8,128)(2,1)}, bf16[128,512]{1,0:T(8,128)(2,1)}) conditional(s32[]{:T(128)} %convert_element_type.42, () %tuple.37, (bf16[4,128,512]{2,1,0:T(8,128)(2,1)S(1)}, bf16[4,128,512]{2,1,0:T(8,128)(2,1)S(1)}) %tuple.38), branch_computations={%region_2.3_spmd, %region_3.4_spmd} | conditional | flops 1048576 | bytes 6291648 | solution.py:287
  41.1 0.1 collective-permute-start
  41.2 1.9 %collective-permute-done = bf16[4,128,512]{2,1,0:T(8,128)(2,1)S(1)} collective-permute-done((bf16[4,128,512]{2,1,0:T(8,128)(2,1)S(1)}, bf16[4,128,512]{2,1,0:T(8,128)(2,1)S(1)}, u32[]{:S(2)}, u32[]{:S(2)}) %collective-permute-start) | collective-permute-done | bytes 524320 | tf_op jit(solution)/shard_map/cond/branch_1_fun/ppermute | solution.py:267
  43.1 0.1 add_convert_fusion
  43.3 1.2 %collective-permute-start.1 = (bf16[128,512]{1,0:T(8,128)(2,1)S(1)}, bf16[128,512]{1,0:T(8,128)(2,1)}, u32[]{:S(2)}, u32[]{:S(2)}) collective-permute-start(bf16[128,512]{1,0:T(8,128)(2,1)S(1)} %get-tuple-element.105), channel_id=1, source_target_pairs={{0,16},{4,20},{8,24},{12,28},{16,0},{20,4},{24,8},{28,12},{1,17},{... | collective-permute-start | bytes 393224 | tf_op jit(solution)/shard_map/cond/branch_1_fun/ppermute | solution.py:267
  44.5 0.9 collective-permute-start.2
  45.4 1.4 %collective-permute-start.3 = (bf16[128,512]{1,0:T(8,128)(2,1)S(1)}, bf16[128,512]{1,0:T(8,128)(2,1)}, u32[]{:S(2)}, u32[]{:S(2)}) collective-permute-start(bf16[128,512]{1,0:T(8,128)(2,1)S(1)} %get-tuple-element.103), channel_id=1, source_target_pairs={{0,24},{4,28},{8,16},{12,20},{16,8},{20,12},{24,0},{28,4},{1,25},{... | collective-permute-start | bytes 393224 | tf_op jit(solution)/shard_map/cond/branch_1_fun/ppermute | solution.py:267
  46.8 2.9 %collective-permute-done.1 = bf16[128,512]{1,0:T(8,128)(2,1)} collective-permute-done((bf16[128,512]{1,0:T(8,128)(2,1)S(1)}, bf16[128,512]{1,0:T(8,128)(2,1)}, u32[]{:S(2)}, u32[]{:S(2)}) %collective-permute-start.1) | collective-permute-done | bytes 131104 | tf_op jit(solution)/shard_map/cond/branch_1_fun/ppermute | solution.py:267
  49.7 1.3 %collective-permute-done.2 = bf16[128,512]{1,0:T(8,128)(2,1)} collective-permute-done((bf16[128,512]{1,0:T(8,128)(2,1)S(1)}, bf16[128,512]{1,0:T(8,128)(2,1)}, u32[]{:S(2)}, u32[]{:S(2)}) %collective-permute-start.2) | collective-permute-done | bytes 131104 | tf_op jit(solution)/shard_map/cond/branch_1_fun/ppermute | solution.py:267
  51.0 1.7 %collective-permute-done.3 = bf16[128,512]{1,0:T(8,128)(2,1)} collective-permute-done((bf16[128,512]{1,0:T(8,128)(2,1)S(1)}, bf16[128,512]{1,0:T(8,128)(2,1)}, u32[]{:S(2)}, u32[]{:S(2)}) %collective-permute-start.3) | collective-permute-done | bytes 131104 | tf_op jit(solution)/shard_map/cond/branch_1_fun/ppermute | solution.py:267
  52.7 0.7 collective-permute-start.11
  53.4 2.1 %collective-permute-start.9 = (bf16[1024,512]{1,0:T(8,128)(2,1)}, bf16[1024,512]{1,0:T(8,128)(2,1)S(1)}, u32[]{:S(2)}, u32[]{:S(2)}) collective-permute-start(bf16[1024,512]{1,0:T(8,128)(2,1)} %collective-permute-done.8.refs_1_), channel_id=1, source_target_pairs={{0,1},{1,0},{2,3},{3,2},{4,5},{5,4},{6,7},{7,6},{8,9},{9,8},{10,11... | collective-permute-start | bytes 3145736 | tf_op jit(solution)/shard_map/ppermute | solution.py:270
  55.6 4.2 %project_both.1 = (bf16[4,128,1024]{2,1,0:T(8,128)(2,1)S(1)}, bf16[4,128,1024]{2,1,0:T(8,128)(2,1)S(1)}) custom-call(bf16[512,1024]{1,0:T(8,128)(2,1)} %get-tuple-element.74.near_hbm, bf16[512,1024]{1,0:T(8,128)(2,1)} %get-tuple-element.80.far_hbm, bf16[1024,512]{1,0:T(8,128)(2,1)} %collective-permute-done.10.refs_0_, ...), custom_call_target="tpu_custom_call" | custom-call | tf_op jit(solution)/shard_map/project_both/pallas_call | solution.py:173
  59.8 17.9 %conditional.5 = (bf16[1,128,1024]{2,1,0:T(8,128)(2,1)S(1)}, bf16[128,1024]{1,0:T(8,128)(2,1)}, bf16[128,1024]{1,0:T(8,128)(2,1)}, bf16[128,1024]{1,0:T(8,128)(2,1)}) conditional(s32[]{:T(128)} %convert_element_type.42, () %tuple.40, (bf16[4,128,1024]{2,1,0:T(8,128)(2,1)S(1)}, bf16[4,128,1024]{2,1,0:T(8,128)(2,1)S(1)}) %project_both.1), branch_computations={%region_4.5_spmd, %region_5.6_spmd} | conditional | flops 2097152 | bytes 12583104 | solution.py:287
  59.8 0.1 collective-permute-start.4
  59.9 2.6 %collective-permute-done.4 = bf16[4,128,1024]{2,1,0:T(8,128)(2,1)S(1)} collective-permute-done((bf16[4,128,1024]{2,1,0:T(8,128)(2,1)S(1)}, bf16[4,128,1024]{2,1,0:T(8,128)(2,1)S(1)}, u32[]{:S(2)}, u32[]{:S(2)}) %collective-permute-start.4) | collective-permute-done | bytes 1048608 | tf_op jit(solution)/shard_map/cond/branch_1_fun/ppermute | solution.py:267
  62.5 0.4 add_convert_fusion.1
  63.0 0.1 slice_bitcast_fusion.3
  63.0 0.9 collective-permute-start.5
  63.9 1.5 %collective-permute-start.6 = (bf16[128,1024]{1,0:T(8,128)(2,1)S(1)}, bf16[128,1024]{1,0:T(8,128)(2,1)}, u32[]{:S(2)}, u32[]{:S(2)}) collective-permute-start(bf16[128,1024]{1,0:T(8,128)(2,1)S(1)} %get-tuple-element.108), channel_id=1, source_target_pairs={{0,8},{4,12},{8,0},{12,4},{16,24},{20,28},{24,16},{28,20},{1,9},{5... | collective-permute-start | bytes 786440 | tf_op jit(solution)/shard_map/cond/branch_1_fun/ppermute | solution.py:267
  65.4 1.2 %collective-permute-start.7 = (bf16[128,1024]{1,0:T(8,128)(2,1)S(1)}, bf16[128,1024]{1,0:T(8,128)(2,1)}, u32[]{:S(2)}, u32[]{:S(2)}) collective-permute-start(bf16[128,1024]{1,0:T(8,128)(2,1)S(1)} %get-tuple-element.107), channel_id=1, source_target_pairs={{0,24},{4,28},{8,16},{12,20},{16,8},{20,12},{24,0},{28,4},{1,25},{... | collective-permute-start | bytes 786440 | tf_op jit(solution)/shard_map/cond/branch_1_fun/ppermute | solution.py:267
  66.6 5.8 %collective-permute-done.5 = bf16[128,1024]{1,0:T(8,128)(2,1)} collective-permute-done((bf16[128,1024]{1,0:T(8,128)(2,1)S(1)}, bf16[128,1024]{1,0:T(8,128)(2,1)}, u32[]{:S(2)}, u32[]{:S(2)}) %collective-permute-start.5) | collective-permute-done | bytes 262176 | tf_op jit(solution)/shard_map/cond/branch_1_fun/ppermute | solution.py:267
  72.3 5.4 %collective-permute-done.6 = bf16[128,1024]{1,0:T(8,128)(2,1)} collective-permute-done((bf16[128,1024]{1,0:T(8,128)(2,1)S(1)}, bf16[128,1024]{1,0:T(8,128)(2,1)}, u32[]{:S(2)}, u32[]{:S(2)}) %collective-permute-start.6) | collective-permute-done | bytes 262176 | tf_op jit(solution)/shard_map/cond/branch_1_fun/ppermute | solution.py:267
  77.7 0.4 collective-permute-done.9
  78.1 0.1 broadcast_select_fusion
  78.2 0.7 copy-done.1
  79.0 0.7 convolution_convert_fusion
  79.8 0.4 copy-done
  80.2 0.7 fusion.1
  80.9 0.8 collective-permute-done.12
  81.7 0.2 add_convert_fusion.2.refs_0_
  81.9 1.2 %collective-permute-start.13 = (bf16[128,512]{1,0:T(8,128)(2,1)S(1)}, bf16[128,512]{1,0:T(8,128)(2,1)S(1)}, u32[]{:S(2)}, u32[]{:S(2)}) collective-permute-start(bf16[128,512]{1,0:T(8,128)(2,1)S(1)} %get-tuple-element.113), channel_id=1, source_target_pairs={{0,16},{4,20},{8,24},{12,28},{16,0},{20,4},{24,8},{28,12},{1,17},{... | collective-permute-start | bytes 393224 | tf_op jit(solution)/shard_map/ppermute | solution.py:267
  83.1 1.0 %collective-permute-start.14 = (bf16[128,512]{1,0:T(8,128)(2,1)S(1)}, bf16[128,512]{1,0:T(8,128)(2,1)S(1)}, u32[]{:S(2)}, u32[]{:S(2)}) collective-permute-start(bf16[128,512]{1,0:T(8,128)(2,1)S(1)} %get-tuple-element.112), channel_id=1, source_target_pairs={{0,8},{4,12},{8,0},{12,4},{16,24},{20,28},{24,16},{28,20},{1,9},{5... | collective-permute-start | bytes 393224 | tf_op jit(solution)/shard_map/ppermute | solution.py:267
  84.1 1.3 %collective-permute-start.15 = (bf16[128,512]{1,0:T(8,128)(2,1)S(1)}, bf16[128,512]{1,0:T(8,128)(2,1)S(1)}, u32[]{:S(2)}, u32[]{:S(2)}) collective-permute-start(bf16[128,512]{1,0:T(8,128)(2,1)S(1)} %get-tuple-element.111), channel_id=1, source_target_pairs={{0,24},{4,28},{8,16},{12,20},{16,8},{20,12},{24,0},{28,4},{1,25},{... | collective-permute-start | bytes 393224 | tf_op jit(solution)/shard_map/ppermute | solution.py:267
  85.4 0.3 fusion
  85.7 0.1 pad_maximum_fusion.1
  85.8 1.8 %finish.3 = (bf16[128,1024]{1,0:T(8,128)(2,1)}, bf16[128,1024]{1,0:T(8,128)(2,1)}) custom-call(bf16[1,128,512]{2,1,0:T(8,128)(2,1)S(1)} %get-tuple-element.93.refs_0_, bf16[128,512]{1,0:T(8,128)(2,1)} %get-tuple-element.94.refs_1_, bf16[128,512]{1,0:T(8,128)(2,1)} %get-tuple-element.95.refs_2_, bf16[128,512]{1,0:T(8,128)(2,1)} %get-tuple-element.96.refs_3_, ...), custom_call_target="tpu_custom_call" | custom-call | tf_op jit(solution)/shard_map/finish/pallas_call | solution.py:224
  87.7 2.0 %finish.4 = (bf16[128,1024]{1,0:T(8,128)(2,1)}, bf16[128,1024]{1,0:T(8,128)(2,1)}) custom-call(bf16[1,128,1024]{2,1,0:T(8,128)(2,1)S(1)} %get-tuple-element.89.refs_0_, bf16[128,1024]{1,0:T(8,128)(2,1)} %get-tuple-element.90.refs_1_, bf16[128,1024]{1,0:T(8,128)(2,1)} %get-tuple-element.91.refs_2_, ...), custom_call_target="tpu_custom_call", output_to_operand_aliasing={{0}: (6, {}), {1}: (7, {})} | custom-call | tf_op jit(solution)/shard_map/finish/pallas_call | solution.py:224
  89.7 1.4 %collective-permute-done.15.refs_3_ = bf16[128,512]{1,0:T(8,128)(2,1)S(1)} collective-permute-done((bf16[128,512]{1,0:T(8,128)(2,1)S(1)}, bf16[128,512]{1,0:T(8,128)(2,1)S(1)}, u32[]{:S(2)}, u32[]{:S(2)}) %collective-permute-start.15) | collective-permute-done | bytes 131104 | tf_op jit(solution)/shard_map/ppermute | solution.py:267
  91.2 0.8 finish.5
  (15 shorter events, 0.2 us)
Async XLA Ops:
  0.6 7.1 %copy-start.2 = (f32[8192]{0:T(1024)S(1)}, f32[8192]{0:T(1024)}, u32[]{:S(2)}) copy-start(f32[8192]{0:T(1024)} %param.11) | copy-start | bytes 98308
  2.0 50.7 %collective-permute-start.8 = (bf16[1024,512]{1,0:T(8,128)(2,1)S(1)}, bf16[1024,512]{1,0:T(8,128)(2,1)}, u32[]{:S(2)}, u32[]{:S(2)}) collective-permute-start(bf16[1024,512]{1,0:T(8,128)(2,1)S(1)} %pad_maximum_fusion.weights_ref), channel_id=1, source_target_pairs={{0,2},{1,3},{2,0},{3,1},{4,6},{5,7},{6,4},{7,5},{8,10},{9,11},{10,... | collective-permute-start | bytes 3145736 | tf_op jit(solution)/shard_map/ppermute | solution.py:270
  6.1 49.4 %collective-permute-start.10 = (bf16[1024,512]{1,0:T(8,128)(2,1)S(1)}, bf16[1024,512]{1,0:T(8,128)(2,1)}, u32[]{:S(2)}, u32[]{:S(2)}) collective-permute-start(bf16[1024,512]{1,0:T(8,128)(2,1)S(1)} %pad_maximum_fusion.weights_ref), channel_id=1, source_target_pairs={{0,1},{1,0},{2,3},{3,2},{4,5},{5,4},{6,7},{7,6},{8,9},{9,8},{10,11... | collective-permute-start | bytes 3145736 | tf_op jit(solution)/shard_map/ppermute | solution.py:270
  41.1 2.0 %collective-permute-start = (bf16[4,128,512]{2,1,0:T(8,128)(2,1)S(1)}, bf16[4,128,512]{2,1,0:T(8,128)(2,1)S(1)}, u32[]{:S(2)}, u32[]{:S(2)}) collective-permute-start(bf16[4,128,512]{2,1,0:T(8,128)(2,1)S(1)} %get-tuple-element.18), channel_id=1, source_target_pairs={{0,4},{4,0},{8,12},{12,8},{16,20},{20,16},{24,28},{28,24},{1,5},{5... | collective-permute-start | bytes 1572872 | tf_op jit(solution)/shard_map/cond/branch_1_fun/ppermute | solution.py:267
  43.3 6.4 %collective-permute-start.1 = (bf16[128,512]{1,0:T(8,128)(2,1)S(1)}, bf16[128,512]{1,0:T(8,128)(2,1)}, u32[]{:S(2)}, u32[]{:S(2)}) collective-permute-start(bf16[128,512]{1,0:T(8,128)(2,1)S(1)} %get-tuple-element.105), channel_id=1, source_target_pairs={{0,16},{4,20},{8,24},{12,28},{16,0},{20,4},{24,8},{28,12},{1,17},{... | collective-permute-start | bytes 393224 | tf_op jit(solution)/shard_map/cond/branch_1_fun/ppermute | solution.py:267
  44.5 6.5 %collective-permute-start.2 = (bf16[128,512]{1,0:T(8,128)(2,1)S(1)}, bf16[128,512]{1,0:T(8,128)(2,1)}, u32[]{:S(2)}, u32[]{:S(2)}) collective-permute-start(bf16[128,512]{1,0:T(8,128)(2,1)S(1)} %get-tuple-element.104), channel_id=1, source_target_pairs={{0,8},{4,12},{8,0},{12,4},{16,24},{20,28},{24,16},{28,20},{1,9},{5... | collective-permute-start | bytes 393224 | tf_op jit(solution)/shard_map/cond/branch_1_fun/ppermute | solution.py:267
  45.4 7.3 %collective-permute-start.3 = (bf16[128,512]{1,0:T(8,128)(2,1)S(1)}, bf16[128,512]{1,0:T(8,128)(2,1)}, u32[]{:S(2)}, u32[]{:S(2)}) collective-permute-start(bf16[128,512]{1,0:T(8,128)(2,1)S(1)} %get-tuple-element.103), channel_id=1, source_target_pairs={{0,24},{4,28},{8,16},{12,20},{16,8},{20,12},{24,0},{28,4},{1,25},{... | collective-permute-start | bytes 393224 | tf_op jit(solution)/shard_map/cond/branch_1_fun/ppermute | solution.py:267
  52.7 25.1 %collective-permute-start.11 = (bf16[1024,512]{1,0:T(8,128)(2,1)S(1)}, bf16[1024,512]{1,0:T(8,128)(2,1)S(1)}, u32[]{:S(2)}, u32[]{:S(2)}) collective-permute-start(bf16[1024,512]{1,0:T(8,128)(2,1)S(1)} %pad_maximum_fusion.weights_ref), channel_id=1, source_target_pairs={{1,2},{2,1},{5,6},{6,5},{9,10},{10,9},{13,14},{14,13},{17,18},{18,... | collective-permute-start | bytes 3145736 | tf_op jit(solution)/shard_map/ppermute | solution.py:270
  53.4 24.7 %collective-permute-start.9 = (bf16[1024,512]{1,0:T(8,128)(2,1)}, bf16[1024,512]{1,0:T(8,128)(2,1)S(1)}, u32[]{:S(2)}, u32[]{:S(2)}) collective-permute-start(bf16[1024,512]{1,0:T(8,128)(2,1)} %collective-permute-done.8.refs_1_), channel_id=1, source_target_pairs={{0,1},{1,0},{2,3},{3,2},{4,5},{5,4},{6,7},{7,6},{8,9},{9,8},{10,11... | collective-permute-start | bytes 3145736 | tf_op jit(solution)/shard_map/ppermute | solution.py:270
  59.8 2.7 %collective-permute-start.4 = (bf16[4,128,1024]{2,1,0:T(8,128)(2,1)S(1)}, bf16[4,128,1024]{2,1,0:T(8,128)(2,1)S(1)}, u32[]{:S(2)}, u32[]{:S(2)}) collective-permute-start(bf16[4,128,1024]{2,1,0:T(8,128)(2,1)S(1)} %get-tuple-element.20), channel_id=1, source_target_pairs={{0,4},{4,0},{8,12},{12,8},{16,20},{20,16},{24,28},{28,24},{1,5},{5... | collective-permute-start | bytes 3145736 | tf_op jit(solution)/shard_map/cond/branch_1_fun/ppermute | solution.py:267
  63.0 9.3 %collective-permute-start.5 = (bf16[128,1024]{1,0:T(8,128)(2,1)S(1)}, bf16[128,1024]{1,0:T(8,128)(2,1)}, u32[]{:S(2)}, u32[]{:S(2)}) collective-permute-start(bf16[128,1024]{1,0:T(8,128)(2,1)S(1)} %get-tuple-element.109), channel_id=1, source_target_pairs={{0,16},{4,20},{8,24},{12,28},{16,0},{20,4},{24,8},{28,12},{1,17},{... | collective-permute-start | bytes 786440 | tf_op jit(solution)/shard_map/cond/branch_1_fun/ppermute | solution.py:267
  63.9 13.8 %collective-permute-start.6 = (bf16[128,1024]{1,0:T(8,128)(2,1)S(1)}, bf16[128,1024]{1,0:T(8,128)(2,1)}, u32[]{:S(2)}, u32[]{:S(2)}) collective-permute-start(bf16[128,1024]{1,0:T(8,128)(2,1)S(1)} %get-tuple-element.108), channel_id=1, source_target_pairs={{0,8},{4,12},{8,0},{12,4},{16,24},{20,28},{24,16},{28,20},{1,9},{5... | collective-permute-start | bytes 786440 | tf_op jit(solution)/shard_map/cond/branch_1_fun/ppermute | solution.py:267
  65.4 12.3 %collective-permute-start.7 = (bf16[128,1024]{1,0:T(8,128)(2,1)S(1)}, bf16[128,1024]{1,0:T(8,128)(2,1)}, u32[]{:S(2)}, u32[]{:S(2)}) collective-permute-start(bf16[128,1024]{1,0:T(8,128)(2,1)S(1)} %get-tuple-element.107), channel_id=1, source_target_pairs={{0,24},{4,28},{8,16},{12,20},{16,8},{20,12},{24,0},{28,4},{1,25},{... | collective-permute-start | bytes 786440 | tf_op jit(solution)/shard_map/cond/branch_1_fun/ppermute | solution.py:267
  77.7 1.2 %copy-start.1 = (bf16[512,1024]{1,0:T(8,128)(2,1)S(1)}, bf16[512,1024]{1,0:T(8,128)(2,1)}, u32[]{:S(2)}) copy-start(bf16[512,1024]{1,0:T(8,128)(2,1)} %get-tuple-element.80.far_hbm) | copy-start | bytes 3145732
  79.0 1.2 %copy-start = (bf16[512,1024]{1,0:T(8,128)(2,1)S(1)}, bf16[512,1024]{1,0:T(8,128)(2,1)}, u32[]{:S(2)}) copy-start(bf16[512,1024]{1,0:T(8,128)(2,1)} %get-tuple-element.74.near_hbm) | copy-start | bytes 3145732
  79.7 2.0 %collective-permute-start.12 = (bf16[4,128,512]{2,1,0:T(8,128)(2,1)S(1)}, bf16[4,128,512]{2,1,0:T(8,128)(2,1)S(1)}, u32[]{:S(2)}, u32[]{:S(2)}) collective-permute-start(bf16[4,128,512]{2,1,0:T(8,128)(2,1)S(1)} %bitcast.27), channel_id=1, source_target_pairs={{0,4},{4,0},{8,12},{12,8},{16,20},{20,16},{24,28},{28,24},{1,5},{5... | collective-permute-start | bytes 1572872 | tf_op jit(solution)/shard_map/ppermute | solution.py:267
  81.9 7.8 %collective-permute-start.13 = (bf16[128,512]{1,0:T(8,128)(2,1)S(1)}, bf16[128,512]{1,0:T(8,128)(2,1)S(1)}, u32[]{:S(2)}, u32[]{:S(2)}) collective-permute-start(bf16[128,512]{1,0:T(8,128)(2,1)S(1)} %get-tuple-element.113), channel_id=1, source_target_pairs={{0,16},{4,20},{8,24},{12,28},{16,0},{20,4},{24,8},{28,12},{1,17},{... | collective-permute-start | bytes 393224 | tf_op jit(solution)/shard_map/ppermute | solution.py:267
  83.1 6.6 %collective-permute-start.14 = (bf16[128,512]{1,0:T(8,128)(2,1)S(1)}, bf16[128,512]{1,0:T(8,128)(2,1)S(1)}, u32[]{:S(2)}, u32[]{:S(2)}) collective-permute-start(bf16[128,512]{1,0:T(8,128)(2,1)S(1)} %get-tuple-element.112), channel_id=1, source_target_pairs={{0,8},{4,12},{8,0},{12,4},{16,24},{20,28},{24,16},{28,20},{1,9},{5... | collective-permute-start | bytes 393224 | tf_op jit(solution)/shard_map/ppermute | solution.py:267
  84.1 7.1 %collective-permute-start.15 = (bf16[128,512]{1,0:T(8,128)(2,1)S(1)}, bf16[128,512]{1,0:T(8,128)(2,1)S(1)}, u32[]{:S(2)}, u32[]{:S(2)}) collective-permute-start(bf16[128,512]{1,0:T(8,128)(2,1)S(1)} %get-tuple-element.111), channel_id=1, source_target_pairs={{0,24},{4,28},{8,16},{12,20},{16,8},{20,12},{24,0},{28,4},{1,25},{... | collective-permute-start | bytes 393224 | tf_op jit(solution)/shard_map/ppermute | solution.py:267
